TPU v7x, 32 devices: a whole 2x2x4 slice. The times are simulated.
32 devices in a mesh: dp: 8 (over z, y), mp: 4 (over x, core).
Axes of the slice: x: 2, y: 2, z: 4, core: 2. Of those that a mesh axis runs over, the one named last changes fastest.
Arguments:
- tokens: bfloat16 [16384, 768], P(('dp', 'mp')), may hold values from -6 to 6
- segment_ids: int32 [8, 2048], P('dp'), may hold values from 0 to 7, never falling along the last dimension, each value on 1 to 1024 neighbouring positions
- gene_owner: int32 [16384, 1], P(('dp', 'mp')), may hold values from 0 to 7; in each aligned block of 512 rows (0 to 511, 512 to 1023, ...) at most 80 rows name the same one
- w_qkv: bfloat16 [3, 768, 768], P(None, None, 'mp'), may hold values from -0.21875 to 0.21875
- w_attn_out: bfloat16 [768, 768], P('mp'), may hold values from -3.5 to 3.5
- w_up: bfloat16 [768, 3072], P(None, 'mp'), may hold values from -0.21875 to 0.21875
- w_down: bfloat16 [768, 3072], P(None, 'mp'), may hold values from -0.109375 to 0.109375
- gain_attn: float32 [768], replicated, may hold values from 0.1 to 1.9
- gain_mlp: float32 [768], replicated, may hold values from 0.1 to 1.9
- cotangent: bfloat16 [20480, 768], P(('dp', 'mp')), may hold values from -6 to 6
Outputs:
- relaid: bfloat16 [20480, 768], P(('dp', 'mp'))
- grad_tokens: bfloat16 [16384, 768], P(('dp', 'mp'))
- grad_qkv: float32 [3, 768, 768], P(None, None, 'mp')
- grad_attn_out: float32 [768, 768], P('mp')
- grad_up: float32 [768, 3072], P(None, 'mp')
- grad_down: float32 [768, 3072], P(None, 'mp')
- grad_gain_attn: float32 [768], replicated
- grad_gain_mlp: float32 [768], replicated
Inputs may be any that keep to these rules, and one draw needn't show every extreme that they name: `segment_ids`: in each packed row the numbers never fall; a cell holds 1 to 1024 tokens, and some cell of each row holds exactly that many. `gene_owner`: among the tokens of one device (aligned blocks of 512 tokens) at most 80 name the same owner, a bound that some block reaches.
All inputs are finite; a program needn't handle non-finite values.
Results may differ from a plain program's by a relative error of at most 0.015.
Values may be sent and summed in bfloat16 or wider, within the bound.
A program may use at most 192 MiB of HBM per device.

v0:
```python
import jax
import jax.numpy as jnp
from jax import lax
from jax.sharding import PartitionSpec as P

HEAD = 64
ROW_LEN = 2048


epsilon = 1e-05
masked_score = -1e30


def norm_parts(values, gain_vec):
    average = jnp.mean(values, axis=-1, keepdims=True)
    centered = values - average
    variance = jnp.mean(centered * centered, axis=-1, keepdims=True)
    inverse = lax.rsqrt(variance + epsilon)
    unit_rows = centered * inverse
    return (unit_rows * gain_vec, unit_rows, inverse)


def norm_back(grad_normed, unit_rows, inverse, gain_vec):
    scaled = grad_normed * gain_vec
    first_mean = jnp.mean(scaled, axis=-1, keepdims=True)
    second_mean = jnp.mean(scaled * unit_rows, axis=-1, keepdims=True)
    grad_input = inverse * (scaled - first_mean - unit_rows * second_mean)
    return (grad_input, jnp.sum(grad_normed * unit_rows, axis=0))


def gelu_exact(values):
    return 0.5 * values * (1.0 + lax.erf(values * 0.7071067811865476))


def gelu_slope(values):
    cumulative = 0.5 * (1.0 + lax.erf(values * 0.7071067811865476))
    density = jnp.exp(-0.5 * values * values) * 0.3989422804014327
    return cumulative + values * density


def block_scores(queries, key_rows, flat_cells, first_row, query_rows):
    row_start = first_row // ROW_LEN * ROW_LEN
    query_block = lax.dynamic_slice_in_dim(queries, first_row, query_rows, 0)
    query_cells = lax.dynamic_slice_in_dim(flat_cells, first_row, query_rows, 0)
    same_cell = query_cells[:, None] == flat_cells[None, :]
    raw_scores = jnp.einsum(
        "qhd,khd->hqk", query_block, key_rows, preferred_element_type=jnp.float32
    )
    scores = jnp.where(same_cell[None], raw_scores * HEAD ** (-0.5), masked_score)
    return (scores, query_block, key_rows, row_start)


def attend_forward(queries, key_rows, value_rows, segment_ids, query_rows):
    flat_cells = segment_ids.reshape(-1)

    def one_block(block_index):
        first_row = block_index * query_rows
        scores, query_block, key_block, row_start = block_scores(
            queries, key_rows, flat_cells, first_row, query_rows
        )
        row_max = jnp.max(scores, axis=-1, keepdims=True)
        powers = jnp.exp(scores - row_max)
        totals = jnp.sum(powers, axis=-1, keepdims=True)
        probs_low = (powers / totals).astype(jnp.bfloat16)
        attended = jnp.einsum(
            "hqk,khd->qhd", probs_low, value_rows, preferred_element_type=jnp.float32
        )
        return (attended, row_max + jnp.log(totals))

    block_count = queries.shape[0] // query_rows
    attended, log_sums = lax.map(one_block, jnp.arange(block_count, dtype=jnp.int32))
    return (attended.reshape(queries.shape), log_sums)


def attend_backward(
    queries, key_rows, value_rows, segment_ids, log_sums, grad_attended, query_rows
):
    flat_cells = segment_ids.reshape(-1)

    def one_block(block_index, partial_grads):
        grad_query, grad_key, grad_value = partial_grads
        first_row = block_index * query_rows
        scores, query_block, key_block, row_start = block_scores(
            queries, key_rows, flat_cells, first_row, query_rows
        )
        grad_block = lax.dynamic_slice_in_dim(grad_attended, first_row, query_rows, 0)
        probs = jnp.exp(scores - log_sums[block_index])
        grad_probs = jnp.einsum(
            "qhd,khd->hqk", grad_block, value_rows, preferred_element_type=jnp.float32
        )
        inner_sum = jnp.sum(probs * grad_probs, axis=-1, keepdims=True)
        grad_scores = (probs * (grad_probs - inner_sum) * HEAD ** (-0.5)).astype(jnp.bfloat16)
        probs_low = probs.astype(jnp.bfloat16)
        query_part = jnp.einsum(
            "hqk,khd->qhd", grad_scores, key_block, preferred_element_type=jnp.float32
        )
        key_part = jnp.einsum(
            "hqk,qhd->khd", grad_scores, query_block, preferred_element_type=jnp.float32
        )
        value_part = jnp.einsum(
            "hqk,qhd->khd", probs_low, grad_block, preferred_element_type=jnp.float32
        )
        grad_query = lax.dynamic_update_slice_in_dim(grad_query, query_part, first_row, 0)
        old_key = grad_key
        grad_key = old_key + key_part
        old_value = grad_value
        grad_value = old_value + value_part
        return (grad_query, grad_key, grad_value)

    empty_grad = jnp.zeros(queries.shape, jnp.float32)
    block_count = queries.shape[0] // query_rows
    grad_query, grad_key, grad_value = lax.fori_loop(
        0, block_count, one_block, (empty_grad, empty_grad, empty_grad)
    )
    return (
        grad_query.astype(jnp.bfloat16),
        grad_key.astype(jnp.bfloat16),
        grad_value.astype(jnp.bfloat16),
    )


def local(
    tokens, segment_ids, gene_owner, w_qkv, w_attn_out, w_up, w_down, gain_attn, gain_mlp, cotangent
):
    width = tokens.shape[1]
    dp_count = lax.axis_size("dp")
    capacity = cotangent.shape[0] // dp_count
    local_width = w_qkv.shape[2]
    local_heads = local_width // HEAD
    query_rows = min(512, ROW_LEN)
    tokens_f = tokens.astype(jnp.float32)
    normed_one, unit_one, inverse_one = norm_parts(tokens_f, gain_attn)
    attn_in = lax.all_gather(normed_one.astype(jnp.bfloat16), "mp", axis=0, tiled=True)
    row_tokens = attn_in.shape[0]
    projected = jnp.einsum(
        "td,kde->kte", attn_in, w_qkv, preferred_element_type=jnp.float32
    ).astype(jnp.bfloat16)
    queries = projected[0].reshape(row_tokens, local_heads, HEAD)
    key_rows = projected[1].reshape(row_tokens, local_heads, HEAD)
    value_rows = projected[2].reshape(row_tokens, local_heads, HEAD)
    attended, log_sums = attend_forward(queries, key_rows, value_rows, segment_ids, query_rows)
    merged = attended.reshape(row_tokens, local_width).astype(jnp.bfloat16)
    residual = tokens_f + lax.psum_scatter(
        jnp.dot(merged, w_attn_out, preferred_element_type=jnp.float32),
        "mp",
        scatter_dimension=0,
        tiled=True,
    )
    normed_two, unit_two, inverse_two = norm_parts(residual, gain_mlp)
    mlp_in = normed_two.astype(jnp.bfloat16)
    contract_last = (((1,), (1,)), ((), ()))
    contract_first = (((0,), (0,)), ((), ()))
    mlp_rows = lax.all_gather(mlp_in, "mp", axis=0, tiled=True)
    pre_act = jnp.dot(mlp_rows, w_up, preferred_element_type=jnp.float32)
    activated = gelu_exact(pre_act).astype(jnp.bfloat16)
    piece = activated
    output = residual + lax.psum_scatter(
        lax.dot_general(piece, w_down, contract_last, preferred_element_type=jnp.float32).astype(
            jnp.bfloat16
        ),
        "mp",
        scatter_dimension=0,
        tiled=True,
    ).astype(jnp.float32)
    owners = gene_owner[:, 0]
    onehot = (owners[:, None] == jnp.arange(dp_count, dtype=jnp.int32)[None, :]).astype(jnp.int32)
    ranking = jnp.sum(
        (jnp.cumsum(onehot, axis=0, dtype=jnp.int32) - onehot) * onehot, axis=1, dtype=jnp.int32
    )
    outgoing = (
        jnp.zeros((dp_count, capacity, width), jnp.bfloat16)
        .at[owners, ranking]
        .set(output.astype(jnp.bfloat16))
    )
    arrived = lax.all_to_all(outgoing, "dp", split_axis=0, concat_axis=0, tiled=True)
    relaid = arrived.reshape(dp_count * capacity, width)
    returned = lax.all_to_all(
        cotangent.reshape(dp_count, capacity, width), "dp", split_axis=0, concat_axis=0, tiled=True
    )
    grad_block = returned[owners, ranking]
    grad_rows = lax.all_gather(grad_block, "mp", axis=0, tiled=True)
    grad_act = jnp.dot(grad_rows, w_down, preferred_element_type=jnp.float32)
    grad_pre = (grad_act * gelu_slope(pre_act)).astype(jnp.bfloat16)
    grad_down_local = lax.dot_general(
        grad_rows, activated, contract_first, preferred_element_type=jnp.float32
    )
    grad_up_local = lax.dot_general(
        mlp_rows, grad_pre, contract_first, preferred_element_type=jnp.float32
    )
    piece = grad_pre
    grad_mlp_in = lax.psum_scatter(
        lax.dot_general(piece, w_up, contract_last, preferred_element_type=jnp.float32),
        "mp",
        scatter_dimension=0,
        tiled=True,
    )
    norm_two_grad, gain_mlp_grad = norm_back(grad_mlp_in, unit_two, inverse_two, gain_mlp)
    grad_residual = grad_block.astype(jnp.float32) + norm_two_grad
    residual_rows = lax.all_gather(grad_residual.astype(jnp.bfloat16), "mp", axis=0, tiled=True)
    grad_attn_local = lax.dot_general(
        merged, residual_rows, contract_first, preferred_element_type=jnp.float32
    )
    grad_merged = lax.dot_general(
        residual_rows, w_attn_out, contract_last, preferred_element_type=jnp.float32
    )
    grad_merged = grad_merged.astype(jnp.bfloat16).reshape(row_tokens, local_heads, HEAD)
    grad_query, grad_key, grad_value = attend_backward(
        queries, key_rows, value_rows, segment_ids, log_sums, grad_merged, query_rows
    )
    grad_proj = jnp.stack(
        [
            grad_query.reshape(row_tokens, local_width),
            grad_key.reshape(row_tokens, local_width),
            grad_value.reshape(row_tokens, local_width),
        ]
    )
    grad_qkv_local = jnp.einsum(
        "td,kte->kde", attn_in, grad_proj, preferred_element_type=jnp.float32
    )
    piece = grad_proj
    grad_attn_in = lax.psum_scatter(
        jnp.einsum("kte,kde->td", piece, w_qkv, preferred_element_type=jnp.float32).astype(
            jnp.bfloat16
        ),
        "mp",
        scatter_dimension=0,
        tiled=True,
    ).astype(jnp.float32)
    norm_one_grad, gain_attn_grad = norm_back(grad_attn_in, unit_one, inverse_one, gain_attn)
    grad_tokens = (grad_residual + norm_one_grad).astype(jnp.bfloat16)
    gain_attn_sum, gain_mlp_sum = lax.psum((gain_attn_grad, gain_mlp_grad), ("dp", "mp"))
    qkv_sum, attn_sum, up_sum, down_sum = lax.psum(
        (grad_qkv_local, grad_attn_local, grad_up_local, grad_down_local), "dp"
    )
    return (relaid, grad_tokens, qkv_sum, attn_sum, up_sum, down_sum, gain_attn_sum, gain_mlp_sum)


def solution(mesh):
    placed = (
        P(("dp", "mp"), None),
        P("dp", None),
        P(("dp", "mp"), None),
        P(None, None, "mp"),
        P("mp", None),
        P(None, "mp"),
        P(None, "mp"),
        P(),
        P(),
        P(("dp", "mp"), None),
    )
    return jax.shard_map(
        local,
        mesh=mesh,
        in_specs=placed,
        out_specs=(
            P(("dp", "mp"), None),
            P(("dp", "mp"), None),
            P(None, None, "mp"),
            P("mp", None),
            P(None, "mp"),
            P(None, "mp"),
            P(),
            P(),
        ),
        check_vma=False,
    )
```

profile of v0, /device:TPU:0, one launch (start us, length us, event | category | flops | bytes accessed | tf_op | source)
XLA Modules:
  0.0 995.9 jit_solution(12525687361870699221)
XLA Ops:
  12.6 31.3 %all-gather.5.cloned.1.call-done = bf16[2048,768]{1,0:T(8,128)(2,1)} async-done(((bf16[512,768]{1,0:T(8,128)(2,1)}), bf16[2048,768]{1,0:T(8,128)(2,1)}) %all-gather.5.cloned.1.call-update) | async-done | bytes 3145744 | tf_op jit(solution)/shard_map/all_gather | solution.py:133
  49.0 89.6 %while.30 = (s32[]{:T(128)}, bf16[4,512,3,64]{1,3,2,0:T(8,128)(2,1)}, f32[4,3,512,1]{2,1,3,0:T(4,128)}, s32[4]{0:T(128)S(1)}, s32[2048]{0:T(1024)S(1)}, /*index=...) while((s32[]{:T(128)}, ...), condition=%wide.region_8.9_spmd, body=%wide.region_5.8_spmd.sunk | while | flops 844102144 | bytes 50467080 | solution.py:71
  145.8 58.5 %reduce-scatter.5.cloned.1.call-done = f32[512,768]{1,0:T(8,128)} async-done(((f32[2048,768]{1,0:T(8,128)}), f32[512,768]{1,0:T(8,128)}) %reduce-scatter.5.cloned.1.call-update) | async-done | bytes 1572880 | tf_op jit(solution)/shard_map/reduce_scatter | solution.py:143
  216.7 22.0 %all-to-all-done.1 = bf16[8,80,768]{2,1,0:T(8,128)(2,1)S(1)} async-done(((bf16[8,80,768]{2,1,0:T(8,128)(2,1)}), bf16[8,80,768]{2,1,0:T(8,128)(2,1)S(1)}, u32[]{:S(2)}, u32[]{:S(2)}) %all-to-all-start.1) | async-done | bytes 983072 | tf_op jit(solution)/shard_map/all_to_all | solution.py:177
  246.1 7.5 multiply_convert_fusion.1
  253.5 19.2 %all-gather.9.cloned.1.call-done = bf16[2048,768]{1,0:T(8,128)(2,1)} async-done(((bf16[512,768]{1,0:T(8,128)(2,1)}), bf16[2048,768]{1,0:T(8,128)(2,1)}) %all-gather.9.cloned.1.call-update) | async-done | bytes 3145744 | tf_op jit(solution)/shard_map/all_gather | solution.py:181
  292.4 51.8 %reduce-scatter.9.cloned.1.call-done = f32[512,768]{1,0:T(8,128)} async-done(((f32[2048,768]{1,0:T(8,128)}), f32[512,768]{1,0:T(8,128)}) %reduce-scatter.9.cloned.1.call-update) | async-done | bytes 1572880 | tf_op jit(solution)/shard_map/reduce_scatter | solution.py:191
  346.8 37.7 %reduce-scatter.7.cloned.1.call-done = bf16[512,768]{1,0:T(8,128)(2,1)} async-done(((bf16[2048,768]{1,0:T(8,128)(2,1)}), bf16[512,768]{1,0:T(8,128)(2,1)}) %reduce-scatter.7.cloned.1.call-update) | async-done | bytes 786448 | tf_op jit(solution)/shard_map/reduce_scatter | solution.py:157
  388.7 28.6 %all-gather.11.cloned.1.call-done = bf16[2048,768]{1,0:T(8,128)(2,1)} async-done(((bf16[512,768]{1,0:T(8,128)(2,1)}), bf16[2048,768]{1,0:T(8,128)(2,1)}) %all-gather.11.cloned.1.call-update) | async-done | bytes 3145744 | tf_op jit(solution)/shard_map/all_gather | solution.py:199
  422.2 252.9 %while.31 = (s32[]{:T(128)}, bf16[2048,3,64]{0,2,1:T(8,128)(2,1)}, f32[2048,3,64]{0,2,1:T(8,128)}, f32[2048,3,64]{0,2,1:T(8,128)}, s32[2048]{0:T(1024)S(1)}, /*i...) while((s32[]{:T(128)}, bf16[2048,3,64]{0,2,1:T(8,128)(2,1)}, ...), condition=%wide.region_19.20_spmd.clone, body=%wide.region_17.19_spmd.clone.sunk | while | flops 2097683456 | bytes 208079120 | solution.py:112
  449.3 20.7 %fusion.185 = bf16[2048,3,64]{0,2,1:T(8,128)(2,1)} fusion(bf16[2048,3,64]{0,2,1:T(8,128)(2,1)} %get-tuple-element.532, s32[]{:T(128)S(6)} %select_n.135, bf16[2048,3,64]{0,2,1:T(8,128)(2,1)S(1)} %get-tuple-element.553, f32[3,512,2048]{2,1,0:T(8,128)} %fusion.183, f32[3,512,2048]{2,1,0:T(8,128)} %copy-done.2, ...), kind=kOutput, calls=%fused_computation.41.clone.1 | convolution fusion | flops 437259776 | bytes 53624836 | tf_op jit(solution)/shard_map/while/body/eval_jaxpr/hqk,khd->qhd/dot_general | solution.py:94
  470.0 21.9 %fusion.186 = f32[2048,3,64]{0,2,1:T(8,128)} fusion(f32[3,512,2048]{2,1,0:T(8,128)} %fusion.183, f32[3,512,2048]{2,1,0:T(8,128)} %copy-done.2, f32[3,512]{1,0:T(4,128)S(1)} %dynamic-slice_bitcast_fusion.2, pred[512,2048]{1,0:T(8,128)(4,1)S(1)} %broadcast_compare_fusion.5, f32[2048,3,64]{0,2,1:T(8,128)} %get-tuple-element.533, pred[]{:T(512)S(6)} %compare.9, ...), kind=kOutput, calls=%fused_computation.37.clone.1 | convolution fusion | flops 438046208 | bytes 55787524 | tf_op jit(solution)/shard_map/while/body/eval_jaxpr/hqk,qhd->khd/dot_general | solution.py:97
  496.2 7.3 fusion.187
  509.9 20.7 %fusion.185 = bf16[2048,3,64]{0,2,1:T(8,128)(2,1)} fusion(bf16[2048,3,64]{0,2,1:T(8,128)(2,1)} %get-tuple-element.532, s32[]{:T(128)S(6)} %select_n.135, bf16[2048,3,64]{0,2,1:T(8,128)(2,1)S(1)} %get-tuple-element.553, f32[3,512,2048]{2,1,0:T(8,128)} %fusion.183, f32[3,512,2048]{2,1,0:T(8,128)} %copy-done.2, ...), kind=kOutput, calls=%fused_computation.41.clone.1 | convolution fusion | flops 437259776 | bytes 53624836 | tf_op jit(solution)/shard_map/while/body/eval_jaxpr/hqk,khd->qhd/dot_general | solution.py:94
  530.5 22.4 %fusion.186 = f32[2048,3,64]{0,2,1:T(8,128)} fusion(f32[3,512,2048]{2,1,0:T(8,128)} %fusion.183, f32[3,512,2048]{2,1,0:T(8,128)} %copy-done.2, f32[3,512]{1,0:T(4,128)S(1)} %dynamic-slice_bitcast_fusion.2, pred[512,2048]{1,0:T(8,128)(4,1)S(1)} %broadcast_compare_fusion.5, f32[2048,3,64]{0,2,1:T(8,128)} %get-tuple-element.533, pred[]{:T(512)S(6)} %compare.9, ...), kind=kOutput, calls=%fused_computation.37.clone.1 | convolution fusion | flops 438046208 | bytes 55787524 | tf_op jit(solution)/shard_map/while/body/eval_jaxpr/hqk,qhd->khd/dot_general | solution.py:97
  570.9 20.7 %fusion.185 = bf16[2048,3,64]{0,2,1:T(8,128)(2,1)} fusion(bf16[2048,3,64]{0,2,1:T(8,128)(2,1)} %get-tuple-element.532, s32[]{:T(128)S(6)} %select_n.135, bf16[2048,3,64]{0,2,1:T(8,128)(2,1)S(1)} %get-tuple-element.553, f32[3,512,2048]{2,1,0:T(8,128)} %fusion.183, f32[3,512,2048]{2,1,0:T(8,128)} %copy-done.2, ...), kind=kOutput, calls=%fused_computation.41.clone.1 | convolution fusion | flops 437259776 | bytes 53624836 | tf_op jit(solution)/shard_map/while/body/eval_jaxpr/hqk,khd->qhd/dot_general | solution.py:94
  591.5 22.4 %fusion.186 = f32[2048,3,64]{0,2,1:T(8,128)} fusion(f32[3,512,2048]{2,1,0:T(8,128)} %fusion.183, f32[3,512,2048]{2,1,0:T(8,128)} %copy-done.2, f32[3,512]{1,0:T(4,128)S(1)} %dynamic-slice_bitcast_fusion.2, pred[512,2048]{1,0:T(8,128)(4,1)S(1)} %broadcast_compare_fusion.5, f32[2048,3,64]{0,2,1:T(8,128)} %get-tuple-element.533, pred[]{:T(512)S(6)} %compare.9, ...), kind=kOutput, calls=%fused_computation.37.clone.1 | convolution fusion | flops 438046208 | bytes 55787524 | tf_op jit(solution)/shard_map/while/body/eval_jaxpr/hqk,qhd->khd/dot_general | solution.py:97
  618.2 7.3 fusion.187
  631.9 20.7 %fusion.185 = bf16[2048,3,64]{0,2,1:T(8,128)(2,1)} fusion(bf16[2048,3,64]{0,2,1:T(8,128)(2,1)} %get-tuple-element.532, s32[]{:T(128)S(6)} %select_n.135, bf16[2048,3,64]{0,2,1:T(8,128)(2,1)S(1)} %get-tuple-element.553, f32[3,512,2048]{2,1,0:T(8,128)} %fusion.183, f32[3,512,2048]{2,1,0:T(8,128)} %copy-done.2, ...), kind=kOutput, calls=%fused_computation.41.clone.1 | convolution fusion | flops 437259776 | bytes 53624836 | tf_op jit(solution)/shard_map/while/body/eval_jaxpr/hqk,khd->qhd/dot_general | solution.py:94
  652.5 22.4 %fusion.186 = f32[2048,3,64]{0,2,1:T(8,128)} fusion(f32[3,512,2048]{2,1,0:T(8,128)} %fusion.183, f32[3,512,2048]{2,1,0:T(8,128)} %copy-done.2, f32[3,512]{1,0:T(4,128)S(1)} %dynamic-slice_bitcast_fusion.2, pred[512,2048]{1,0:T(8,128)(4,1)S(1)} %broadcast_compare_fusion.5, f32[2048,3,64]{0,2,1:T(8,128)} %get-tuple-element.533, pred[]{:T(512)S(6)} %compare.9, ...), kind=kOutput, calls=%fused_computation.37.clone.1 | convolution fusion | flops 438046208 | bytes 55787524 | tf_op jit(solution)/shard_map/while/body/eval_jaxpr/hqk,qhd->khd/dot_general | solution.py:97
  700.2 30.2 %scatter_fusion = bf16[8,80,768]{2,1,0:T(8,128)(2,1)S(1)} fusion(bf16[8,80,768]{2,1,0:T(8,128)(2,1)S(1)} %broadcast_in_dim.82, s32[512]{0:T(512)S(1)} %bitcast.126, bf16[512,768]{1,0:T(8,128)(2,1)S(1)} %copy-done.17), kind=kCustom, calls=%fused_computation.1 | custom fusion | bytes 2363392 | tf_op jit(solution)/shard_map/scatter | solution.py:173
  730.5 55.8 %all_to_all.10 = bf16[8,80,768]{2,1,0:T(8,128)(2,1)} all-to-all(bf16[8,80,768]{2,1,0:T(8,128)(2,1)S(1)} %scatter_fusion), channel_id=1, replica_groups=mesh['dp'=8,'mp'=4] {'dp'}, dimensions={0} | all-to-all | bytes 1966080 | tf_op jit(solution)/shard_map/all_to_all | solution.py:175
  788.4 41.2 %all-reduce = (f32[768]{0:T(1024)}, f32[768]{0:T(1024)}) all-reduce(f32[768]{0:T(1024)S(1)} %get-tuple-element.286, f32[768]{0:T(1024)S(1)} %copy-done.41), channel_id=1, replica_groups=mesh['dp'=8,'mp'=4] {'dp','mp'}, use_global_device_ids=true, to_apply=%region_28.29 | all-reduce | flops 1536 | bytes 12288 | tf_op jit(solution)/shard_map/psum | solution.py:231
  832.3 150.0 %all-reduce.4.cloned.1.call-done = (f32[3,768,192]{1,2,0:T(8,128)}, f32[192,768]{1,0:T(8,128)}, f32[768,768]{1,0:T(8,128)}, f32[768,768]{1,0:T(8,128)}) async-done(((f32[3,768,192]{1,2,0:T(8,128)}, f32[192,768]{1,0:T(8,128)}, f32[768,768]{1,0:T(8,128)}, f32[768,768]{1,0:T(8,128)}), (f32[3,768,192]{1,2,0:T(8,128)}, f32[192,768]{1,0:T(8,128)}, f32[768,768]{1,0:T(8,128)}, ...) | async-done | bytes 7077904 | tf_op jit(solution)/shard_map/psum | solution.py:232
  (247 shorter events, 246.8 us)
Async XLA Ops:
  7.2 238.9 %copy-start = (bf16[768,768]{1,0:T(8,128)(2,1)S(1)}, bf16[768,768]{1,0:T(8,128)(2,1)}, u32[]{:S(2)}) copy-start(bf16[768,768]{1,0:T(8,128)(2,1)} %param.19) | copy-start | bytes 3538948
  7.2 36.8 %all-gather.5.cloned.1.call-start = ((), (), s32[]{:S(2)}) async-start(), calls=%async_computation.6 | async-start | bytes 3932160 | tf_op jit(solution)/shard_map/all_gather | solution.py:133
  8.7 39.2 %copy-start.32 = (f32[512]{0:T(512)}, f32[512]{0:T(512)S(1)}, u32[]{:S(2)}) copy-start(f32[512]{0:T(512)S(1)} %broadcast_multiply_fusion.5) | copy-start | bytes 6148
  12.6 191.7 %reduce-scatter.5.cloned.1.call-start = ((), (), s32[]{:S(2)}) async-start(), calls=%async_computation.7 | async-start | bytes 7864320 | tf_op jit(solution)/shard_map/reduce_scatter | solution.py:143
  145.7 58.5 %copy-start.8 = (bf16[512,768]{1,0:T(8,128)(2,1)S(1)}, bf16[512,768]{1,0:T(8,128)(2,1)}, u32[]{:S(2)}) copy-start(bf16[512,768]{1,0:T(8,128)(2,1)} %param.14) | copy-start | bytes 2359300
  145.7 61.9 %copy-start.34 = (f32[768]{0:T(1024)S(1)}, f32[768]{0:T(1024)}, u32[]{:S(2)}) copy-start(f32[768]{0:T(1024)} %param.22) | copy-start | bytes 9220
  145.7 100.3 %all-gather.7.cloned.1.call-start = ((), (), s32[]{:S(2)}) async-start(), calls=%async_computation.8 | async-start | bytes 3932160 | tf_op jit(solution)/shard_map/all_gather | solution.py:153
  208.8 29.9 %all-to-all-start.1 = ((bf16[8,80,768]{2,1,0:T(8,128)(2,1)}), bf16[8,80,768]{2,1,0:T(8,128)(2,1)S(1)}, u32[]{:S(2)}, u32[]{:S(2)}) async-start(bf16[8,80,768]{2,1,0:T(8,128)(2,1)} %bitcast.142), calls=%async_computation.3 | async-start | bytes 1966080 | tf_op jit(solution)/shard_map/all_to_all | solution.py:177
  214.3 58.4 %all-gather.9.cloned.1.call-start = ((), (), s32[]{:S(2)}) async-start(), calls=%async_computation.10 | async-start | bytes 3932160 | tf_op jit(solution)/shard_map/all_gather | solution.py:181
  246.0 98.2 %reduce-scatter.9.cloned.1.call-start = ((), (), s32[]{:S(2)}) async-start(), calls=%async_computation.11 | async-start | bytes 7864320 | tf_op jit(solution)/shard_map/reduce_scatter | solution.py:191
  285.7 98.9 %reduce-scatter.7.cloned.1.call-start = ((), (), s32[]{:S(2)}) async-start(), calls=%async_computation.9 | async-start | bytes 3932160 | tf_op jit(solution)/shard_map/reduce_scatter | solution.py:157
  292.3 51.9 %copy-start.6 = (f32[512,768]{1,0:T(8,128)S(1)}, f32[512,768]{1,0:T(8,128)}, u32[]{:S(2)}) copy-start(f32[512,768]{1,0:T(8,128)} %copy-done.5) | copy-start | bytes 4718596
  292.3 51.9 %copy-start.39 = (f32[512]{0:T(512)S(1)}, f32[512]{0:T(512)}, u32[]{:S(2)}) copy-start(f32[512]{0:T(512)} %copy-done.38) | copy-start | bytes 6148
  292.3 92.3 %copy-start.12 = (bf16[512,768]{1,0:T(8,128)(2,1)S(1)}, bf16[512,768]{1,0:T(8,128)(2,1)}, u32[]{:S(2)}) copy-start(bf16[512,768]{1,0:T(8,128)(2,1)} %gather_fusion) | copy-start | bytes 2359300
  292.3 125.0 %all-gather.11.cloned.1.call-start = ((), (), s32[]{:S(2)}) async-start(), calls=%async_computation.12 | async-start | bytes 3932160 | tf_op jit(solution)/shard_map/all_gather | solution.py:199
  388.6 397.7 %reduce-scatter.11.cloned.1.call-start = ((), (), s32[]{:S(2)}) async-start(), calls=%async_computation.13 | async-start | bytes 3932160 | tf_op jit(solution)/shard_map/reduce_scatter | solution.py:221
  682.0 300.3 %all-reduce.4.cloned.1.call-start = ((), (), s32[]{:S(2)}) async-start(), calls=%async_computation.14 | async-start | bytes 14155776 | tf_op jit(solution)/shard_map/psum | solution.py:232
  700.2 86.1 %copy-start.9 = (bf16[512,768]{1,0:T(8,128)(2,1)S(1)}, bf16[512,768]{1,0:T(8,128)(2,1)}, u32[]{:S(2)}) copy-start(bf16[512,768]{1,0:T(8,128)(2,1)} %param.14) | copy-start | bytes 2359300
  700.2 86.1 %copy-start.33 = (f32[512]{0:T(512)S(1)}, f32[512]{0:T(512)}, u32[]{:S(2)}) copy-start(f32[512]{0:T(512)} %copy-done.32) | copy-start | bytes 6148
  700.2 86.1 %copy-start.35 = (f32[768]{0:T(1024)S(1)}, f32[768]{0:T(1024)}, u32[]{:S(2)}) copy-start(f32[768]{0:T(1024)} %param.21) | copy-start | bytes 9220
  700.2 86.1 %copy-start.37 = (f32[512]{0:T(512)S(1)}, f32[512]{0:T(512)}, u32[]{:S(2)}) copy-start(f32[512]{0:T(512)} %copy-done.36) | copy-start | bytes 6148
  730.5 58.0 %copy-start.41 = (f32[768]{0:T(1024)S(1)}, f32[768]{0:T(1024)}, u32[]{:S(2)}) copy-start(f32[768]{0:T(1024)} %get-tuple-element.283) | copy-start | bytes 9220
  730.5 99.1 %copy-start.13 = (f32[512,768]{1,0:T(8,128)S(1)}, f32[512,768]{1,0:T(8,128)}, u32[]{:S(2)}) copy-start(f32[512,768]{1,0:T(8,128)} %get-tuple-element.336) | copy-start | bytes 4718596
  786.3 196.0 %copy-start.15 = (bf16[8,80,768]{2,1,0:T(8,128)(2,1)S(1)}, bf16[8,80,768]{2,1,0:T(8,128)(2,1)}, u32[]{:S(2)}) copy-start(bf16[8,80,768]{2,1,0:T(8,128)(2,1)} %all_to_all.10) | copy-start | bytes 2949124
  (47 other events, 319.0 us)
Sparse Core Ops, SparseCore 0:
  12.7 31.2 all-gather.4
  145.8 58.3 reduce-scatter.4
  208.9 28.5 all-gather.6
  246.1 26.5 all-gather.8
  285.8 58.3 reduce-scatter.8
  346.6 37.9 reduce-scatter.6
  388.7 28.5 all-gather.10
  682.2 37.9 reduce-scatter.10
  725.2 257.0 all-reduce.3
where the time goes:
time: 1000 us; the launch traced here: 996 us
  waiting for transfers between devices  399 us (40%)
  matrix products  343 us (34%)
  blocking collectives  97 us (10%)
  local copies, waits for them, and re-layouts  62.1 us (6%)
  other arithmetic  59 us (6%)
  between operations  14.7 us (1%)
  loops' own time  14.3 us (1%)
    psum x1, waiting for transfers between devices, local(): lax.psum((grad_qkv_local, grad_attn_local, grad_up_local, grad_down_local...  150 us
    dot_general x4, matrix products, one_block(): jnp.einsum('hqk,qhd->khd', grad_scores, query_block, preferred_element_ty...  89.1 us
    dot_general x4, matrix products, one_block(): jnp.einsum('hqk,khd->qhd', grad_scores, key_block, preferred_element_type...  82.6 us
    reduce_scatter x1, waiting for transfers between devices, local(): lax.psum_scatter(jnp.dot(merged, w_attn_out, preferred_element_type=jnp.f...  58.5 us
    all_to_all x1, blocking collectives, local(): lax.all_to_all(outgoing, 'dp', split_axis=0, concat_axis=0, tiled=True)  55.8 us
    reduce_scatter x1, waiting for transfers between devices, local(): lax.psum_scatter(lax.dot_general(piece, w_up, contract_last, preferred_el...  51.8 us
    psum x1, blocking collectives, local(): lax.psum((gain_attn_grad, gain_mlp_grad), ('dp', 'mp'))  41.2 us
    reduce_scatter x1, waiting for transfers between devices, local(): lax.psum_scatter(lax.dot_general(piece, w_down, contract_last, preferred_...  37.7 us
  transfers between devices with their start and end apart: 10, of which 8 were waited for; matrix products, arithmetic and copies ran while one was open for 8% of the time, Pallas kernels for 0%

commit v1 on v0

v1 whole, which is shorter than its diff:
```python
import functools
import jax
import jax.numpy as jnp
from jax import lax
from jax.experimental import pallas as pl
from jax.experimental.pallas import tpu as pltpu
from jax.sharding import PartitionSpec as P

epsilon = 1e-05


def norm_parts(values, gain_vec):
    average = jnp.mean(values, axis=-1, keepdims=True)
    centered = values - average
    variance = jnp.mean(centered * centered, axis=-1, keepdims=True)
    inverse = lax.rsqrt(variance + epsilon)
    unit_rows = centered * inverse
    return (unit_rows * gain_vec, unit_rows, inverse)


def norm_back(grad_normed, unit_rows, inverse, gain_vec):
    scaled = grad_normed * gain_vec
    first_mean = jnp.mean(scaled, axis=-1, keepdims=True)
    second_mean = jnp.mean(scaled * unit_rows, axis=-1, keepdims=True)
    grad_input = inverse * (scaled - first_mean - unit_rows * second_mean)
    return (grad_input, jnp.sum(grad_normed * unit_rows, axis=0))


def gelu_exact(values):
    return 0.5 * values * (1.0 + lax.erf(values * 0.7071067811865476))


def gelu_slope(values):
    cumulative = 0.5 * (1.0 + lax.erf(values * 0.7071067811865476))
    density = jnp.exp(-0.5 * values * values) * 0.3989422804014327
    return cumulative + values * density


HEAD = 64
TQ = 256
TK = 256
NT = (((1,), (1,)), ((), ()))
NN = (((1,), (0,)), ((), ()))
MASKED = -1e30


def lower_bound(seg, n, value):
    def step(_, c):
        lo, hi = c
        mid = (lo + hi) // 2
        less = seg[jnp.minimum(mid, n - 1)] < value
        go = lo < hi
        return (jnp.where(go & less, mid + 1, lo), jnp.where(go & ~less, mid, hi))
    lo, hi = lax.fori_loop(0, n.bit_length(), step, (jnp.int32(0), jnp.int32(n)))
    return lo


def key_range(seg, n, tile):
    first = lower_bound(seg, n, seg[tile * TQ])
    end = lower_bound(seg, n, seg[tile * TQ + TQ - 1] + 1)
    return first // TK, (end + TK - 1) // TK


def head_masks(width, heads):
    lane = lax.broadcasted_iota(jnp.int32, (1, width), 1)
    return [(lane // HEAD == h) for h in range(heads)]


def seg_columns(segv_ref, cols, n):
    for t in range(n // 128):
        row = segv_ref[0:1, t * 128:(t + 1) * 128].astype(jnp.float32)
        cols[t * 128:(t + 1) * 128, :] = jnp.broadcast_to(row, (128, 128)).T


def fwd_kernel(n, heads, seg, segv_ref, q_ref, k_ref, v_ref, o_ref, lse_ref, vt, cols, scores):
    tile = pl.program_id(0)
    width = heads * HEAD

    @pl.when(tile == 0)
    def _():
        seg_columns(segv_ref, cols, n)
        for t in range(n // TK):
            vt[:, t * TK:(t + 1) * TK] = v_ref[t * TK:(t + 1) * TK, :].astype(jnp.float32).T.astype(jnp.bfloat16)

    lo, hi = key_range(seg, n, tile)
    q0 = pl.multiple_of(tile * TQ, TQ)
    q = q_ref[...] * jnp.bfloat16(HEAD ** -0.5)
    masks = head_masks(width, heads)
    qm = [jnp.where(m, q, jnp.bfloat16(0)) for m in masks]
    seg_row = segv_ref[0:1, pl.ds(q0, TQ)].astype(jnp.float32)

    def first(b, tops):
        k0 = pl.multiple_of(b * TK, TK)
        keys = k_ref[pl.ds(k0, TK), :]
        col = cols[pl.ds(k0, TK), :]
        same = jnp.concatenate([col] * (TQ // 128), axis=1) == seg_row
        out = []
        for h in range(heads):
            s = lax.dot_general(keys, qm[h], NT, preferred_element_type=jnp.float32)
            s = jnp.where(same, s, MASKED)
            scores[h, pl.ds(k0, TK), :] = s
            out.append(jnp.maximum(tops[h], jnp.max(s, axis=0, keepdims=True)))
        return tuple(out)

    tops = lax.fori_loop(lo, hi, first, tuple(jnp.full((1, TQ), MASKED, jnp.float32) for _ in range(heads)))

    def second(b, acc):
        k0 = pl.multiple_of(b * TK, TK)
        out = []
        for h in range(heads):
            p = jnp.exp(scores[h, pl.ds(k0, TK), :] - tops[h])
            total = acc[h][1] + jnp.sum(p, axis=0, keepdims=True)
            part = lax.dot_general(vt[h * HEAD:(h + 1) * HEAD, pl.ds(k0, TK)], p.astype(jnp.bfloat16), NN, preferred_element_type=jnp.float32)
            out.append((acc[h][0] + part, total))
        return tuple(out)

    acc = lax.fori_loop(lo, hi, second, tuple((jnp.zeros((HEAD, TQ), jnp.float32), jnp.zeros((1, TQ), jnp.float32)) for _ in range(heads)))
    ot = jnp.concatenate([acc[h][0] / acc[h][1] for h in range(heads)], axis=0)
    o_ref[...] = ot.T.astype(jnp.bfloat16)
    lse_ref[...] = jnp.concatenate([tops[h] + jnp.log(acc[h][1]) for h in range(heads)] + [jnp.zeros((8 - heads, TQ), jnp.float32)], axis=0)


def attend_forward(seg, q, k, v):
    n, width = q.shape
    heads = width // HEAD
    whole = pl.BlockSpec(memory_space=pltpu.VMEM)
    return pl.pallas_call(
        functools.partial(fwd_kernel, n, heads),
        grid_spec=pltpu.PrefetchScalarGridSpec(
            num_scalar_prefetch=1,
            grid=(n // TQ,),
            in_specs=[whole, pl.BlockSpec((TQ, width), lambda t, s: (t, 0)), whole, whole],
            out_specs=[pl.BlockSpec((TQ, width), lambda t, s: (t, 0)), pl.BlockSpec((8, TQ), lambda t, s: (0, t))],
            scratch_shapes=[pltpu.VMEM((width, n), jnp.bfloat16), pltpu.VMEM((n, 128), jnp.float32), pltpu.VMEM((heads, n, TQ), jnp.float32)],
        ),
        out_shape=[jax.ShapeDtypeStruct((n, width), jnp.bfloat16), jax.ShapeDtypeStruct((8, n), jnp.float32)],
        compiler_params=pltpu.CompilerParams(vmem_limit_bytes=40 << 20),
        cost_estimate=pl.CostEstimate(flops=4 * heads * n * n * HEAD, bytes_accessed=8 * n * width, transcendentals=heads * n * n // 2),
        name="attend_forward",
    )(seg.reshape(-1), seg.reshape(1, -1), q, k, v)


def bwd_kernel(n, heads, seg, segv_ref, q_ref, k_ref, v_ref, o_ref, do_ref, lse_ref, dq_ref, dk_ref, dv_ref, kt, cols, dk_acc, dv_acc):
    tile = pl.program_id(0)
    width = heads * HEAD

    @pl.when(tile == 0)
    def _():
        seg_columns(segv_ref, cols, n)
        for t in range(n // TK):
            kt[:, t * TK:(t + 1) * TK] = k_ref[t * TK:(t + 1) * TK, :].astype(jnp.float32).T.astype(jnp.bfloat16)
        dk_acc[...] = jnp.zeros_like(dk_acc)
        dv_acc[...] = jnp.zeros_like(dv_acc)

    lo, hi = key_range(seg, n, tile)
    q0 = pl.multiple_of(tile * TQ, TQ)
    masks = head_masks(width, heads)
    q = q_ref[...] * jnp.bfloat16(HEAD ** -0.5)
    do = do_ref[...]
    qm = [jnp.where(m, q, jnp.bfloat16(0)) for m in masks]
    dm = [jnp.where(m, do, jnp.bfloat16(0)) for m in masks]
    seg_row = segv_ref[0:1, pl.ds(q0, TQ)].astype(jnp.float32)
    prod = do.astype(jnp.float32) * o_ref[...].astype(jnp.float32)
    high = prod.astype(jnp.bfloat16)
    rest = (prod - high.astype(jnp.float32)).astype(jnp.bfloat16)
    row = lax.broadcasted_iota(jnp.int32, (16, width), 0)
    lane = lax.broadcasted_iota(jnp.int32, (16, width), 1)
    pick = jnp.where(lane // HEAD == row, 1.0, 0.0).astype(jnp.bfloat16)
    delta = lax.dot_general(pick, high, NT, preferred_element_type=jnp.float32) + lax.dot_general(pick, rest, NT, preferred_element_type=jnp.float32)
    lse = lse_ref[...]

    def body(b, acc):
        k0 = pl.multiple_of(b * TK, TK)
        keys = k_ref[pl.ds(k0, TK), :]
        vals = v_ref[pl.ds(k0, TK), :]
        col = cols[pl.ds(k0, TK), :]
        same = jnp.concatenate([col] * (TQ // 128), axis=1) == seg_row
        out = []
        dks = jnp.zeros((TK, width), jnp.float32)
        dvs = jnp.zeros((TK, width), jnp.float32)
        for h in range(heads):
            s = lax.dot_general(keys, qm[h], NT, preferred_element_type=jnp.float32)
            p = jnp.where(same, jnp.exp(s - lse[h:h + 1, :]), 0.0)
            dp = lax.dot_general(vals, dm[h], NT, preferred_element_type=jnp.float32)
            ds = (p * (dp - delta[h:h + 1, :])).astype(jnp.bfloat16)
            dvs = dvs + lax.dot_general(p.astype(jnp.bfloat16), dm[h], NN, preferred_element_type=jnp.float32)
            dks = dks + lax.dot_general(ds, qm[h], NN, preferred_element_type=jnp.float32)
            out.append(acc[h] + lax.dot_general(kt[h * HEAD:(h + 1) * HEAD, pl.ds(k0, TK)], ds, NN, preferred_element_type=jnp.float32))
        dk_acc[pl.ds(k0, TK), :] += dks
        dv_acc[pl.ds(k0, TK), :] += dvs
        return tuple(out)

    acc = lax.fori_loop(lo, hi, body, tuple(jnp.zeros((HEAD, TQ), jnp.float32) for _ in range(heads)))
    dq_ref[...] = (jnp.concatenate(acc, axis=0).T * HEAD ** -0.5).astype(jnp.bfloat16)

    @pl.when(tile == n // TQ - 1)
    def _():
        dk_ref[...] = dk_acc[...].astype(jnp.bfloat16)
        dv_ref[...] = dv_acc[...].astype(jnp.bfloat16)


def attend_backward(seg, q, k, v, o, do, lse):
    n, width = q.shape
    heads = width // HEAD
    whole = pl.BlockSpec(memory_space=pltpu.VMEM)
    rows = pl.BlockSpec((TQ, width), lambda t, s: (t, 0))
    return pl.pallas_call(
        functools.partial(bwd_kernel, n, heads),
        grid_spec=pltpu.PrefetchScalarGridSpec(
            num_scalar_prefetch=1,
            grid=(n // TQ,),
            in_specs=[whole, rows, whole, whole, rows, rows, pl.BlockSpec((8, TQ), lambda t, s: (0, t))],
            out_specs=[rows, whole, whole],
            scratch_shapes=[pltpu.VMEM((width, n), jnp.bfloat16), pltpu.VMEM((n, 128), jnp.float32), pltpu.VMEM((n, width), jnp.float32), pltpu.VMEM((n, width), jnp.float32)],
        ),
        out_shape=[jax.ShapeDtypeStruct((n, width), jnp.bfloat16)] * 3,
        compiler_params=pltpu.CompilerParams(vmem_limit_bytes=40 << 20),
        cost_estimate=pl.CostEstimate(flops=10 * heads * n * n * HEAD, bytes_accessed=16 * n * width, transcendentals=heads * n * n // 2),
        name="attend_backward",
    )(seg.reshape(-1), seg.reshape(1, -1), q, k, v, o, do, lse)


def local(
    tokens, segment_ids, gene_owner, w_qkv, w_attn_out, w_up, w_down, gain_attn, gain_mlp, cotangent
):
    width = tokens.shape[1]
    dp_count = lax.axis_size("dp")
    capacity = cotangent.shape[0] // dp_count
    own_rows = tokens.shape[0]
    contract_last = (((1,), (1,)), ((), ()))
    contract_first = (((0,), (0,)), ((), ()))
    low = jnp.bfloat16

    def scatter_sum(partial):
        return lax.psum_scatter(partial.astype(low), "mp", scatter_dimension=0, tiled=True).astype(jnp.float32)

    returned = lax.all_to_all(
        cotangent.reshape(dp_count, capacity, width), "dp", split_axis=0, concat_axis=0, tiled=True
    ).reshape(dp_count * capacity, width)
    owners = gene_owner[:, 0]
    place = jnp.arange(own_rows, dtype=jnp.int32)
    earlier = (owners[:, None] == owners[None, :]) & (place[None, :] < place[:, None])
    slots = owners * capacity + jnp.sum(earlier.astype(jnp.int32), axis=1)
    onehot = (slots[:, None] == jnp.arange(dp_count * capacity, dtype=jnp.int32)[None, :]).astype(low)

    tokens_f = tokens.astype(jnp.float32)
    normed_one, unit_one, inverse_one = norm_parts(tokens_f, gain_attn)
    attn_in = lax.all_gather(normed_one.astype(low), "mp", axis=0, tiled=True)
    projected = [jnp.dot(attn_in, w_qkv[p], preferred_element_type=jnp.float32).astype(low) for p in range(3)]
    merged, log_sums = attend_forward(segment_ids, *projected)
    residual = tokens_f + scatter_sum(jnp.dot(merged, w_attn_out, preferred_element_type=jnp.float32))
    normed_two, unit_two, inverse_two = norm_parts(residual, gain_mlp)
    mlp_rows = lax.all_gather(normed_two.astype(low), "mp", axis=0, tiled=True)
    grad_block = jnp.dot(onehot, returned, preferred_element_type=jnp.float32).astype(low)
    grad_rows = lax.all_gather(grad_block, "mp", axis=0, tiled=True)
    pre_act = jnp.dot(mlp_rows, w_up, preferred_element_type=jnp.float32)
    activated = gelu_exact(pre_act).astype(low)
    grad_act = jnp.dot(grad_rows, w_down, preferred_element_type=jnp.float32)
    grad_pre = (grad_act * gelu_slope(pre_act)).astype(low)
    grad_mlp_in = scatter_sum(
        lax.dot_general(grad_pre, w_up, contract_last, preferred_element_type=jnp.float32)
    )
    grad_down_local = lax.dot_general(
        grad_rows, activated, contract_first, preferred_element_type=jnp.float32
    ).astype(low)
    grad_up_local = lax.dot_general(
        mlp_rows, grad_pre, contract_first, preferred_element_type=jnp.float32
    ).astype(low)
    norm_two_grad, gain_mlp_grad = norm_back(grad_mlp_in, unit_two, inverse_two, gain_mlp)
    up_sum, down_sum = lax.psum((grad_up_local, grad_down_local), "dp")
    output = residual + scatter_sum(
        lax.dot_general(activated, w_down, contract_last, preferred_element_type=jnp.float32)
    )
    outgoing = lax.dot_general(
        onehot, output.astype(low), contract_first, preferred_element_type=jnp.float32
    ).astype(low)
    relaid = lax.all_to_all(
        outgoing.reshape(dp_count, capacity, width), "dp", split_axis=0, concat_axis=0, tiled=True
    ).reshape(dp_count * capacity, width)
    grad_residual = grad_block.astype(jnp.float32) + norm_two_grad
    residual_rows = lax.all_gather(grad_residual.astype(low), "mp", axis=0, tiled=True)
    grad_attn_local = lax.dot_general(
        merged, residual_rows, contract_first, preferred_element_type=jnp.float32
    ).astype(low)
    grad_merged = lax.dot_general(
        residual_rows, w_attn_out, contract_last, preferred_element_type=jnp.float32
    ).astype(low)
    grad_proj = attend_backward(segment_ids, *projected, merged, grad_merged, log_sums)
    grad_attn_in = scatter_sum(
        sum(
            lax.dot_general(grad_proj[p], w_qkv[p], contract_last, preferred_element_type=jnp.float32)
            for p in range(3)
        )
    )
    grad_qkv_local = jnp.stack(
        [
            lax.dot_general(attn_in, grad_proj[p], contract_first, preferred_element_type=jnp.float32).astype(low)
            for p in range(3)
        ]
    )
    grad_qkv_local, up_sum, down_sum = lax.optimization_barrier((grad_qkv_local, up_sum, down_sum))
    qkv_sum, attn_sum = lax.psum((grad_qkv_local, grad_attn_local), "dp")
    norm_one_grad, gain_attn_grad = norm_back(grad_attn_in, unit_one, inverse_one, gain_attn)
    grad_tokens = (grad_residual + norm_one_grad).astype(low)
    gain_attn_sum, gain_mlp_sum = lax.psum((gain_attn_grad, gain_mlp_grad), ("dp", "mp"))
    full = jnp.float32
    return (
        relaid,
        grad_tokens,
        qkv_sum.astype(full),
        attn_sum.astype(full),
        up_sum.astype(full),
        down_sum.astype(full),
        gain_attn_sum,
        gain_mlp_sum,
    )


def solution(mesh):
    placed = (
        P(("dp", "mp"), None),
        P("dp", None),
        P(("dp", "mp"), None),
        P(None, None, "mp"),
        P("mp", None),
        P(None, "mp"),
        P(None, "mp"),
        P(),
        P(),
        P(("dp", "mp"), None),
    )
    return jax.shard_map(
        local,
        mesh=mesh,
        in_specs=placed,
        out_specs=(
            P(("dp", "mp"), None),
            P(("dp", "mp"), None),
            P(None, None, "mp"),
            P("mp", None),
            P(None, "mp"),
            P(None, "mp"),
            P(),
            P(),
        ),
        check_vma=False,
    )
```

time: 1000 us -> 608 us (0.61)
  matrix products: 343 us -> 61.9 us
  Pallas kernels: 0 us -> 67.1 us
  waiting for transfers between devices: 399 us -> 338 us
  local copies, waits for them, and re-layouts: 62.1 us -> 10.4 us
  other arithmetic: 59 us -> 26.6 us
  blocking collectives: 97 us -> 82.2 us
  loops' own time: 14.3 us -> 0 us
    dot_general x32 -> x13, matrix products: 305 us -> 28.5 us  [the longest x1 6.21 us: local(): lax.dot_general(activated, w_down, contract_last, preferred_element_type=...]
    pallas_call x0 -> x2, Pallas kernels: none -> 67.1 us  [the longest x1 41.5 us: attend_backward(): pl.pallas_call(functools.partial(bwd_kernel, n, heads), grid_spec=pltpu.P...]
    psum x1 -> x2, waiting for transfers between devices: 150 us -> 110 us  [the longest x1 58.8 us: local(): up_sum, down_sum = lax.psum((grad_up_local, grad_down_local), 'dp')]
    scatter x1 -> x0, local copies, waits for them, and re-layouts: 30.2 us -> none  [local(): outgoing = jnp.zeros((dp_count, capacity, width), jnp.bfloat16).at[owners...]
    reduce_sum x5 -> x1, other arithmetic: 27.4 us -> 0.25 us  [local(): slots = owners * capacity + jnp.sum(earlier.astype(jnp.int32), axis=1)]
    all_gather x3, waiting for transfers between devices: 59.9 us -> 42.1 us  [the longest x1 31.3 us: local(): attn_in = lax.all_gather(normed_one.astype(low), 'mp', axis=0, tiled=True)]
    another operation x2 -> x0, loops' own time: 14.3 us -> none  [the longest x1 11.5 us: attend_backward(): lax.fori_loop(0, block_count, one_block, (empty_grad, empty_grad, empty_g...]
    all_to_all x1, blocking collectives: 55.8 us -> 42.7 us  [local(): lax.all_to_all(outgoing.reshape(dp_count, capacity, width), 'dp', split_a...]
  transfers between devices with their start and end apart: 10 -> 11, of which waited for: 8 -> 10; matrix products, arithmetic and copies ran while one was open for 8% -> 9% of each run, Pallas kernels for 0% -> 7%
where the time goes in v1:
time: 608 us; the launch traced here: 607 us
  waiting for transfers between devices  338 us (56%)
  blocking collectives  82.2 us (14%)
  Pallas kernels  67.1 us (11%)
  matrix products  61.9 us (10%)
  other arithmetic  26.6 us (4%)
  between operations  14.6 us (2%)
  local copies, waits for them, and re-layouts  10.4 us (2%)
  starting transfers between devices  6.34 us (1%)
    reduce_scatter x4, waiting for transfers between devices, scatter_sum(): lax.psum_scatter(partial.astype(low), 'mp', scatter_dimension=0, tiled=True)  142 us
    psum x1, waiting for transfers between devices, local(): up_sum, down_sum = lax.psum((grad_up_local, grad_down_local), 'dp')  58.8 us
    psum x1, waiting for transfers between devices, local(): qkv_sum, attn_sum = lax.psum((grad_qkv_local, grad_attn_local), 'dp')  51.1 us
    all_to_all x1, blocking collectives, local(): lax.all_to_all(outgoing.reshape(dp_count, capacity, width), 'dp', split_a...  42.7 us
    pallas_call x1, Pallas kernels, attend_backward(): pl.pallas_call(functools.partial(bwd_kernel, n, heads), grid_spec=pltpu.P...  41.5 us
    psum x1, blocking collectives, local(): lax.psum((gain_attn_grad, gain_mlp_grad), ('dp', 'mp'))  39.5 us
    all_gather x1, waiting for transfers between devices, local(): attn_in = lax.all_gather(normed_one.astype(low), 'mp', axis=0, tiled=True)  31.3 us
    pallas_call x1, Pallas kernels, attend_forward(): pl.pallas_call(functools.partial(fwd_kernel, n, heads), grid_spec=pltpu.P...  25.6 us
  transfers between devices with their start and end apart: 11, of which 10 were waited for; matrix products, arithmetic and copies ran while one was open for 9% of the time, Pallas kernels for 7%

profile of v1, /device:TPU:0, one launch (start us, length us, event | category | flops | bytes accessed | tf_op | source)
XLA Modules:
  0.0 606.6 jit_solution(3072568540056641908)
XLA Ops:
  11.6 31.3 %all-gather.5.cloned.1.call-done = bf16[2048,768]{1,0:T(8,128)(2,1)} async-done(((bf16[512,768]{1,0:T(8,128)(2,1)}), bf16[2048,768]{1,0:T(8,128)(2,1)}) %all-gather.5.cloned.1.call-update) | async-done | bytes 3145744 | tf_op jit(solution)/shard_map/all_gather | solution.py:248
  48.2 25.6 %attend_forward.1 = (bf16[2048,192]{1,0:T(8,128)(2,1)S(1)}, f32[8,2048]{1,0:T(8,128)S(1)}) custom-call(s32[2048]{0:T(1024)S(1)} %bitcast.60, s32[1,2048]{1,0:T(1,128)S(1)} %copy-done.5, bf16[2048,192]{1,0:T(8,128)(2,1)S(1)} %convolution_convert_fusion.5.q_ref, bf16[2048,192]{1,0:T(8,128)(2,1)S(1)} %convolution_convert_fusion.4.k_ref, ...), custom_call_target="tpu_custom_call" | custom-call | flops 3221225472 | bytes 3145728 | tf_op jit(solution)/shard_map/attend_forward/pallas_call | solution.py:127
  76.5 38.3 %reduce-scatter.5.cloned.1.call-done = bf16[512,768]{1,0:T(8,128)(2,1)} async-done(((bf16[2048,768]{1,0:T(8,128)(2,1)}), bf16[512,768]{1,0:T(8,128)(2,1)}) %reduce-scatter.5.cloned.1.call-update) | async-done | bytes 786448 | tf_op jit(solution)/shard_map/reduce_scatter | solution.py:235
  118.0 5.5 all-to-all-start.1
  123.9 24.2 %all-to-all-done.1 = bf16[8,80,768]{2,1,0:T(8,128)(2,1)} async-done(((bf16[8,80,768]{2,1,0:T(8,128)(2,1)}), bf16[8,80,768]{2,1,0:T(8,128)(2,1)}, u32[]{:S(2)}, u32[]{:S(2)}) %all-to-all-start.1) | async-done | bytes 983072 | tf_op jit(solution)/shard_map/all_to_all | solution.py:237
  151.2 7.4 %multiply_convert_fusion = (bf16[2048,768]{1,0:T(8,128)(2,1)}, f32[2048,768]{1,0:T(8,128)}) fusion(bf16[2048,768]{1,0:T(8,128)(2,1)} %all-gather.7.cloned.1.call-done, bf16[768,768]{1,0:T(8,128)(2,1)S(1)} %copy-done), kind=kOutput, calls=%fused_computation.8 | convolution fusion | flops 2423783424 | bytes 13762560 | tf_op jit(solution)/shard_map/dot_general | solution.py:256
  158.7 19.0 %all-gather.9.cloned.1.call-done = bf16[2048,768]{1,0:T(8,128)(2,1)} async-done(((bf16[512,768]{1,0:T(8,128)(2,1)}), bf16[2048,768]{1,0:T(8,128)(2,1)}) %all-gather.9.cloned.1.call-update) | async-done | bytes 3145744 | tf_op jit(solution)/shard_map/all_gather | solution.py:255
  177.7 6.5 %fusion.5 = bf16[2048,768]{1,0:T(8,128)(2,1)S(1)} fusion(f32[2048,768]{1,0:T(8,128)} %get-tuple-element.37, bf16[2048,768]{1,0:T(8,128)(2,1)} %all-gather.9.cloned.1.call-done, bf16[768,768]{1,0:T(8,128)(2,1)} %param.16), kind=kOutput, calls=%fused_computation.6 | convolution fusion | flops 2431647744 | bytes 13762560 | tf_op jit(solution)/shard_map/dot_general | solution.py:258
  185.9 4.0 convolution_convert_fusion
  190.0 38.1 %reduce-scatter.9.cloned.1.call-done = bf16[512,768]{1,0:T(8,128)(2,1)} async-done(((bf16[2048,768]{1,0:T(8,128)(2,1)}), bf16[512,768]{1,0:T(8,128)(2,1)}) %reduce-scatter.9.cloned.1.call-update) | async-done | bytes 786448 | tf_op jit(solution)/shard_map/reduce_scatter | solution.py:235
  233.1 6.7 %convolution_convert_fusion.8 = bf16[768,768]{1,0:T(8,128)(2,1)} fusion(bf16[2048,768]{1,0:T(8,128)(2,1)} %all-gather.7.cloned.1.call-done, bf16[2048,768]{1,0:T(8,128)(2,1)} %copy-done.33), kind=kOutput, calls=%fused_computation.51 | convolution fusion | flops 2416508928 | bytes 7471104 | tf_op jit(solution)/shard_map/dot_general | solution.py:266
  239.8 3.7 convolution_convert_fusion.7
  244.8 6.2 %convolution_convert_fusion.1 = bf16[2048,768]{1,0:T(8,128)(2,1)} fusion(bf16[2048,768]{1,0:T(8,128)(2,1)} %get-tuple-element.36, bf16[768,768]{1,0:T(8,128)(2,1)S(1)} %copy-done.31), kind=kOutput, calls=%fused_computation.11 | convolution fusion | flops 2417491968 | bytes 7471104 | tf_op jit(solution)/shard_map/dot_general | solution.py:272
  251.0 10.7 %all-gather.11.cloned.1.call-done = bf16[2048,768]{1,0:T(8,128)(2,1)} async-done(((bf16[512,768]{1,0:T(8,128)(2,1)}), bf16[2048,768]{1,0:T(8,128)(2,1)}) %all-gather.11.cloned.1.call-update) | async-done | bytes 3145744 | tf_op jit(solution)/shard_map/all_gather | solution.py:281
  261.8 3.1 convolution_convert_fusion.6
  271.0 41.5 %attend_backward.1 = (bf16[2048,192]{1,0:T(8,128)(2,1)S(1)}, bf16[2048,192]{1,0:T(8,128)(2,1)S(1)}, bf16[2048,192]{1,0:T(8,128)(2,1)S(1)}) custom-call(s32[2048]{0:T(1024)S(1)} %bitcast.61, s32[1,2048]{1,0:T(1,128)S(1)} %copy-done.5, bf16[2048,192]{1,0:T(8,128)(2,1)S(1)} %copy-done.11, bf16[2048,192]{1,0:T(8,128)(2,1)S(1)} %copy-done.9, ...), custom_call_target="tpu_custom_call" | custom-call | flops 8053063680 | bytes 6291456 | tf_op jit(solution)/shard_map/attend_backward/pallas_call | solution.py:207
  316.2 58.8 %all-reduce.8.cloned.1.call-done = (bf16[768,768]{1,0:T(8,128)(2,1)}, bf16[768,768]{1,0:T(8,128)(2,1)}) async-done(((bf16[768,768]{1,0:T(8,128)(2,1)}, bf16[768,768]{1,0:T(8,128)(2,1)}), (bf16[768,768]{1,0:T(8,128)(2,1)}, bf16[768,768]{1,0:T(8,128)(2,1)})) %all-reduce.8.cloned.1.call-update) | async-done | bytes 2359312 | tf_op jit(solution)/shard_map/psum | solution.py:270
  375.0 3.4 convolution_convert_fusion.11
  384.4 30.3 %reduce-scatter.7.cloned.1.call-done = bf16[512,768]{1,0:T(8,128)(2,1)} async-done(((bf16[2048,768]{1,0:T(8,128)(2,1)}), bf16[512,768]{1,0:T(8,128)(2,1)}) %reduce-scatter.7.cloned.1.call-update) | async-done | bytes 786448 | tf_op jit(solution)/shard_map/reduce_scatter | solution.py:235
  416.8 42.7 %all_to_all.10 = bf16[8,80,768]{2,1,0:T(8,128)(2,1)} all-to-all(bf16[8,80,768]{2,1,0:T(8,128)(2,1)S(1)} %bitcast.64), channel_id=1, replica_groups=mesh['dp'=8,'mp'=4] {'dp'}, dimensions={0} | all-to-all | bytes 1966080 | tf_op jit(solution)/shard_map/all_to_all | solution.py:277
  462.9 51.1 %all-reduce.6.cloned.1.call-done = (bf16[3,768,192]{1,2,0:T(8,128)(2,1)}, bf16[192,768]{1,0:T(8,128)(2,1)}) async-done(((bf16[3,768,192]{1,2,0:T(8,128)(2,1)}, bf16[192,768]{1,0:T(8,128)(2,1)}), (bf16[3,768,192]{1,2,0:T(8,128)(2,1)}, bf16[192,768]{1,0:T(8,128)(2,1)})) %all-reduce.6.cloned.1.call-update) | async-done | bytes 1179664 | tf_op jit(solution)/shard_map/psum | solution.py:302
  518.3 35.5 %reduce-scatter.11.cloned.1.call-done = bf16[512,768]{1,0:T(8,128)(2,1)} async-done(((bf16[2048,768]{1,0:T(8,128)(2,1)}), bf16[512,768]{1,0:T(8,128)(2,1)}) %reduce-scatter.11.cloned.1.call-update) | async-done | bytes 786448 | tf_op jit(solution)/shard_map/reduce_scatter | solution.py:235
  555.8 39.5 %all-reduce = (f32[768]{0:T(1024)}, f32[768]{0:T(1024)}) all-reduce(f32[768]{0:T(1024)S(1)} %get-tuple-element.26, f32[768]{0:T(1024)S(1)} %get-tuple-element.24), channel_id=1, replica_groups=mesh['dp'=8,'mp'=4] {'dp','mp'}, use_global_device_ids=true, to_apply=%region_18.0 | all-reduce | flops 1536 | bytes 12288 | tf_op jit(solution)/shard_map/psum | solution.py:305
  595.2 3.5 fusion.20
  (126 shorter events, 55.3 us)
Async XLA Ops:
  7.2 144.1 %copy-start = (bf16[768,768]{1,0:T(8,128)(2,1)S(1)}, bf16[768,768]{1,0:T(8,128)(2,1)}, u32[]{:S(2)}) copy-start(bf16[768,768]{1,0:T(8,128)(2,1)} %param.15) | copy-start | bytes 3538948
  7.2 35.7 %all-gather.5.cloned.1.call-start = ((), (), s32[]{:S(2)}) async-start(), calls=%async_computation.6 | async-start | bytes 3932160 | tf_op jit(solution)/shard_map/all_gather | solution.py:248
  8.7 34.2 %copy-start.22 = (bf16[3,768,192]{1,2,0:T(8,128)(2,1)S(1)}, bf16[3,768,192]{1,2,0:T(8,128)(2,1)}, u32[]{:S(2)}) copy-start(bf16[3,768,192]{1,2,0:T(8,128)(2,1)} %param.13) | copy-start | bytes 2654212
  11.5 103.3 %reduce-scatter.5.cloned.1.call-start = ((), (), s32[]{:S(2)}) async-start(), calls=%async_computation.7 | async-start | bytes 3932160 | tf_op jit(solution)/shard_map/reduce_scatter | solution.py:235
  48.1 25.7 %copy-start.10 = (bf16[2048,192]{1,0:T(8,128)(2,1)}, bf16[2048,192]{1,0:T(8,128)(2,1)S(1)}, u32[]{:S(2)}) copy-start(bf16[2048,192]{1,0:T(8,128)(2,1)S(1)} %convolution_convert_fusion.5.q_ref) | copy-start | bytes 2359300
  48.1 25.7 %copy-start.24 = (bf16[192,768]{1,0:T(8,128)(2,1)S(1)}, bf16[192,768]{1,0:T(8,128)(2,1)}, u32[]{:S(2)}) copy-start(bf16[192,768]{1,0:T(8,128)(2,1)} %param.14) | copy-start | bytes 884740
  76.4 38.4 %copy-start.13 = (bf16[512,768]{1,0:T(8,128)(2,1)S(1)}, bf16[512,768]{1,0:T(8,128)(2,1)}, u32[]{:S(2)}) copy-start(bf16[512,768]{1,0:T(8,128)(2,1)} %param.10) | copy-start | bytes 2359300
  76.4 40.3 %copy-start.25 = (f32[768]{0:T(1024)S(1)}, f32[768]{0:T(1024)}, u32[]{:S(2)}) copy-start(f32[768]{0:T(1024)} %param.18) | copy-start | bytes 9220
  76.5 74.8 %all-gather.7.cloned.1.call-start = ((), (), s32[]{:S(2)}) async-start(), calls=%async_computation.8 | async-start | bytes 3932160 | tf_op jit(solution)/shard_map/all_gather | solution.py:253
  118.0 30.0 %all-to-all-start.1 = ((bf16[8,80,768]{2,1,0:T(8,128)(2,1)}), bf16[8,80,768]{2,1,0:T(8,128)(2,1)}, u32[]{:S(2)}, u32[]{:S(2)}) async-start(bf16[8,80,768]{2,1,0:T(8,128)(2,1)} %bitcast.63), calls=%async_computation.3 | async-start | bytes 1966080 | tf_op jit(solution)/shard_map/all_to_all | solution.py:237
  123.6 54.1 %all-gather.9.cloned.1.call-start = ((), (), s32[]{:S(2)}) async-start(), calls=%async_computation.10 | async-start | bytes 3932160 | tf_op jit(solution)/shard_map/all_gather | solution.py:255
  151.0 77.1 %reduce-scatter.9.cloned.1.call-start = ((), (), s32[]{:S(2)}) async-start(), calls=%async_computation.11 | async-start | bytes 3932160 | tf_op jit(solution)/shard_map/reduce_scatter | solution.py:235
  189.9 38.2 %copy-start.16 = (bf16[512,768]{1,0:T(8,128)(2,1)S(1)}, bf16[512,768]{1,0:T(8,128)(2,1)}, u32[]{:S(2)}) copy-start(bf16[512,768]{1,0:T(8,128)(2,1)} %reduce-scatter.5.cloned.1.call-done) | copy-start | bytes 2359300
  190.0 71.8 %all-gather.11.cloned.1.call-start = ((), (), s32[]{:S(2)}) async-start(), calls=%async_computation.12 | async-start | bytes 3932160 | tf_op jit(solution)/shard_map/all_gather | solution.py:281
  233.1 142.0 %all-reduce.8.cloned.1.call-start = ((), (), s32[]{:S(2)}) async-start(), calls=%async_computation.15 | async-start | bytes 4718592 | tf_op jit(solution)/shard_map/psum | solution.py:270
  233.1 6.7 %copy-start.30 = (bf16[2048,768]{1,0:T(8,128)(2,1)S(1)}, bf16[2048,768]{1,0:T(8,128)(2,1)}, u32[]{:S(2)}) copy-start(bf16[2048,768]{1,0:T(8,128)(2,1)} %all-gather.9.cloned.1.call-done) | copy-start | bytes 9437188
  233.1 6.7 %copy-start.32 = (bf16[2048,768]{1,0:T(8,128)(2,1)S(1)}, bf16[2048,768]{1,0:T(8,128)(2,1)}, u32[]{:S(2)}) copy-start(bf16[2048,768]{1,0:T(8,128)(2,1)} %get-tuple-element.36) | copy-start | bytes 9437188
  243.5 171.2 %reduce-scatter.7.cloned.1.call-start = ((), (), s32[]{:S(2)}) async-start(), calls=%async_computation.9 | async-start | bytes 3932160 | tf_op jit(solution)/shard_map/reduce_scatter | solution.py:235
  251.0 263.0 %all-reduce.6.cloned.1.call-start = ((), (), s32[]{:S(2)}) async-start(), calls=%async_computation.14 | async-start | bytes 2359296 | tf_op jit(solution)/shard_map/psum | solution.py:302
  271.0 41.5 %copy-start.29 = (bf16[2048,768]{1,0:T(8,128)(2,1)S(1)}, bf16[2048,768]{1,0:T(8,128)(2,1)}, u32[]{:S(2)}) copy-start(bf16[2048,768]{1,0:T(8,128)(2,1)} %all-gather.5.cloned.1.call-done) | copy-start | bytes 9437188
  378.5 175.3 %reduce-scatter.11.cloned.1.call-start = ((), (), s32[]{:S(2)}) async-start(), calls=%async_computation.13 | async-start | bytes 3932160 | tf_op jit(solution)/shard_map/reduce_scatter | solution.py:235
  384.4 30.3 %copy-start.14 = (bf16[512,768]{1,0:T(8,128)(2,1)S(1)}, bf16[512,768]{1,0:T(8,128)(2,1)}, u32[]{:S(2)}) copy-start(bf16[512,768]{1,0:T(8,128)(2,1)} %param.10) | copy-start | bytes 2359300
  384.4 30.3 %copy-start.17 = (bf16[512,768]{1,0:T(8,128)(2,1)S(1)}, bf16[512,768]{1,0:T(8,128)(2,1)}, u32[]{:S(2)}) copy-start(bf16[512,768]{1,0:T(8,128)(2,1)} %reduce-scatter.5.cloned.1.call-done) | copy-start | bytes 2359300
  416.8 42.7 %copy-start.21 = (bf16[768,768]{1,0:T(8,128)(2,1)S(1)}, bf16[768,768]{1,0:T(8,128)(2,1)}, u32[]{:S(2)}) copy-start(bf16[768,768]{1,0:T(8,128)(2,1)} %get-tuple-element.22) | copy-start | bytes 3538948
  (21 other events, 45.6 us)
Sparse Core Ops, SparseCore 0:
  11.6 31.2 all-gather.4
  76.6 38.1 reduce-scatter.4
  118.2 28.5 all-gather.6
  151.1 26.5 all-gather.8
  190.1 37.9 reduce-scatter.8
  233.2 28.5 all-gather.10
  265.9 109.0 all-reduce.7
  377.7 36.9 reduce-scatter.6
  418.8 95.0 all-reduce.5
  516.5 37.2 reduce-scatter.10

commit v2 on v1

--- a/solution.py
+++ b/solution.py
@@ -220,6 +220,121 @@
     )(seg.reshape(-1), seg.reshape(1, -1), q, k, v, o, do, lse)
 
 
+MESH_ID = pl.DeviceIdType.MESH
+PARTS = 4
+
+
+def remote(src, dst, send, recv, device):
+    return pltpu.make_async_remote_copy(
+        src_ref=src, dst_ref=dst, send_sem=send, recv_sem=recv, device_id=device, device_id_type=MESH_ID
+    )
+
+
+def greet(devices):
+    barrier = pltpu.get_barrier_semaphore()
+    for device in devices:
+        pl.semaphore_signal(barrier, inc=1, device_id=device, device_id_type=MESH_ID)
+    pl.semaphore_wait(barrier, len(devices))
+
+
+def norm_unit(values):
+    average = jnp.mean(values, axis=-1, keepdims=True)
+    centered = values - average
+    variance = jnp.mean(centered * centered, axis=-1, keepdims=True)
+    inverse = lax.rsqrt(variance + epsilon)
+    return centered * inverse, inverse
+
+
+def project_kernel(
+    dp_count, tokens_ref, gain_ref, w_ref, cot_ref, rows_ref, q_ref, k_ref, v_ref, returned_ref,
+    across_send, across_recv, pair_send, pair_recv, pass_send, pass_recv, slot_send, slot_recv, self_sem,
+):
+    dp, mp = lax.axis_index("dp"), lax.axis_index("mp")
+    pair, across, far = mp ^ 1, mp ^ 2, mp ^ 3
+    own = tokens_ref.shape[0]
+    part = own // PARTS
+    greet([(dp, pair), (dp, across)] + [(lax.rem(dp + k, dp_count), mp) for k in range(1, dp_count)])
+
+    def spot(owner, c, size):
+        return pl.ds(pl.multiple_of(owner * own + c * size, size), size)
+
+    def gather_copy(c, owner, device, send, recv):
+        rows = rows_ref.at[spot(owner, c, part)]
+        return remote(rows, rows, send.at[c], recv.at[c], device)
+
+    def slot_copy(k):
+        other = lax.rem(dp + k, dp_count)
+        return remote(cot_ref.at[other], returned_ref.at[dp], slot_send.at[k], slot_recv.at[k], (other, mp))
+
+    for c in range(PARTS):
+        values = tokens_ref[c * part:(c + 1) * part, :].astype(jnp.float32)
+        unit, _ = norm_unit(values)
+        rows_ref[spot(mp, c, part), :] = (unit * gain_ref[...]).astype(jnp.bfloat16)
+        gather_copy(c, mp, (dp, across), across_send, across_recv).start()
+        gather_copy(c, mp, (dp, pair), pair_send, pair_recv).start()
+    for k in range(1, dp_count):
+        slot_copy(k).start()
+    self_copy = pltpu.make_async_copy(cot_ref.at[dp], returned_ref.at[dp], self_sem)
+    self_copy.start()
+
+    def product(owner, half):
+        where = spot(owner, half, own // 2)
+        rows = rows_ref[where, :]
+        for p, out in enumerate((q_ref, k_ref, v_ref)):
+            out[where, :] = jnp.dot(rows, w_ref[p], preferred_element_type=jnp.float32).astype(jnp.bfloat16)
+
+    def both(owner):
+        def step(half, _):
+            product(owner, half)
+            return 0
+        lax.fori_loop(0, 2, step, 0)
+
+    both(mp)
+    for c in range(PARTS):
+        gather_copy(c, pair, (dp, pair), pair_send, pair_recv).wait_recv()
+    both(pair)
+    for half in range(2):
+        for c in range(half * PARTS // 2, (half + 1) * PARTS // 2):
+            gather_copy(c, across, (dp, across), across_send, across_recv).wait_recv()
+            gather_copy(c, across, (dp, pair), pass_send, pass_recv).start()
+        product(across, half)
+    for half in range(2):
+        for c in range(half * PARTS // 2, (half + 1) * PARTS // 2):
+            gather_copy(c, far, (dp, pair), pass_send, pass_recv).wait_recv()
+        product(far, half)
+    for c in range(PARTS):
+        gather_copy(c, mp, (dp, across), across_send, across_recv).wait_send()
+        gather_copy(c, mp, (dp, pair), pair_send, pair_recv).wait_send()
+        gather_copy(c, across, (dp, pair), pass_send, pass_recv).wait_send()
+    self_copy.wait()
+    for k in range(1, dp_count):
+        slot_copy(k).wait_send()
+        other = lax.rem(dp + dp_count - k, dp_count)
+        remote(cot_ref.at[dp], returned_ref.at[other], slot_send.at[k], slot_recv.at[k], (other, mp)).wait_recv()
+
+
+def project(tokens, gain, w_qkv, cot):
+    own, width = tokens.shape
+    dp_count = cot.shape[0]
+    total = own * 4
+    cols = w_qkv.shape[2]
+    vmem = pl.BlockSpec(memory_space=pltpu.VMEM)
+    hbm = pl.BlockSpec(memory_space=pl.ANY)
+    dma = pltpu.SemaphoreType.DMA
+    return pl.pallas_call(
+        functools.partial(project_kernel, dp_count),
+        out_shape=[jax.ShapeDtypeStruct((total, width), jnp.bfloat16)]
+        + [jax.ShapeDtypeStruct((total, cols), jnp.bfloat16)] * 3
+        + [jax.ShapeDtypeStruct(cot.shape, cot.dtype)],
+        in_specs=[vmem, vmem, vmem, hbm],
+        out_specs=[vmem] * 4 + [hbm],
+        scratch_shapes=[dma((PARTS,))] * 6 + [dma((dp_count,))] * 2 + [dma],
+        compiler_params=pltpu.CompilerParams(collective_id=1, has_side_effects=True, vmem_limit_bytes=40 << 20),
+        cost_estimate=pl.CostEstimate(flops=6 * total * width * cols, bytes_accessed=10 * total * width, transcendentals=0),
+        name="project",
+    )(tokens, gain, w_qkv, cot)
+
+
 def local(
     tokens, segment_ids, gene_owner, w_qkv, w_attn_out, w_up, w_down, gain_attn, gain_mlp, cotangent
 ):
@@ -234,9 +349,6 @@
     def scatter_sum(partial):
         return lax.psum_scatter(partial.astype(low), "mp", scatter_dimension=0, tiled=True).astype(jnp.float32)
 
-    returned = lax.all_to_all(
-        cotangent.reshape(dp_count, capacity, width), "dp", split_axis=0, concat_axis=0, tiled=True
-    ).reshape(dp_count * capacity, width)
     owners = gene_owner[:, 0]
     place = jnp.arange(own_rows, dtype=jnp.int32)
     earlier = (owners[:, None] == owners[None, :]) & (place[None, :] < place[:, None])
@@ -245,8 +357,10 @@
 
     tokens_f = tokens.astype(jnp.float32)
     normed_one, unit_one, inverse_one = norm_parts(tokens_f, gain_attn)
-    attn_in = lax.all_gather(normed_one.astype(low), "mp", axis=0, tiled=True)
-    projected = [jnp.dot(attn_in, w_qkv[p], preferred_element_type=jnp.float32).astype(low) for p in range(3)]
+    attn_in, *projected, returned = project(
+        tokens, gain_attn.reshape(1, -1), w_qkv, cotangent.reshape(dp_count, capacity, width)
+    )
+    returned = returned.reshape(dp_count * capacity, width)
     merged, log_sums = attend_forward(segment_ids, *projected)
     residual = tokens_f + scatter_sum(jnp.dot(merged, w_attn_out, preferred_element_type=jnp.float32))
     normed_two, unit_two, inverse_two = norm_parts(residual, gain_mlp)

time: 608 us -> 603 us (level)
  blocking collectives: 82.2 us -> 39.4 us
  Pallas kernels: 67.1 us -> 94.1 us
  waiting for transfers between devices: 338 us -> 347 us
  local copies, waits for them, and re-layouts: 10.4 us -> 16.7 us
    all_to_all x1 -> x0, blocking collectives: 42.7 us -> none  [local(): lax.all_to_all(outgoing.reshape(dp_count, capacity, width), 'dp', split_a...]
    all_gather x1 -> x0, waiting for transfers between devices: 31.3 us -> none  [local(): attn_in = lax.all_gather(normed_one.astype(low), 'mp', axis=0, tiled=True)]
    pallas_call x0 -> x1, Pallas kernels: none -> 27.1 us  [project(): pl.pallas_call(functools.partial(project_kernel, dp_count), out_shape=[ja...]
    all_gather x1, waiting for transfers between devices: 0.02 us -> 25.4 us  [local(): mlp_rows = lax.all_gather(normed_two.astype(low), 'mp', axis=0, tiled=True)]
    all_to_all x1, waiting for transfers between devices: 24.2 us -> 37 us  [local(): lax.all_to_all(outgoing.reshape(dp_count, capacity, width), 'dp', split_a...]
    unnamed x69 -> x80, local copies, waits for them, and re-layouts: 9.06 us -> 14.5 us
  transfers between devices with their start and end apart: 11 -> 10, of which waited for: 10 -> 10; matrix products, arithmetic and copies ran while one was open for 9% -> 9% of each run, Pallas kernels for 7% -> 7%
where the time goes in v2:
time: 603 us; the launch traced here: 602 us
  waiting for transfers between devices  347 us (58%)
  Pallas kernels  94.1 us (16%)
  matrix products  58.2 us (10%)
  blocking collectives  39.4 us (7%)
  other arithmetic  25.7 us (4%)
  local copies, waits for them, and re-layouts  16.7 us (3%)
  between operations  14.2 us (2%)
  starting transfers between devices  6.28 us (1%)
    reduce_scatter x4, waiting for transfers between devices, scatter_sum(): lax.psum_scatter(partial.astype(low), 'mp', scatter_dimension=0, tiled=True)  143 us
    psum x1, waiting for transfers between devices, local(): up_sum, down_sum = lax.psum((grad_up_local, grad_down_local), 'dp')  58.7 us
    psum x1, waiting for transfers between devices, local(): qkv_sum, attn_sum = lax.psum((grad_qkv_local, grad_attn_local), 'dp')  49.3 us
    pallas_call x1, Pallas kernels, attend_backward(): pl.pallas_call(functools.partial(bwd_kernel, n, heads), grid_spec=pltpu.P...  41.4 us
    psum x1, blocking collectives, local(): lax.psum((gain_attn_grad, gain_mlp_grad), ('dp', 'mp'))  39.4 us
    all_to_all x1, waiting for transfers between devices, local(): lax.all_to_all(outgoing.reshape(dp_count, capacity, width), 'dp', split_a...  37 us
    pallas_call x1, Pallas kernels, project(): pl.pallas_call(functools.partial(project_kernel, dp_count), out_shape=[ja...  27.1 us
    pallas_call x1, Pallas kernels, attend_forward(): pl.pallas_call(functools.partial(fwd_kernel, n, heads), grid_spec=pltpu.P...  25.6 us
  transfers between devices with their start and end apart: 10, of which 10 were waited for; matrix products, arithmetic and copies ran while one was open for 9% of the time, Pallas kernels for 7%

profile of v2, /device:TPU:0, one launch (start us, length us, event | category | flops | bytes accessed | tf_op | source)
XLA Modules:
  0.0 601.7 jit_solution(1688677965167487163)
XLA Ops:
  10.8 27.1 %project.1 = (bf16[2048,768]{1,0:T(8,128)(2,1)S(1)}, bf16[2048,192]{1,0:T(8,128)(2,1)S(1)}, bf16[2048,192]{1,0:T(8,128)(2,1)S(1)}, bf16[2048,192]{1,0:T(8,128)(2,1)S(1)}, bf16[8,80,768]{2,1,0:T(8,128)(2,1)S(1)}) custom-call(bf16[512,768]{1,0:T(8,128)(2,1)S(1)} %copy-done.2, f32[1,768]{1,0:T(1,128)S(1)} %reshape.80.gain_ref, ...), custom_call_target="tpu_custom_call" | custom-call | flops 1811939328 | bytes 15728640 | tf_op jit(solution)/shard_map/project/pallas_call | solution.py:324
  40.6 25.6 %attend_forward.1 = (bf16[2048,192]{1,0:T(8,128)(2,1)S(1)}, f32[8,2048]{1,0:T(8,128)S(1)}) custom-call(s32[2048]{0:T(1024)S(1)} %bitcast.52, s32[1,2048]{1,0:T(1,128)S(1)} %copy-done.9, bf16[2048,192]{1,0:T(8,128)(2,1)S(1)} %get-tuple-element.21.q_ref, bf16[2048,192]{1,0:T(8,128)(2,1)S(1)} %get-tuple-element.22.k_ref, ...), custom_call_target="tpu_custom_call" | custom-call | flops 3221225472 | bytes 3145728 | tf_op jit(solution)/shard_map/attend_forward/pallas_call | solution.py:127
  68.9 40.2 %reduce-scatter.5.cloned.1.call-done = bf16[512,768]{1,0:T(8,128)(2,1)} async-done(((bf16[2048,768]{1,0:T(8,128)(2,1)}), bf16[512,768]{1,0:T(8,128)(2,1)}) %reduce-scatter.5.cloned.1.call-update) | async-done | bytes 786448 | tf_op jit(solution)/shard_map/reduce_scatter | solution.py:350
  115.6 25.4 %all-gather.4.cloned.1.call-done = bf16[2048,768]{1,0:T(8,128)(2,1)} async-done(((bf16[512,768]{1,0:T(8,128)(2,1)}), bf16[2048,768]{1,0:T(8,128)(2,1)}) %all-gather.4.cloned.1.call-update) | async-done | bytes 3145744 | tf_op jit(solution)/shard_map/all_gather | solution.py:367
  141.0 7.5 %multiply_convert_fusion = (bf16[2048,768]{1,0:T(8,128)(2,1)}, f32[2048,768]{1,0:T(8,128)}) fusion(bf16[2048,768]{1,0:T(8,128)(2,1)} %all-gather.4.cloned.1.call-done, bf16[768,768]{1,0:T(8,128)(2,1)S(1)} %copy-done), kind=kOutput, calls=%fused_computation.8 | convolution fusion | flops 2423783424 | bytes 13762560 | tf_op jit(solution)/shard_map/dot_general | solution.py:370
  148.5 22.7 %all-gather.6.cloned.1.call-done = bf16[2048,768]{1,0:T(8,128)(2,1)} async-done(((bf16[512,768]{1,0:T(8,128)(2,1)}), bf16[2048,768]{1,0:T(8,128)(2,1)}) %all-gather.6.cloned.1.call-update) | async-done | bytes 3145744 | tf_op jit(solution)/shard_map/all_gather | solution.py:369
  171.2 6.6 %fusion.5 = bf16[2048,768]{1,0:T(8,128)(2,1)S(1)} fusion(f32[2048,768]{1,0:T(8,128)} %get-tuple-element.50, bf16[2048,768]{1,0:T(8,128)(2,1)} %all-gather.6.cloned.1.call-done, bf16[768,768]{1,0:T(8,128)(2,1)} %param.16), kind=kOutput, calls=%fused_computation.6 | convolution fusion | flops 2431647744 | bytes 13762560 | tf_op jit(solution)/shard_map/dot_general | solution.py:372
  179.4 4.0 convolution_convert_fusion
  183.7 37.9 %reduce-scatter.9.cloned.1.call-done = bf16[512,768]{1,0:T(8,128)(2,1)} async-done(((bf16[2048,768]{1,0:T(8,128)(2,1)}), bf16[512,768]{1,0:T(8,128)(2,1)}) %reduce-scatter.9.cloned.1.call-update) | async-done | bytes 786448 | tf_op jit(solution)/shard_map/reduce_scatter | solution.py:350
  227.1 6.7 %convolution_convert_fusion.5 = bf16[768,768]{1,0:T(8,128)(2,1)} fusion(bf16[2048,768]{1,0:T(8,128)(2,1)} %all-gather.4.cloned.1.call-done, bf16[2048,768]{1,0:T(8,128)(2,1)} %copy-done.38), kind=kOutput, calls=%fused_computation.46 | convolution fusion | flops 2416508928 | bytes 7471104 | tf_op jit(solution)/shard_map/dot_general | solution.py:380
  233.8 3.8 convolution_convert_fusion.4
  237.6 6.5 %convolution_convert_fusion.1 = bf16[2048,768]{1,0:T(8,128)(2,1)} fusion(bf16[2048,768]{1,0:T(8,128)(2,1)} %get-tuple-element.49, bf16[768,768]{1,0:T(8,128)(2,1)} %param.16), kind=kOutput, calls=%fused_computation.11 | convolution fusion | flops 2417491968 | bytes 7471104 | tf_op jit(solution)/shard_map/dot_general | solution.py:386
  244.5 11.2 %all-gather.8.cloned.1.call-done = bf16[2048,768]{1,0:T(8,128)(2,1)} async-done(((bf16[512,768]{1,0:T(8,128)(2,1)}), bf16[2048,768]{1,0:T(8,128)(2,1)}) %all-gather.8.cloned.1.call-update) | async-done | bytes 3145744 | tf_op jit(solution)/shard_map/all_gather | solution.py:395
  265.0 41.4 %attend_backward.1 = (bf16[2048,192]{1,0:T(8,128)(2,1)S(1)}, bf16[2048,192]{1,0:T(8,128)(2,1)S(1)}, bf16[2048,192]{1,0:T(8,128)(2,1)S(1)}) custom-call(s32[2048]{0:T(1024)S(1)} %bitcast.53, s32[1,2048]{1,0:T(1,128)S(1)} %copy-done.9, bf16[2048,192]{1,0:T(8,128)(2,1)S(1)} %copy-done.14, bf16[2048,192]{1,0:T(8,128)(2,1)S(1)} %copy-done.16, ...), custom_call_target="tpu_custom_call" | custom-call | flops 8053063680 | bytes 6291456 | tf_op jit(solution)/shard_map/attend_backward/pallas_call | solution.py:207
  310.1 58.7 %all-reduce.8.cloned.1.call-done = (bf16[768,768]{1,0:T(8,128)(2,1)}, bf16[768,768]{1,0:T(8,128)(2,1)}) async-done(((bf16[768,768]{1,0:T(8,128)(2,1)}, bf16[768,768]{1,0:T(8,128)(2,1)}), (bf16[768,768]{1,0:T(8,128)(2,1)}, bf16[768,768]{1,0:T(8,128)(2,1)})) %all-reduce.8.cloned.1.call-update) | async-done | bytes 2359312 | tf_op jit(solution)/shard_map/psum | solution.py:384
  368.8 3.4 convolution_convert_fusion.8
  379.4 29.1 %reduce-scatter.7.cloned.1.call-done = bf16[512,768]{1,0:T(8,128)(2,1)} async-done(((bf16[2048,768]{1,0:T(8,128)(2,1)}), bf16[512,768]{1,0:T(8,128)(2,1)}) %reduce-scatter.7.cloned.1.call-update) | async-done | bytes 786448 | tf_op jit(solution)/shard_map/reduce_scatter | solution.py:350
  411.5 5.5 all-to-all-start
  417.0 37.0 %all-to-all-done = bf16[8,80,768]{2,1,0:T(8,128)(2,1)S(1)} async-done(((bf16[8,80,768]{2,1,0:T(8,128)(2,1)}), bf16[8,80,768]{2,1,0:T(8,128)(2,1)S(1)}, u32[]{:S(2)}, u32[]{:S(2)}) %all-to-all-start) | async-done | bytes 983072 | tf_op jit(solution)/shard_map/all_to_all | solution.py:391
  454.0 3.2 convert_element_type.119
  458.9 49.3 %all-reduce.6.cloned.1.call-done = (bf16[3,768,192]{1,2,0:T(8,128)(2,1)}, bf16[192,768]{1,0:T(8,128)(2,1)}) async-done(((bf16[3,768,192]{1,2,0:T(8,128)(2,1)}, bf16[192,768]{1,0:T(8,128)(2,1)}), (bf16[3,768,192]{1,2,0:T(8,128)(2,1)}, bf16[192,768]{1,0:T(8,128)(2,1)})) %all-reduce.6.cloned.1.call-update) | async-done | bytes 1179664 | tf_op jit(solution)/shard_map/psum | solution.py:416
  512.6 35.5 %reduce-scatter.11.cloned.1.call-done = bf16[512,768]{1,0:T(8,128)(2,1)} async-done(((bf16[2048,768]{1,0:T(8,128)(2,1)}), bf16[512,768]{1,0:T(8,128)(2,1)}) %reduce-scatter.11.cloned.1.call-update) | async-done | bytes 786448 | tf_op jit(solution)/shard_map/reduce_scatter | solution.py:350
  551.3 39.4 %all-reduce = (f32[768]{0:T(1024)}, f32[768]{0:T(1024)}) all-reduce(f32[768]{0:T(1024)S(1)} %get-tuple-element.36, f32[768]{0:T(1024)S(1)} %get-tuple-element.34), channel_id=1, replica_groups=mesh['dp'=8,'mp'=4] {'dp','mp'}, use_global_device_ids=true, to_apply=%region_18.0 | all-reduce | flops 1536 | bytes 12288 | tf_op jit(solution)/shard_map/psum | solution.py:419
  590.7 3.5 fusion.18
  (129 shorter events, 56.2 us)
Async XLA Ops:
  7.2 133.8 %copy-start = (bf16[768,768]{1,0:T(8,128)(2,1)S(1)}, bf16[768,768]{1,0:T(8,128)(2,1)}, u32[]{:S(2)}) copy-start(bf16[768,768]{1,0:T(8,128)(2,1)} %param.15) | copy-start | bytes 3538948
  7.2 101.9 %reduce-scatter.5.cloned.1.call-start = ((), (), s32[]{:S(2)}) async-start(), calls=%async_computation.5 | async-start | bytes 3932160 | tf_op jit(solution)/shard_map/reduce_scatter | solution.py:350
  10.8 29.8 %copy-start.9 = (s32[1,2048]{1,0:T(1,128)S(1)}, s32[1,2048]{1,0:T(1,128)}, u32[]{:S(2)}) copy-start(s32[1,2048]{1,0:T(1,128)} %segv_ref.3) | copy-start | bytes 24580
  39.7 26.5 %copy-start.13 = (bf16[2048,192]{1,0:T(8,128)(2,1)}, bf16[2048,192]{1,0:T(8,128)(2,1)S(1)}, u32[]{:S(2)}) copy-start(bf16[2048,192]{1,0:T(8,128)(2,1)S(1)} %get-tuple-element.21.q_ref) | copy-start | bytes 2359300
  39.7 26.5 %copy-start.15 = (bf16[2048,192]{1,0:T(8,128)(2,1)}, bf16[2048,192]{1,0:T(8,128)(2,1)S(1)}, u32[]{:S(2)}) copy-start(bf16[2048,192]{1,0:T(8,128)(2,1)S(1)} %get-tuple-element.22.k_ref) | copy-start | bytes 2359300
  39.7 26.5 %copy-start.17 = (bf16[2048,192]{1,0:T(8,128)(2,1)}, bf16[2048,192]{1,0:T(8,128)(2,1)S(1)}, u32[]{:S(2)}) copy-start(bf16[2048,192]{1,0:T(8,128)(2,1)S(1)} %get-tuple-element.23.v_ref) | copy-start | bytes 2359300
  40.6 25.6 %copy-start.28 = (bf16[192,768]{1,0:T(8,128)(2,1)S(1)}, bf16[192,768]{1,0:T(8,128)(2,1)}, u32[]{:S(2)}) copy-start(bf16[192,768]{1,0:T(8,128)(2,1)} %param.14) | copy-start | bytes 884740
  68.8 42.2 %copy-start.29 = (f32[768]{0:T(1024)S(1)}, f32[768]{0:T(1024)}, u32[]{:S(2)}) copy-start(f32[768]{0:T(1024)} %param.18) | copy-start | bytes 9220
  68.9 72.1 %all-gather.4.cloned.1.call-start = ((), (), s32[]{:S(2)}) async-start(), calls=%async_computation.6 | async-start | bytes 3932160 | tf_op jit(solution)/shard_map/all_gather | solution.py:367
  112.3 58.9 %all-gather.6.cloned.1.call-start = ((), (), s32[]{:S(2)}) async-start(), calls=%async_computation.8 | async-start | bytes 3932160 | tf_op jit(solution)/shard_map/all_gather | solution.py:369
  115.6 106.0 %reduce-scatter.9.cloned.1.call-start = ((), (), s32[]{:S(2)}) async-start(), calls=%async_computation.9 | async-start | bytes 3932160 | tf_op jit(solution)/shard_map/reduce_scatter | solution.py:350
  183.4 38.2 %copy-start.20 = (bf16[512,768]{1,0:T(8,128)(2,1)S(1)}, bf16[512,768]{1,0:T(8,128)(2,1)}, u32[]{:S(2)}) copy-start(bf16[512,768]{1,0:T(8,128)(2,1)} %reduce-scatter.5.cloned.1.call-done) | copy-start | bytes 2359300
  183.4 72.3 %all-gather.8.cloned.1.call-start = ((), (), s32[]{:S(2)}) async-start(), calls=%async_computation.10 | async-start | bytes 3932160 | tf_op jit(solution)/shard_map/all_gather | solution.py:395
  223.9 324.3 %copy-start.31 = (f32[512]{0:T(512)}, f32[512]{0:T(512)S(1)}, u32[]{:S(2)}) copy-start(f32[512]{0:T(512)S(1)} %get-tuple-element.51) | copy-start | bytes 6148
  227.0 141.8 %all-reduce.8.cloned.1.call-start = ((), (), s32[]{:S(2)}) async-start(), calls=%async_computation.13 | async-start | bytes 4718592 | tf_op jit(solution)/shard_map/psum | solution.py:384
  237.6 171.0 %reduce-scatter.7.cloned.1.call-start = ((), (), s32[]{:S(2)}) async-start(), calls=%async_computation.7 | async-start | bytes 3932160 | tf_op jit(solution)/shard_map/reduce_scatter | solution.py:350
  244.2 264.0 %all-reduce.6.cloned.1.call-start = ((), (), s32[]{:S(2)}) async-start(), calls=%async_computation.12 | async-start | bytes 2359296 | tf_op jit(solution)/shard_map/psum | solution.py:416
  265.0 41.4 %copy-start.12 = (bf16[2048,768]{1,0:T(8,128)(2,1)S(1)}, bf16[2048,768]{1,0:T(8,128)(2,1)}, u32[]{:S(2)}) copy-start(bf16[2048,768]{1,0:T(8,128)(2,1)} %copy-done.11) | copy-start | bytes 9437188
  372.3 175.9 %reduce-scatter.11.cloned.1.call-start = ((), (), s32[]{:S(2)}) async-start(), calls=%async_computation.11 | async-start | bytes 3932160 | tf_op jit(solution)/shard_map/reduce_scatter | solution.py:350
  379.4 29.1 %copy-start.21 = (bf16[512,768]{1,0:T(8,128)(2,1)S(1)}, bf16[512,768]{1,0:T(8,128)(2,1)}, u32[]{:S(2)}) copy-start(bf16[512,768]{1,0:T(8,128)(2,1)} %reduce-scatter.5.cloned.1.call-done) | copy-start | bytes 2359300
  411.5 42.6 %all-to-all-start = ((bf16[8,80,768]{2,1,0:T(8,128)(2,1)}), bf16[8,80,768]{2,1,0:T(8,128)(2,1)S(1)}, u32[]{:S(2)}, u32[]{:S(2)}) async-start(bf16[8,80,768]{2,1,0:T(8,128)(2,1)} %bitcast.56), calls=%async_computation.2 | async-start | bytes 1966080 | tf_op jit(solution)/shard_map/all_to_all | solution.py:391
  417.0 131.2 %copy-start.33 = (f32[512]{0:T(512)}, f32[512]{0:T(512)S(1)}, u32[]{:S(2)}) copy-start(f32[512]{0:T(512)S(1)} %add_rsqrt_fusion) | copy-start | bytes 6148
  508.2 40.0 %copy-start.30 = (f32[768]{0:T(1024)S(1)}, f32[768]{0:T(1024)}, u32[]{:S(2)}) copy-start(f32[768]{0:T(1024)} %param.17) | copy-start | bytes 9220
  510.0 80.6 %copy-start.22 = (bf16[512,768]{1,0:T(8,128)(2,1)S(1)}, bf16[512,768]{1,0:T(8,128)(2,1)}, u32[]{:S(2)}) copy-start(bf16[512,768]{1,0:T(8,128)(2,1)} %convolution_convert_fusion.7) | copy-start | bytes 2359300
  (25 other events, 59.5 us)
Sparse Core Ops, SparseCore 0:
  69.0 40.0 reduce-scatter.4
  112.4 28.5 all-gather.3
  142.6 28.5 all-gather.5
  183.6 37.9 reduce-scatter.8
  227.1 28.5 all-gather.7
  259.7 109.0 all-reduce.7
  371.5 36.9 reduce-scatter.6
  412.6 95.5 all-reduce.5
  510.9 37.2 reduce-scatter.10

commit v3 on v2

--- a/solution.py
+++ b/solution.py
@@ -41,6 +41,7 @@
 TK = 256
 NT = (((1,), (1,)), ((), ()))
 NN = (((1,), (0,)), ((), ()))
+TN = (((0,), (0,)), ((), ()))
 MASKED = -1e30
 
 
@@ -335,6 +336,229 @@
     )(tokens, gain, w_qkv, cot)
 
 
+def gelu_and_slope(values):
+    cumulative = 0.5 * (1.0 + lax.erf(values * 0.7071067811865476))
+    density = jnp.exp(-0.5 * values * values) * 0.3989422804014327
+    return values * cumulative, cumulative + values * density
+
+
+def middle_kernel(
+    merged_ref, w_out_ref, tokens_ref, gain_ref, w_up_ref, w_down_ref, grad_own_ref, grad_across_ref,
+    back_rows_ref, grad_merged_ref, grad_residual_ref, output_ref, d_up_ref, d_down_ref, d_out_ref,
+    mlp_rows, grad_rows, active, grad_pre, residual, mine, bufs,
+    sum_send, sum_recv, row_send, row_recv, grad_send, grad_recv, self_sem,
+):
+    low, full = jnp.bfloat16, jnp.float32
+    dp, mp = lax.axis_index("dp"), lax.axis_index("mp")
+    pair, across, far = mp ^ 1, mp ^ 2, mp ^ 3
+    own, width = tokens_ref.shape
+    part = own // PARTS
+    to_pair, to_across = (dp, pair), (dp, across)
+    greet([to_pair, to_across])
+
+    def spot(owner, c=None):
+        if c is None:
+            return pl.ds(pl.multiple_of(owner * own, own), own)
+        return pl.ds(pl.multiple_of(owner * own + c * part, part), part)
+
+    def piece(c):
+        return pl.ds(pl.multiple_of(c * part, part), part)
+
+    def grad_copy(i, owner, src):
+        return remote(src, grad_rows.at[spot(owner)], grad_send.at[i], grad_recv.at[i], to_pair)
+
+    local_copies = [
+        pltpu.make_async_copy(grad_own_ref, grad_rows.at[spot(mp)], self_sem.at[0]),
+        pltpu.make_async_copy(grad_across_ref, grad_rows.at[spot(across)], self_sem.at[1]),
+    ]
+
+    FAR, ACROSS, PAIR = 0, 1, 2
+
+    def sum_copy(which, kind, c):
+        src, dst = bufs.at[which, 0, kind, piece(c)], bufs.at[which, 1, kind, piece(c)]
+        return remote(src, dst, sum_send.at[which, kind, c], sum_recv.at[which, kind, c], to_across if kind == ACROSS else to_pair)
+
+    def arrived(which, kind, c):
+        sum_copy(which, kind, c).wait_recv()
+        return bufs[which, 1, kind, piece(c), :].astype(full)
+
+    def ship(which, kind, c, values):
+        bufs[which, 0, kind, piece(c), :] = values.astype(low)
+        sum_copy(which, kind, c).start()
+
+    def row_copy(which, kind, c, owner, ref):
+        rows = ref.at[spot(owner, c)]
+        return remote(rows, rows, row_send.at[which, kind, c], row_recv.at[which, kind, c], to_across if kind == 0 else to_pair)
+
+    def each(count, body):
+        def step(i, _):
+            body(i)
+            return 0
+        lax.fori_loop(0, count, step, 0)
+
+    def out_part(owner):
+        return jnp.dot(merged_ref[spot(owner), :], w_out_ref[...], preferred_element_type=full)
+
+    bufs[0, 0, FAR] = out_part(far).astype(low)
+    each(PARTS, lambda c: sum_copy(0, FAR, c).start())
+    mine[0] = out_part(across)
+
+    def pass_across(c):
+        ship(0, ACROSS, c, mine[0, piece(c), :] + arrived(0, FAR, c))
+    each(PARTS, pass_across)
+    bufs[0, 0, PAIR] = out_part(pair).astype(low)
+    each(PARTS, lambda c: sum_copy(0, PAIR, c).start())
+    for copy in local_copies:
+        copy.start()
+    grad_copy(0, mp, grad_own_ref).start()
+    grad_copy(1, across, grad_across_ref).start()
+    mine[0] = out_part(mp) + tokens_ref[...].astype(full)
+    for copy in local_copies:
+        copy.wait()
+    grad_copy(0, pair, grad_own_ref).wait_recv()
+    grad_copy(1, far, grad_across_ref).wait_recv()
+
+    blocks = w_up_ref.shape[1] // 256
+    both = 2 * part
+
+    def mlp(first, second, c):
+        rows = jnp.concatenate([mlp_rows[spot(first, c), :], mlp_rows[spot(second, c), :]], axis=0)
+        grads = jnp.concatenate([grad_rows[spot(first, c), :], grad_rows[spot(second, c), :]], axis=0)
+
+        def block(b):
+            cols = pl.ds(pl.multiple_of(b * 256, 256), 256)
+            pre = jnp.dot(rows, w_up_ref[:, cols], preferred_element_type=full)
+            value, slope = gelu_and_slope(pre)
+            value = value.astype(low)
+            active[spot(first, c), cols] = value[:part]
+            active[spot(second, c), cols] = value[part:]
+            back = (jnp.dot(grads, w_down_ref[:, cols], preferred_element_type=full) * slope).astype(low)
+            grad_pre[spot(first, c), cols] = back[:part]
+            grad_pre[spot(second, c), cols] = back[part:]
+        each(blocks, block)
+        back = jnp.concatenate([grad_pre[spot(first, c), :], grad_pre[spot(second, c), :]], axis=0)
+        return lax.dot_general(back, w_up_ref[...], NT, preferred_element_type=full)
+
+    def near(c):
+        values = mine[0, piece(c), :] + arrived(0, PAIR, c) + arrived(0, ACROSS, c)
+        residual[piece(c), :] = values
+        unit, _ = norm_unit(values)
+        mlp_rows[spot(mp, c), :] = (unit * gain_ref[...]).astype(low)
+        row_copy(0, 0, c, mp, mlp_rows).start()
+        row_copy(0, 1, c, mp, mlp_rows).start()
+        row_copy(0, 1, c, pair, mlp_rows).wait_recv()
+        got = mlp(mp, pair, c)
+        mine[1, piece(c), :] = got[:part]
+        ship(1, PAIR, c, got[part:])
+    each(PARTS, near)
+
+    def distant(c):
+        row_copy(0, 0, c, across, mlp_rows).wait_recv()
+        row_copy(0, 2, c, across, mlp_rows).start()
+        row_copy(0, 2, c, far, mlp_rows).wait_recv()
+        got = mlp(far, across, c)
+        ship(1, FAR, c, got[:part])
+        ship(1, ACROSS, c, got[part:] + arrived(1, FAR, c))
+    each(PARTS, distant)
+
+    def weight_block(b):
+        cols = pl.ds(pl.multiple_of(b * 256, 256), 256)
+        d_down_ref[cols, :] = lax.dot_general(grad_rows[:, cols], active[...], TN, preferred_element_type=full).astype(low)
+        d_up_ref[cols, :] = lax.dot_general(mlp_rows[:, cols], grad_pre[...], TN, preferred_element_type=full).astype(low)
+    each(width // 256, weight_block)
+
+    def down_part(owner):
+        return lax.dot_general(active[spot(owner), :], w_down_ref[...], NT, preferred_element_type=full)
+
+    bufs[2, 0, FAR] = down_part(far).astype(low)
+    each(PARTS, lambda c: sum_copy(2, FAR, c).start())
+    bufs[2, 0, PAIR] = down_part(pair).astype(low)
+    each(PARTS, lambda c: sum_copy(2, PAIR, c).start())
+
+    def back_norm(c):
+        grad = mine[1, piece(c), :] + arrived(1, PAIR, c) + arrived(1, ACROSS, c)
+        unit, inverse = norm_unit(residual[piece(c), :])
+        scaled = grad * gain_ref[...]
+        first_mean = jnp.mean(scaled, axis=-1, keepdims=True)
+        second_mean = jnp.mean(scaled * unit, axis=-1, keepdims=True)
+        total = inverse * (scaled - first_mean - unit * second_mean) + grad_own_ref[piece(c), :].astype(full)
+        grad_residual_ref[piece(c), :] = total
+        back_rows_ref[spot(mp, c), :] = total.astype(low)
+        row_copy(1, 0, c, mp, back_rows_ref).start()
+        row_copy(1, 1, c, mp, back_rows_ref).start()
+    each(PARTS, back_norm)
+
+    mine[1] = down_part(across)
+
+    def pass_output(c):
+        ship(2, ACROSS, c, mine[1, piece(c), :] + arrived(2, FAR, c))
+    each(PARTS, pass_output)
+    mine[0] = residual[...] + down_part(mp)
+
+    def merged_part(owner):
+        grad_merged_ref[spot(owner), :] = lax.dot_general(
+            back_rows_ref[spot(owner), :], w_out_ref[...], NT, preferred_element_type=full
+        ).astype(low)
+
+    merged_part(mp)
+    each(PARTS, lambda c: row_copy(1, 1, c, pair, back_rows_ref).wait_recv())
+    merged_part(pair)
+
+    def hand_on(c):
+        row_copy(1, 0, c, across, back_rows_ref).wait_recv()
+        row_copy(1, 2, c, across, back_rows_ref).start()
+    each(PARTS, hand_on)
+    merged_part(across)
+    each(PARTS, lambda c: row_copy(1, 2, c, far, back_rows_ref).wait_recv())
+    merged_part(far)
+    d_out_ref[...] = lax.dot_general(merged_ref[...], back_rows_ref[...], TN, preferred_element_type=full).astype(low)
+
+    def finish(c):
+        output_ref[piece(c), :] = (mine[0, piece(c), :] + arrived(2, PAIR, c) + arrived(2, ACROSS, c)).astype(low)
+    each(PARTS, finish)
+
+    def drain(c):
+        for which in range(3):
+            for kind in range(3):
+                sum_copy(which, kind, c).wait_send()
+        for which, ref in ((0, mlp_rows), (1, back_rows_ref)):
+            row_copy(which, 0, c, mp, ref).wait_send()
+            row_copy(which, 1, c, mp, ref).wait_send()
+            row_copy(which, 2, c, across, ref).wait_send()
+    each(PARTS, drain)
+    grad_copy(0, mp, grad_own_ref).wait_send()
+    grad_copy(1, across, grad_across_ref).wait_send()
+
+
+def middle(merged, w_out, tokens, gain, w_up, w_down, grad_own, grad_across):
+    total, cols = merged.shape
+    own, width = tokens.shape
+    hidden = w_up.shape[1]
+    low, full = jnp.bfloat16, jnp.float32
+    vmem = pl.BlockSpec(memory_space=pltpu.VMEM)
+    dma = pltpu.SemaphoreType.DMA
+    shape = jax.ShapeDtypeStruct
+    return pl.pallas_call(
+        middle_kernel,
+        out_shape=[
+            shape((total, width), low), shape((total, cols), low), shape((own, width), full), shape((own, width), low),
+            shape((width, hidden), low), shape((width, hidden), low), shape((cols, width), low),
+        ],
+        in_specs=[vmem] * 8,
+        out_specs=[vmem] * 7,
+        scratch_shapes=[
+            pltpu.VMEM((total, width), low), pltpu.VMEM((total, width), low),
+            pltpu.VMEM((total, hidden), low), pltpu.VMEM((total, hidden), low),
+            pltpu.VMEM((own, width), full), pltpu.VMEM((2, own, width), full),
+            pltpu.VMEM((3, 2, 3, own, width), low),
+            dma((3, 3, PARTS)), dma((3, 3, PARTS)), dma((2, 3, PARTS)), dma((2, 3, PARTS)), dma((2,)), dma((2,)), dma((2,)),
+        ],
+        compiler_params=pltpu.CompilerParams(collective_id=2, has_side_effects=True, vmem_limit_bytes=56 << 20),
+        cost_estimate=pl.CostEstimate(flops=16 * total * width * hidden, bytes_accessed=20 * total * width, transcendentals=0),
+        name="middle",
+    )(merged, w_out, tokens, gain, w_up, w_down, grad_own, grad_across)
+
+
 def local(
     tokens, segment_ids, gene_owner, w_qkv, w_attn_out, w_up, w_down, gain_attn, gain_mlp, cotangent
 ):
@@ -361,44 +585,17 @@
         tokens, gain_attn.reshape(1, -1), w_qkv, cotangent.reshape(dp_count, capacity, width)
     )
     returned = returned.reshape(dp_count * capacity, width)
+    grad_block = jnp.dot(onehot, returned, preferred_element_type=jnp.float32).astype(low)
+    grad_across = lax.ppermute(grad_block, "mp", [(i, i ^ 2) for i in range(lax.axis_size("mp"))])
     merged, log_sums = attend_forward(segment_ids, *projected)
-    residual = tokens_f + scatter_sum(jnp.dot(merged, w_attn_out, preferred_element_type=jnp.float32))
-    normed_two, unit_two, inverse_two = norm_parts(residual, gain_mlp)
-    mlp_rows = lax.all_gather(normed_two.astype(low), "mp", axis=0, tiled=True)
-    grad_block = jnp.dot(onehot, returned, preferred_element_type=jnp.float32).astype(low)
-    grad_rows = lax.all_gather(grad_block, "mp", axis=0, tiled=True)
-    pre_act = jnp.dot(mlp_rows, w_up, preferred_element_type=jnp.float32)
-    activated = gelu_exact(pre_act).astype(low)
-    grad_act = jnp.dot(grad_rows, w_down, preferred_element_type=jnp.float32)
-    grad_pre = (grad_act * gelu_slope(pre_act)).astype(low)
-    grad_mlp_in = scatter_sum(
-        lax.dot_general(grad_pre, w_up, contract_last, preferred_element_type=jnp.float32)
-    )
-    grad_down_local = lax.dot_general(
-        grad_rows, activated, contract_first, preferred_element_type=jnp.float32
-    ).astype(low)
-    grad_up_local = lax.dot_general(
-        mlp_rows, grad_pre, contract_first, preferred_element_type=jnp.float32
-    ).astype(low)
-    norm_two_grad, gain_mlp_grad = norm_back(grad_mlp_in, unit_two, inverse_two, gain_mlp)
+    residual_rows, grad_merged, grad_residual, output, grad_up_local, grad_down_local, grad_attn_local = middle(
+        merged, w_attn_out, tokens, gain_mlp.reshape(1, -1), w_up, w_down, grad_block, grad_across
+    )
     up_sum, down_sum = lax.psum((grad_up_local, grad_down_local), "dp")
-    output = residual + scatter_sum(
-        lax.dot_general(activated, w_down, contract_last, preferred_element_type=jnp.float32)
-    )
-    outgoing = lax.dot_general(
-        onehot, output.astype(low), contract_first, preferred_element_type=jnp.float32
-    ).astype(low)
+    outgoing = lax.dot_general(onehot, output, contract_first, preferred_element_type=jnp.float32).astype(low)
     relaid = lax.all_to_all(
         outgoing.reshape(dp_count, capacity, width), "dp", split_axis=0, concat_axis=0, tiled=True
     ).reshape(dp_count * capacity, width)
-    grad_residual = grad_block.astype(jnp.float32) + norm_two_grad
-    residual_rows = lax.all_gather(grad_residual.astype(low), "mp", axis=0, tiled=True)
-    grad_attn_local = lax.dot_general(
-        merged, residual_rows, contract_first, preferred_element_type=jnp.float32
-    ).astype(low)
-    grad_merged = lax.dot_general(
-        residual_rows, w_attn_out, contract_last, preferred_element_type=jnp.float32
-    ).astype(low)
     grad_proj = attend_backward(segment_ids, *projected, merged, grad_merged, log_sums)
     grad_attn_in = scatter_sum(
         sum(
@@ -416,7 +613,8 @@
     qkv_sum, attn_sum = lax.psum((grad_qkv_local, grad_attn_local), "dp")
     norm_one_grad, gain_attn_grad = norm_back(grad_attn_in, unit_one, inverse_one, gain_attn)
     grad_tokens = (grad_residual + norm_one_grad).astype(low)
-    gain_attn_sum, gain_mlp_sum = lax.psum((gain_attn_grad, gain_mlp_grad), ("dp", "mp"))
+    gain_mlp_grad = jnp.sum(w_up.astype(jnp.float32) * up_sum.astype(jnp.float32), axis=1) / gain_mlp
+    gain_attn_sum, gain_mlp_sum = lax.psum((gain_attn_grad, gain_mlp_grad / dp_count), ("dp", "mp"))
     full = jnp.float32
     return (
         relaid,

time: 603 us -> 428 us (0.71)
  waiting for transfers between devices: 347 us -> 134 us
  Pallas kernels: 94.1 us -> 194 us
  matrix products: 58.2 us -> 10.9 us
  other arithmetic: 25.7 us -> 13.4 us
    reduce_scatter x4 -> x1, waiting for transfers between devices: 143 us -> 0.01 us  [scatter_sum(): lax.psum_scatter(partial.astype(low), 'mp', scatter_dimension=0, tiled=True)]
    pallas_call x0 -> x1, Pallas kernels: none -> 96.5 us  [middle(): pl.pallas_call(middle_kernel, out_shape=[shape((total, width), low), shap...]
    all_gather x3 -> x0, waiting for transfers between devices: 59.3 us -> none  [the longest x1 25.4 us: local(): mlp_rows = lax.all_gather(normed_two.astype(low), 'mp', axis=0, tiled=True)]
    dot_general x10 -> x1, matrix products: 47.1 us -> 1.75 us  [local(): lax.dot_general(onehot, output, contract_first, preferred_element_type=jn...]
    unnamed x80 -> x56, local copies, waits for them, and re-layouts: 14.5 us -> 14.4 us
  transfers between devices with their start and end apart: 10 -> 5, of which waited for: 10 -> 3; matrix products, arithmetic and copies ran while one was open for 9% -> 4% of each run, Pallas kernels for 7% -> 16%
where the time goes in v3:
time: 428 us; the launch traced here: 427 us
  Pallas kernels  194 us (45%)
  waiting for transfers between devices  134 us (31%)
  blocking collectives  39.9 us (9%)
  between operations  15.8 us (4%)
  local copies, waits for them, and re-layouts  15 us (4%)
  other arithmetic  13.4 us (3%)
  matrix products  10.9 us (3%)
  starting transfers between devices  4.64 us (1%)
    pallas_call x1, Pallas kernels, middle(): pl.pallas_call(middle_kernel, out_shape=[shape((total, width), low), shap...  96.5 us
    psum x1, waiting for transfers between devices, local(): up_sum, down_sum = lax.psum((grad_up_local, grad_down_local), 'dp')  55.1 us
    psum x1, waiting for transfers between devices, local(): qkv_sum, attn_sum = lax.psum((grad_qkv_local, grad_attn_local), 'dp')  45.1 us
    pallas_call x1, Pallas kernels, attend_backward(): pl.pallas_call(functools.partial(bwd_kernel, n, heads), grid_spec=pltpu.P...  43.4 us
    psum x1, blocking collectives, local(): lax.psum((gain_attn_grad, gain_mlp_grad / dp_count), ('dp', 'mp'))  39.9 us
    all_to_all x1, waiting for transfers between devices, local(): lax.all_to_all(outgoing.reshape(dp_count, capacity, width), 'dp', split_a...  33.2 us
    pallas_call x1, Pallas kernels, project(): pl.pallas_call(functools.partial(project_kernel, dp_count), out_shape=[ja...  27.2 us
    pallas_call x1, Pallas kernels, attend_forward(): pl.pallas_call(functools.partial(fwd_kernel, n, heads), grid_spec=pltpu.P...  26.7 us
  transfers between devices with their start and end apart: 5, of which 3 were waited for; matrix products, arithmetic and copies ran while one was open for 4% of the time, Pallas kernels for 16%

profile of v3, /device:TPU:0, one launch (start us, length us, event | category | flops | bytes accessed | tf_op | source)
XLA Modules:
  0.0 427.0 jit_solution(5335002466475422633)
XLA Ops:
  8.1 1.6 copy.19.w_ref
  10.1 27.2 %project.1 = (bf16[2048,768]{1,0:T(8,128)(2,1)S(1)}, bf16[2048,192]{1,0:T(8,128)(2,1)S(1)}, bf16[2048,192]{1,0:T(8,128)(2,1)S(1)}, bf16[2048,192]{1,0:T(8,128)(2,1)S(1)}, bf16[8,80,768]{2,1,0:T(8,128)(2,1)S(1)}) custom-call(bf16[512,768]{1,0:T(8,128)(2,1)S(1)} %copy-done, f32[1,768]{1,0:T(1,128)S(1)} %reshape.62.gain_ref, ...), custom_call_target="tpu_custom_call" | custom-call | flops 1811939328 | bytes 15728640 | tf_op jit(solution)/shard_map/project/pallas_call | solution.py:325
  37.2 1.6 copy-done.4
  40.9 26.7 %attend_forward.1 = (bf16[2048,192]{1,0:T(8,128)(2,1)S(1)}, f32[8,2048]{1,0:T(8,128)S(1)}) custom-call(s32[2048]{0:T(1024)S(1)} %bitcast.35, s32[1,2048]{1,0:T(1,128)S(1)} %copy-done.3, bf16[2048,192]{1,0:T(8,128)(2,1)S(1)} %get-tuple-element.27.q_ref, bf16[2048,192]{1,0:T(8,128)(2,1)S(1)} %get-tuple-element.28.k_ref, ...), custom_call_target="tpu_custom_call" | custom-call | flops 3221225472 | bytes 3145728 | tf_op jit(solution)/shard_map/attend_forward/pallas_call | solution.py:128
  69.6 96.5 %middle.1 = (bf16[2048,768]{1,0:T(8,128)(2,1)}, bf16[2048,192]{1,0:T(8,128)(2,1)}, f32[512,768]{1,0:T(8,128)}, bf16[512,768]{1,0:T(8,128)(2,1)}, bf16[768,768]{1...) custom-call(bf16[2048,192]{1,0:T(8,128)(2,1)} %copy-done.12, bf16[192,768]{1,0:T(8,128)(2,1)} %w_out_ref.1, ...), custom_call_target="tpu_custom_call" | custom-call | flops 19327352832 | bytes 31457280 | tf_op jit(solution)/shard_map/middle/pallas_call | solution.py:541
  166.2 1.2 copy-done.7
  167.4 1.2 copy-done.9
  168.6 1.2 copy-done.11
  169.9 1.4 copy-done.13
  171.2 1.2 copy-done.14
  172.5 43.4 %attend_backward.1 = (bf16[2048,192]{1,0:T(8,128)(2,1)S(1)}, bf16[2048,192]{1,0:T(8,128)(2,1)S(1)}, bf16[2048,192]{1,0:T(8,128)(2,1)S(1)}) custom-call(s32[2048]{0:T(1024)S(1)} %bitcast.36, s32[1,2048]{1,0:T(1,128)S(1)} %copy-done.3, bf16[2048,192]{1,0:T(8,128)(2,1)S(1)} %copy-done.7, bf16[2048,192]{1,0:T(8,128)(2,1)S(1)} %copy-done.9, ...), custom_call_target="tpu_custom_call" | custom-call | flops 8053063680 | bytes 6291456 | tf_op jit(solution)/shard_map/attend_backward/pallas_call | solution.py:208
  219.5 55.1 %all-reduce.8.cloned.1.call-done = (bf16[768,768]{1,0:T(8,128)(2,1)}, bf16[768,768]{1,0:T(8,128)(2,1)}) async-done(((bf16[768,768]{1,0:T(8,128)(2,1)}, bf16[768,768]{1,0:T(8,128)(2,1)}), (bf16[768,768]{1,0:T(8,128)(2,1)}, bf16[768,768]{1,0:T(8,128)(2,1)})) %all-reduce.8.cloned.1.call-update) | async-done | bytes 2359312 | tf_op jit(solution)/shard_map/psum | solution.py:594
  274.7 2.0 fusion.20
  277.7 2.7 add_convert_fusion
  281.6 1.8 convolution_convert_fusion
  283.3 3.9 all-to-all-start
  287.8 33.2 %all-to-all-done = bf16[8,80,768]{2,1,0:T(8,128)(2,1)S(1)} async-done(((bf16[8,80,768]{2,1,0:T(8,128)(2,1)}), bf16[8,80,768]{2,1,0:T(8,128)(2,1)S(1)}, u32[]{:S(2)}, u32[]{:S(2)}) %all-to-all-start) | async-done | bytes 983072 | tf_op jit(solution)/shard_map/all_to_all | solution.py:596
  321.1 1.6 convert_element_type.60
  323.5 1.7 multiply_reduce_fusion
  325.2 45.1 %all-reduce.6.cloned.1.call-done = (bf16[3,768,192]{1,2,0:T(8,128)(2,1)}, bf16[192,768]{1,0:T(8,128)(2,1)}) async-done(((bf16[3,768,192]{1,2,0:T(8,128)(2,1)}, bf16[192,768]{1,0:T(8,128)(2,1)}), (bf16[3,768,192]{1,2,0:T(8,128)(2,1)}, bf16[192,768]{1,0:T(8,128)(2,1)})) %all-reduce.6.cloned.1.call-update) | async-done | bytes 1179664 | tf_op jit(solution)/shard_map/psum | solution.py:613
  370.3 2.6 convert_element_type.57
  373.8 2.0 fusion.12
  375.8 39.9 %all-reduce = (f32[768]{0:T(1024)}, f32[768]{0:T(1024)}) all-reduce(f32[768]{0:T(1024)S(1)} %get-tuple-element.46, f32[768]{0:T(1024)S(1)} %divide_multiply_fusion), channel_id=1, replica_groups=mesh['dp'=8,'mp'=4] {'dp','mp'}, use_global_device_ids=true, to_apply=%region_11.0 | all-reduce | flops 1536 | bytes 12288 | tf_op jit(solution)/shard_map/psum | solution.py:617
  415.7 2.9 fusion.9
  (75 shorter events, 13.3 us)
Async XLA Ops:
  8.0 1.7 copy-start.21
  8.0 1.8 copy-start.22
  8.0 2.0 copy-start.2
  8.0 2.0 copy-start
  8.0 266.6 %all-reduce.8.cloned.1.call-start = ((), (), s32[]{:S(2)}) async-start(), calls=%async_computation.4 | async-start | bytes 4718592 | tf_op jit(solution)/shard_map/psum | solution.py:594
  37.2 1.6 copy-start.4
  38.9 28.8 %copy-start.6 = (bf16[2048,192]{1,0:T(8,128)(2,1)}, bf16[2048,192]{1,0:T(8,128)(2,1)S(1)}, u32[]{:S(2)}) copy-start(bf16[2048,192]{1,0:T(8,128)(2,1)S(1)} %get-tuple-element.27.q_ref) | copy-start | bytes 2359300
  38.9 28.8 %copy-start.8 = (bf16[2048,192]{1,0:T(8,128)(2,1)}, bf16[2048,192]{1,0:T(8,128)(2,1)S(1)}, u32[]{:S(2)}) copy-start(bf16[2048,192]{1,0:T(8,128)(2,1)S(1)} %get-tuple-element.28.k_ref) | copy-start | bytes 2359300
  38.9 28.8 %copy-start.10 = (bf16[2048,192]{1,0:T(8,128)(2,1)}, bf16[2048,192]{1,0:T(8,128)(2,1)S(1)}, u32[]{:S(2)}) copy-start(bf16[2048,192]{1,0:T(8,128)(2,1)S(1)} %get-tuple-element.29.v_ref) | copy-start | bytes 2359300
  38.9 1.5 copy-start.23
  38.9 2.0 copy-start.3
  39.7 28.0 %copy-start.24 = (bf16[512,768]{1,0:T(8,128)(2,1)}, bf16[512,768]{1,0:T(8,128)(2,1)S(1)}, u32[]{:S(2)}) copy-start(bf16[512,768]{1,0:T(8,128)(2,1)S(1)} %convolution_convert_fusion.1.grad_own_ref) | copy-start | bytes 2359300
  39.7 28.9 %collective-permute-start = (bf16[512,768]{1,0:T(8,128)(2,1)S(1)}, bf16[512,768]{1,0:T(8,128)(2,1)S(1)}, u32[]{:S(2)}, u32[]{:S(2)}) collective-permute-start(bf16[512,768]{1,0:T(8,128)(2,1)S(1)} %convolution_convert_fusion.1.grad_own_ref), channel_id=1, source_target_pairs={{0,2},{1,3},{2,0},{3,1},{4,6},{5,7},{6,4},{7,5},{8,10},{9,11},{10,... | collective-permute-start | bytes 2359304 | tf_op jit(solution)/shard_map/ppermute | solution.py:589
  166.1 204.2 %all-reduce.6.cloned.1.call-start = ((), (), s32[]{:S(2)}) async-start(), calls=%async_computation.3 | async-start | bytes 2359296 | tf_op jit(solution)/shard_map/psum | solution.py:613
  172.5 43.4 %copy-start.5 = (bf16[2048,768]{1,0:T(8,128)(2,1)S(1)}, bf16[2048,768]{1,0:T(8,128)(2,1)}, u32[]{:S(2)}) copy-start(bf16[2048,768]{1,0:T(8,128)(2,1)} %copy-done.4) | copy-start | bytes 9437188
  274.7 99.1 %reduce-scatter.2.cloned.1.call-start = ((), (), s32[]{:S(2)}) async-start(), calls=%async_computation.2 | async-start | bytes 3932160 | tf_op jit(solution)/shard_map/reduce_scatter | solution.py:574
  274.7 2.0 copy-start.15
  283.3 3.9 copy-start.1
  283.3 37.7 %copy-start.17 = (bf16[768,768]{1,0:T(8,128)(2,1)S(1)}, bf16[768,768]{1,0:T(8,128)(2,1)}, u32[]{:S(2)}) copy-start(bf16[768,768]{1,0:T(8,128)(2,1)} %get-tuple-element.45) | copy-start | bytes 3538948
  283.3 37.7 %all-to-all-start = ((bf16[8,80,768]{2,1,0:T(8,128)(2,1)}), bf16[8,80,768]{2,1,0:T(8,128)(2,1)S(1)}, u32[]{:S(2)}, u32[]{:S(2)}) async-start(bf16[8,80,768]{2,1,0:T(8,128)(2,1)} %bitcast.39), calls=%async_computation | async-start | bytes 1966080 | tf_op jit(solution)/shard_map/all_to_all | solution.py:596
  321.0 1.7 copy-start.18
  321.0 2.5 copy-start.19
  370.3 2.6 copy-start.20
  373.8 41.9 %copy-start.16 = (bf16[512,768]{1,0:T(8,128)(2,1)S(1)}, bf16[512,768]{1,0:T(8,128)(2,1)}, u32[]{:S(2)}) copy-start(bf16[512,768]{1,0:T(8,128)(2,1)} %reduce-scatter.2.cloned.1.call-done) | copy-start | bytes 2359300
  (8 other events, 9.3 us)
Sparse Core Ops, SparseCore 0:
  166.3 108.3 all-reduce.7
  278.7 91.5 all-reduce.5
Sparse Core Ops, SparseCore 1:
  280.5 36.9 reduce-scatter.1

commit v4 on v3

--- a/solution.py
+++ b/solution.py
@@ -6,36 +6,6 @@
 from jax.experimental.pallas import tpu as pltpu
 from jax.sharding import PartitionSpec as P
 
-epsilon = 1e-05
-
-
-def norm_parts(values, gain_vec):
-    average = jnp.mean(values, axis=-1, keepdims=True)
-    centered = values - average
-    variance = jnp.mean(centered * centered, axis=-1, keepdims=True)
-    inverse = lax.rsqrt(variance + epsilon)
-    unit_rows = centered * inverse
-    return (unit_rows * gain_vec, unit_rows, inverse)
-
-
-def norm_back(grad_normed, unit_rows, inverse, gain_vec):
-    scaled = grad_normed * gain_vec
-    first_mean = jnp.mean(scaled, axis=-1, keepdims=True)
-    second_mean = jnp.mean(scaled * unit_rows, axis=-1, keepdims=True)
-    grad_input = inverse * (scaled - first_mean - unit_rows * second_mean)
-    return (grad_input, jnp.sum(grad_normed * unit_rows, axis=0))
-
-
-def gelu_exact(values):
-    return 0.5 * values * (1.0 + lax.erf(values * 0.7071067811865476))
-
-
-def gelu_slope(values):
-    cumulative = 0.5 * (1.0 + lax.erf(values * 0.7071067811865476))
-    density = jnp.exp(-0.5 * values * values) * 0.3989422804014327
-    return cumulative + values * density
-
-
 HEAD = 64
 TQ = 256
 TK = 256
@@ -43,6 +13,7 @@
 NN = (((1,), (0,)), ((), ()))
 TN = (((0,), (0,)), ((), ()))
 MASKED = -1e30
+epsilon = 1e-05
 
 
 def lower_bound(seg, n, value):
@@ -223,6 +194,8 @@
 
 MESH_ID = pl.DeviceIdType.MESH
 PARTS = 4
+MLP_CHUNKS = 3
+QKV_CHUNKS = 3
 
 
 def remote(src, dst, send, recv, device):
@@ -244,6 +217,77 @@
     variance = jnp.mean(centered * centered, axis=-1, keepdims=True)
     inverse = lax.rsqrt(variance + epsilon)
     return centered * inverse, inverse
+
+
+def sum_stages(rows, chunks, dp_count):
+    stages = dp_count.bit_length() - 1
+    return stages if dp_count == 1 << stages and rows % (16 * chunks * dp_count) == 0 else 0
+
+
+def sum_scratch(rows, width, chunks, stages):
+    dma = pltpu.SemaphoreType.DMA
+    return [
+        pltpu.VMEM((rows, width), jnp.bfloat16), pltpu.VMEM((rows, width), jnp.bfloat16),
+        dma((chunks, max(1, 2 * stages))), dma((chunks, max(1, 2 * stages))),
+    ]
+
+
+def sum_steps(stages, chunks, acc, came, send, recv, out):
+    dp, mp = lax.axis_index("dp"), lax.axis_index("mp")
+    chunk = acc.shape[0] // chunks
+
+    def bit(s):
+        return lax.rem(dp // (1 << s), 2)
+
+    def held(k, s):
+        start = k * chunk
+        for j in range(s):
+            start = start + bit(j) * (chunk >> (j + 1))
+        return start
+
+    def span(start, size):
+        return pl.ds(pl.multiple_of(start, 16), size)
+
+    def halve(k, s):
+        size = chunk >> (s + 1)
+        return remote(
+            acc.at[span(held(k, s) + (1 - bit(s)) * size, size)],
+            came.at[span(k * chunk + chunk - (chunk >> s), size)],
+            send.at[k, s], recv.at[k, s], (dp ^ (1 << s), mp),
+        )
+
+    def double(k, s, mine=True):
+        size = chunk >> (s + 1)
+        rows = out.at[span(held(k, s + 1) if mine else held(k, s) + (1 - bit(s)) * size, size)]
+        return remote(rows, rows, send.at[k, stages + s], recv.at[k, stages + s], (dp ^ (1 << s), mp))
+
+    def step(k, i):
+        if i == 0:
+            halve(k, 0).start()
+        elif i <= stages:
+            halve(k, i - 1).wait_recv()
+            size = chunk >> i
+            rows = span(held(k, i), size)
+            total = acc[rows, :].astype(jnp.float32) + came[span(k * chunk + chunk - (chunk >> (i - 1)), size), :].astype(jnp.float32)
+            if i < stages:
+                acc[rows, :] = total.astype(jnp.bfloat16)
+                halve(k, i).start()
+            else:
+                out[rows, :] = total.astype(jnp.bfloat16)
+                double(k, stages - 1).start()
+        else:
+            s = 2 * stages - i
+            double(k, s, False).wait_recv()
+            if s > 0:
+                double(k, s - 1).start()
+
+    def drain():
+        for k in range(chunks):
+            for s in range(stages):
+                halve(k, s).wait_send()
+                double(k, s).wait_send()
+
+    return step, drain
 
 
 def project_kernel(
@@ -282,7 +326,7 @@
         where = spot(owner, half, own // 2)
         rows = rows_ref[where, :]
         for p, out in enumerate((q_ref, k_ref, v_ref)):
-            out[where, :] = jnp.dot(rows, w_ref[p], preferred_element_type=jnp.float32).astype(jnp.bfloat16)
+            out[where, :] = lax.dot_general(rows, w_ref[p], NT, preferred_element_type=jnp.float32).astype(jnp.bfloat16)
 
     def both(owner):
         def step(half, _):
@@ -318,7 +362,7 @@
     own, width = tokens.shape
     dp_count = cot.shape[0]
     total = own * 4
-    cols = w_qkv.shape[2]
+    cols = w_qkv.shape[1]
     vmem = pl.BlockSpec(memory_space=pltpu.VMEM)
     hbm = pl.BlockSpec(memory_space=pl.ANY)
     dma = pltpu.SemaphoreType.DMA
@@ -343,10 +387,10 @@
 
 
 def middle_kernel(
-    merged_ref, w_out_ref, tokens_ref, gain_ref, w_up_ref, w_down_ref, grad_own_ref, grad_across_ref,
-    back_rows_ref, grad_merged_ref, grad_residual_ref, output_ref, d_up_ref, d_down_ref, d_out_ref,
+    stages, merged_ref, w_out_ref, tokens_ref, gain_ref, w_up_ref, w_down_ref, grad_own_ref, grad_across_ref,
+    back_rows_ref, grad_merged_ref, grad_residual_ref, output_ref, d_mlp_ref, d_out_ref,
     mlp_rows, grad_rows, active, grad_pre, residual, mine, bufs,
-    sum_send, sum_recv, row_send, row_recv, grad_send, grad_recv, self_sem,
+    sum_send, sum_recv, row_send, row_recv, grad_send, grad_recv, self_sem, acc, came, dp_send, dp_recv,
 ):
     low, full = jnp.bfloat16, jnp.float32
     dp, mp = lax.axis_index("dp"), lax.axis_index("mp")
@@ -354,7 +398,8 @@
     own, width = tokens_ref.shape
     part = own // PARTS
     to_pair, to_across = (dp, pair), (dp, across)
-    greet([to_pair, to_across])
+    greet([to_pair, to_across] + [(dp ^ (1 << j), mp) for j in range(stages)])
+    add_step, add_drain = sum_steps(stages, MLP_CHUNKS, acc, came, dp_send, dp_recv, d_mlp_ref)
 
     def spot(owner, c=None):
         if c is None:
@@ -461,11 +506,22 @@
         ship(1, ACROSS, c, got[part:] + arrived(1, FAR, c))
     each(PARTS, distant)
 
-    def weight_block(b):
-        cols = pl.ds(pl.multiple_of(b * 256, 256), 256)
-        d_down_ref[cols, :] = lax.dot_general(grad_rows[:, cols], active[...], TN, preferred_element_type=full).astype(low)
-        d_up_ref[cols, :] = lax.dot_general(mlp_rows[:, cols], grad_pre[...], TN, preferred_element_type=full).astype(low)
-    each(width // 256, weight_block)
+    for b in range(MLP_CHUNKS):
+        cols = slice(b * 256, (b + 1) * 256)
+        target = acc if stages else d_mlp_ref
+        target[b * 512:b * 512 + 256, :] = lax.dot_general(
+            mlp_rows[:, cols], grad_pre[...], TN, preferred_element_type=full
+        ).astype(low)
+        target[b * 512 + 256:b * 512 + 512, :] = lax.dot_general(
+            grad_rows[:, cols], active[...], TN, preferred_element_type=full
+        ).astype(low)
+        if stages:
+            add_step(b, 0)
+
+    def add(*steps):
+        if stages:
+            for k, i in steps:
+                add_step(k, i)
 
     def down_part(owner):
         return lax.dot_general(active[spot(owner), :], w_down_ref[...], NT, preferred_element_type=full)
@@ -486,13 +542,16 @@
         back_rows_ref[spot(mp, c), :] = total.astype(low)
         row_copy(1, 0, c, mp, back_rows_ref).start()
         row_copy(1, 1, c, mp, back_rows_ref).start()
-    each(PARTS, back_norm)
+    each(2, back_norm)
+    add((0, 1))
+    each(2, lambda c: back_norm(c + 2))
 
     mine[1] = down_part(across)
 
     def pass_output(c):
         ship(2, ACROSS, c, mine[1, piece(c), :] + arrived(2, FAR, c))
     each(PARTS, pass_output)
+    add((0, 2), (1, 1))
     mine[0] = residual[...] + down_part(mp)
 
     def merged_part(owner):
@@ -507,15 +566,26 @@
     def hand_on(c):
         row_copy(1, 0, c, across, back_rows_ref).wait_recv()
         row_copy(1, 2, c, across, back_rows_ref).start()
-    each(PARTS, hand_on)
+    each(2, hand_on)
+    add((0, 3), (1, 2))
+    each(1, lambda c: hand_on(c + 2))
+    add((2, 1))
+    each(1, lambda c: hand_on(c + 3))
+    add((0, 4), (1, 3), (2, 2))
     merged_part(across)
     each(PARTS, lambda c: row_copy(1, 2, c, far, back_rows_ref).wait_recv())
     merged_part(far)
     d_out_ref[...] = lax.dot_general(merged_ref[...], back_rows_ref[...], TN, preferred_element_type=full).astype(low)
+    add((0, 5), (1, 4), (2, 3))
 
     def finish(c):
         output_ref[piece(c), :] = (mine[0, piece(c), :] + arrived(2, PAIR, c) + arrived(2, ACROSS, c)).astype(low)
-    each(PARTS, finish)
+    each(2, finish)
+    add((1, 5), (2, 4))
+    each(2, lambda c: finish(c + 2))
+    add((2, 5), (0, 6), (1, 6), (2, 6))
+    if stages:
+        add_drain()
 
     def drain(c):
         for which in range(3):
@@ -530,7 +600,8 @@
     grad_copy(1, across, grad_across_ref).wait_send()
 
 
-def middle(merged, w_out, tokens, gain, w_up, w_down, grad_own, grad_across):
+def middle(dp_count, merged, w_out, tokens, gain, w_up, w_down, grad_own, grad_across):
+    stages = sum_stages(2 * w_up.shape[0], MLP_CHUNKS, dp_count)
     total, cols = merged.shape
     own, width = tokens.shape
     hidden = w_up.shape[1]
@@ -539,24 +610,163 @@
     dma = pltpu.SemaphoreType.DMA
     shape = jax.ShapeDtypeStruct
     return pl.pallas_call(
-        middle_kernel,
+        functools.partial(middle_kernel, stages),
         out_shape=[
             shape((total, width), low), shape((total, cols), low), shape((own, width), full), shape((own, width), low),
-            shape((width, hidden), low), shape((width, hidden), low), shape((cols, width), low),
+            shape((2 * width, hidden), low), shape((cols, width), low),
         ],
         in_specs=[vmem] * 8,
-        out_specs=[vmem] * 7,
+        out_specs=[vmem] * 6,
         scratch_shapes=[
             pltpu.VMEM((total, width), low), pltpu.VMEM((total, width), low),
             pltpu.VMEM((total, hidden), low), pltpu.VMEM((total, hidden), low),
             pltpu.VMEM((own, width), full), pltpu.VMEM((2, own, width), full),
             pltpu.VMEM((3, 2, 3, own, width), low),
             dma((3, 3, PARTS)), dma((3, 3, PARTS)), dma((2, 3, PARTS)), dma((2, 3, PARTS)), dma((2,)), dma((2,)), dma((2,)),
-        ],
+        ]
+        + sum_scratch(2 * width, hidden, MLP_CHUNKS, stages),
         compiler_params=pltpu.CompilerParams(collective_id=2, has_side_effects=True, vmem_limit_bytes=56 << 20),
         cost_estimate=pl.CostEstimate(flops=16 * total * width * hidden, bytes_accessed=20 * total * width, transcendentals=0),
         name="middle",
     )(merged, w_out, tokens, gain, w_up, w_down, grad_own, grad_across)
+
+
+def last_kernel(
+    stages, dq_ref, dk_ref, dv_ref, w_ref, rows_ref, grad_residual_ref, tokens_ref, gain_ref, d_out_ref, gain_part_ref,
+    grad_tokens_ref, d_sum_ref, gains_ref,
+    mine, bufs, gain_all, sum_send, sum_recv, gain_send, gain_recv, acc, came, dp_send, dp_recv,
+):
+    low, full = jnp.bfloat16, jnp.float32
+    dp, mp = lax.axis_index("dp"), lax.axis_index("mp")
+    pair, across, far = mp ^ 1, mp ^ 2, mp ^ 3
+    own, width = tokens_ref.shape
+    part = own // PARTS
+    cols = dq_ref.shape[1]
+    to_pair, to_across = (dp, pair), (dp, across)
+    greet([to_pair, to_across, (dp, far)] + [(dp ^ (1 << j), mp) for j in range(stages)])
+    add_step, add_drain = sum_steps(stages, QKV_CHUNKS, acc, came, dp_send, dp_recv, d_sum_ref)
+    target = acc if stages else d_sum_ref
+    chunk = target.shape[0] // QKV_CHUNKS
+    FAR, ACROSS, PAIR = 0, 1, 2
+
+    def add(*steps):
+        if stages:
+            for k, i in steps:
+                add_step(k, i)
+
+    def piece(c):
+        return pl.ds(pl.multiple_of(c * part, part), part)
+
+    def each(count, body):
+        def step(i, _):
+            body(i)
+            return 0
+        lax.fori_loop(0, count, step, 0)
+
+    def sum_copy(kind, c):
+        src, dst = bufs.at[0, kind, piece(c)], bufs.at[1, kind, piece(c)]
+        return remote(src, dst, sum_send.at[kind, c], sum_recv.at[kind, c], to_across if kind == ACROSS else to_pair)
+
+    def arrived(kind, c):
+        sum_copy(kind, c).wait_recv()
+        return bufs[1, kind, piece(c), :].astype(full)
+
+    target[0:cols, :] = d_out_ref[...]
+    started = 0
+    for p, ref in enumerate((dq_ref, dk_ref, dv_ref)):
+        target[(p + 1) * cols:(p + 2) * cols, :] = lax.dot_general(
+            ref[...], rows_ref[...], TN, preferred_element_type=full
+        ).astype(low)
+        while started < QKV_CHUNKS and (started + 1) * chunk <= (p + 2) * cols:
+            add((started, 0))
+            started += 1
+
+    def in_part(owner):
+        where = pl.ds(pl.multiple_of(owner * own, own), own)
+        total = jnp.dot(dq_ref[where, :], w_ref[0], preferred_element_type=full)
+        total = total + jnp.dot(dk_ref[where, :], w_ref[1], preferred_element_type=full)
+        return total + jnp.dot(dv_ref[where, :], w_ref[2], preferred_element_type=full)
+
+    bufs[0, FAR] = in_part(far).astype(low)
+    each(PARTS, lambda c: sum_copy(FAR, c).start())
+    mine[...] = in_part(across)
+
+    def pass_across(c):
+        bufs[0, ACROSS, piece(c), :] = (mine[piece(c), :] + arrived(FAR, c)).astype(low)
+        sum_copy(ACROSS, c).start()
+    each(PARTS, pass_across)
+    bufs[0, PAIR] = in_part(pair).astype(low)
+    each(PARTS, lambda c: sum_copy(PAIR, c).start())
+    mine[...] = in_part(mp)
+    add((0, 1))
+
+    def back_norm(c):
+        grad = mine[piece(c), :] + arrived(PAIR, c) + arrived(ACROSS, c)
+        unit, inverse = norm_unit(tokens_ref[piece(c), :].astype(full))
+        scaled = grad * gain_ref[...]
+        first_mean = jnp.mean(scaled, axis=-1, keepdims=True)
+        second_mean = jnp.mean(scaled * unit, axis=-1, keepdims=True)
+        total = inverse * (scaled - first_mean - unit * second_mean) + grad_residual_ref[piece(c), :]
+        grad_tokens_ref[piece(c), :] = total.astype(low)
+
+    each(1, back_norm)
+    add((0, 2), (1, 1))
+    each(1, lambda c: back_norm(c + 1))
+    add((0, 3), (1, 2), (2, 1))
+    each(1, lambda c: back_norm(c + 2))
+    add((0, 4), (1, 3), (2, 2))
+    each(1, lambda c: back_norm(c + 3))
+    add((0, 5), (1, 4), (2, 3), (1, 5), (2, 4), (2, 5), (0, 6), (1, 6), (2, 6))
+    if stages:
+        add_drain()
+
+    total = jnp.zeros((1, width), full)
+    for p in range(3):
+        prod = w_ref[p].astype(full) * d_sum_ref[(p + 1) * cols:(p + 2) * cols, :].astype(full)
+        total = total + jnp.sum(prod, axis=0, keepdims=True)
+    row = lax.broadcasted_iota(jnp.int32, (8, width), 0)
+    gain_all[mp] = jnp.where(row == 0, gain_part_ref[...], jnp.where(row == 1, total / gain_ref[...], 0.0))
+
+    def gain_copy(i, owner, other):
+        return remote(gain_all.at[owner], gain_all.at[owner], gain_send.at[i], gain_recv.at[i], (dp, other))
+
+    others = (pair, across, far)
+    for i, other in enumerate(others):
+        gain_copy(i, mp, other).start()
+    for i, other in enumerate(others):
+        gain_copy(i, other, other).wait_recv()
+    gains_ref[...] = (gain_all[0] + gain_all[1]) + (gain_all[2] + gain_all[3])
+    for i, other in enumerate(others):
+        gain_copy(i, mp, other).wait_send()
+
+    def drain(c):
+        for kind in range(3):
+            sum_copy(kind, c).wait_send()
+    each(PARTS, drain)
+
+
+def last(dp_count, dq, dk, dv, w_qkv, rows, grad_residual, tokens, gain, d_out, gain_part):
+    own, width = tokens.shape
+    cols = dq.shape[1]
+    stages = sum_stages(4 * cols, QKV_CHUNKS, dp_count)
+    low, full = jnp.bfloat16, jnp.float32
+    vmem = pl.BlockSpec(memory_space=pltpu.VMEM)
+    dma = pltpu.SemaphoreType.DMA
+    shape = jax.ShapeDtypeStruct
+    return pl.pallas_call(
+        functools.partial(last_kernel, stages),
+        out_shape=[shape((own, width), low), shape((4 * cols, width), low), shape((8, width), full)],
+        in_specs=[vmem] * 10,
+        out_specs=[vmem] * 3,
+        scratch_shapes=[
+            pltpu.VMEM((own, width), full), pltpu.VMEM((2, 3, own, width), low), pltpu.VMEM((4, 8, width), full),
+            dma((3, PARTS)), dma((3, PARTS)), dma((3,)), dma((3,)),
+        ]
+        + sum_scratch(4 * cols, width, QKV_CHUNKS, stages),
+        compiler_params=pltpu.CompilerParams(collective_id=3, has_side_effects=True, vmem_limit_bytes=48 << 20),
+        cost_estimate=pl.CostEstimate(flops=12 * 4 * own * width * cols, bytes_accessed=20 * own * width, transcendentals=0),
+        name="last",
+    )(dq, dk, dv, w_qkv, rows, grad_residual, tokens, gain, d_out, gain_part)
 
 
 def local(
@@ -566,12 +776,8 @@
     dp_count = lax.axis_size("dp")
     capacity = cotangent.shape[0] // dp_count
     own_rows = tokens.shape[0]
-    contract_last = (((1,), (1,)), ((), ()))
     contract_first = (((0,), (0,)), ((), ()))
     low = jnp.bfloat16
-
-    def scatter_sum(partial):
-        return lax.psum_scatter(partial.astype(low), "mp", scatter_dimension=0, tiled=True).astype(jnp.float32)
 
     owners = gene_owner[:, 0]
     place = jnp.arange(own_rows, dtype=jnp.int32)
@@ -579,52 +785,44 @@
     slots = owners * capacity + jnp.sum(earlier.astype(jnp.int32), axis=1)
     onehot = (slots[:, None] == jnp.arange(dp_count * capacity, dtype=jnp.int32)[None, :]).astype(low)
 
-    tokens_f = tokens.astype(jnp.float32)
-    normed_one, unit_one, inverse_one = norm_parts(tokens_f, gain_attn)
-    attn_in, *projected, returned = project(
-        tokens, gain_attn.reshape(1, -1), w_qkv, cotangent.reshape(dp_count, capacity, width)
-    )
+    w_rows = jnp.swapaxes(w_qkv, 1, 2)
+    gain_one = gain_attn.reshape(1, -1)
+    attn_in, *projected, returned = project(tokens, gain_one, w_rows, cotangent.reshape(dp_count, capacity, width))
     returned = returned.reshape(dp_count * capacity, width)
     grad_block = jnp.dot(onehot, returned, preferred_element_type=jnp.float32).astype(low)
     grad_across = lax.ppermute(grad_block, "mp", [(i, i ^ 2) for i in range(lax.axis_size("mp"))])
     merged, log_sums = attend_forward(segment_ids, *projected)
-    residual_rows, grad_merged, grad_residual, output, grad_up_local, grad_down_local, grad_attn_local = middle(
-        merged, w_attn_out, tokens, gain_mlp.reshape(1, -1), w_up, w_down, grad_block, grad_across
+    residual_rows, grad_merged, grad_residual, output, mlp_sum, d_out = middle(
+        dp_count, merged, w_attn_out, tokens, gain_mlp.reshape(1, -1), w_up, w_down, grad_block, grad_across
     )
-    up_sum, down_sum = lax.psum((grad_up_local, grad_down_local), "dp")
+    if not sum_stages(2 * width, MLP_CHUNKS, dp_count):
+        mlp_sum = lax.psum(mlp_sum, "dp")
+    mlp_sum = mlp_sum.reshape(MLP_CHUNKS, 2, width // MLP_CHUNKS, w_up.shape[1]).astype(jnp.float32)
+    up_sum, down_sum = (mlp_sum[:, i].reshape(w_up.shape) for i in range(2))
+    gain_part = (jnp.sum(w_up.astype(jnp.float32) * up_sum, axis=1) / gain_mlp).reshape(1, -1)
     outgoing = lax.dot_general(onehot, output, contract_first, preferred_element_type=jnp.float32).astype(low)
     relaid = lax.all_to_all(
         outgoing.reshape(dp_count, capacity, width), "dp", split_axis=0, concat_axis=0, tiled=True
     ).reshape(dp_count * capacity, width)
     grad_proj = attend_backward(segment_ids, *projected, merged, grad_merged, log_sums)
-    grad_attn_in = scatter_sum(
-        sum(
-            lax.dot_general(grad_proj[p], w_qkv[p], contract_last, preferred_element_type=jnp.float32)
-            for p in range(3)
-        )
+    grad_tokens, weight_sum, gains = last(
+        dp_count, *grad_proj, w_rows, attn_in, grad_residual, tokens, gain_one, d_out, gain_part
     )
-    grad_qkv_local = jnp.stack(
-        [
-            lax.dot_general(attn_in, grad_proj[p], contract_first, preferred_element_type=jnp.float32).astype(low)
-            for p in range(3)
-        ]
-    )
-    grad_qkv_local, up_sum, down_sum = lax.optimization_barrier((grad_qkv_local, up_sum, down_sum))
-    qkv_sum, attn_sum = lax.psum((grad_qkv_local, grad_attn_local), "dp")
-    norm_one_grad, gain_attn_grad = norm_back(grad_attn_in, unit_one, inverse_one, gain_attn)
-    grad_tokens = (grad_residual + norm_one_grad).astype(low)
-    gain_mlp_grad = jnp.sum(w_up.astype(jnp.float32) * up_sum.astype(jnp.float32), axis=1) / gain_mlp
-    gain_attn_sum, gain_mlp_sum = lax.psum((gain_attn_grad, gain_mlp_grad / dp_count), ("dp", "mp"))
-    full = jnp.float32
+    cols = w_qkv.shape[2]
+    if not sum_stages(4 * cols, QKV_CHUNKS, dp_count):
+        weight_sum = lax.psum(weight_sum, "dp")
+        products = w_rows.astype(jnp.float32) * weight_sum[cols:].reshape(w_rows.shape).astype(jnp.float32)
+        gains = gains.at[1].set(lax.psum(jnp.sum(products, axis=(0, 1)) / gain_attn, "mp"))
+    weight_sum = weight_sum.astype(jnp.float32)
     return (
         relaid,
         grad_tokens,
-        qkv_sum.astype(full),
-        attn_sum.astype(full),
-        up_sum.astype(full),
-        down_sum.astype(full),
-        gain_attn_sum,
-        gain_mlp_sum,
+        jnp.swapaxes(weight_sum[cols:].reshape(3, cols, width), 1, 2),
+        weight_sum[:cols],
+        up_sum,
+        down_sum,
+        gains[1],
+        gains[0],
     )
 
 

time: 428 us -> 307 us (0.72)
  waiting for transfers between devices: 134 us -> 0.01 us
  Pallas kernels: 194 us -> 274 us
  blocking collectives: 39.9 us -> 0 us
  between operations: 15.8 us -> 0.81 us
  other arithmetic: 13.4 us -> 2 us
  matrix products: 10.9 us -> 3.71 us
  local copies, waits for them, and re-layouts: 15 us -> 21 us
    psum x2 -> x0, waiting for transfers between devices: 100 us -> none  [the longest x1 55.1 us: local(): up_sum, down_sum = lax.psum((grad_up_local, grad_down_local), 'dp')]
    pallas_call x1 -> x2, Pallas kernels: 96.5 us -> 189 us  [the longest x1 130 us: middle(): pl.pallas_call(functools.partial(middle_kernel, stages), out_shape=[shape...]
    psum x1 -> x0, blocking collectives: 39.9 us -> none  [local(): lax.psum((gain_attn_grad, gain_mlp_grad / dp_count), ('dp', 'mp'))]
    all_to_all x1, waiting for transfers between devices: 33.2 us -> 0.01 us  [local(): lax.all_to_all(outgoing.reshape(dp_count, capacity, width), 'dp', split_a...]
    dot_general x6 -> x0, matrix products: 8.29 us -> none  [the longest x3 5.7 us: local(): lax.dot_general(grad_proj[p], w_qkv[p], contract_last, preferred_element_...]
    pallas_call x1, Pallas kernels: 43.4 us -> 35.5 us  [attend_backward(): pl.pallas_call(functools.partial(bwd_kernel, n, heads), grid_spec=pltpu.P...]
    convert_element_type x4 -> x0, other arithmetic: 7.88 us -> none  [the longest x1 2.88 us: local(): grad_tokens = (grad_residual + norm_one_grad).astype(low)]
    slice x0 -> x4, local copies, waits for them, and re-layouts: none -> 7.29 us  [the longest x1 3.44 us: local(): up_sum, down_sum = (mlp_sum[:, i].reshape(w_up.shape) for i in range(2))]
  transfers between devices with their start and end apart: 5 -> 2, of which waited for: 3 -> 0; matrix products, arithmetic and copies ran while one was open for 4% -> 3% of each run, Pallas kernels for 16% -> 38%
where the time goes in v4:
time: 307 us
  Pallas kernels  274 us (89%)
  local copies, waits for them, and re-layouts  21 us (7%)
  starting transfers between devices  5.8 us (2%)
  matrix products  3.71 us (1%)
    pallas_call x1, Pallas kernels, middle(): pl.pallas_call(functools.partial(middle_kernel, stages), out_shape=[shape...  130 us
    pallas_call x1, Pallas kernels, last(): pl.pallas_call(functools.partial(last_kernel, stages), out_shape=[shape((...  59.4 us
    pallas_call x1, Pallas kernels, attend_backward(): pl.pallas_call(functools.partial(bwd_kernel, n, heads), grid_spec=pltpu.P...  35.5 us
    pallas_call x1, Pallas kernels, project(): pl.pallas_call(functools.partial(project_kernel, dp_count), out_shape=[ja...  27.2 us
    pallas_call x1, Pallas kernels, attend_forward(): pl.pallas_call(functools.partial(fwd_kernel, n, heads), grid_spec=pltpu.P...  22.1 us
    unnamed x40, local copies, waits for them, and re-layouts  12.5 us
  transfers between devices with their start and end apart: 2, of which 0 were waited for; matrix products, arithmetic and copies ran while one was open for 3% of the time, Pallas kernels for 38%

profile of v4, /device:TPU:0, one launch (start us, length us, event | category | flops | bytes accessed | tf_op | source)
XLA Modules:
  0.0 307.1 jit_solution(14173648747397071108)
XLA Ops:
  0.6 1.0 convert_reduce_fusion
  1.6 0.7 multiply_add_fusion
  2.3 0.7 reshape.50.gain_ref
  3.0 1.2 copy-done
  4.2 1.2 copy-done.1
  5.4 1.1 copy-done.3
  6.5 27.2 %project.1 = (bf16[2048,768]{1,0:T(8,128)(2,1)S(1)}, bf16[2048,192]{1,0:T(8,128)(2,1)S(1)}, bf16[2048,192]{1,0:T(8,128)(2,1)S(1)}, bf16[2048,192]{1,0:T(8,128)(2,1)S(1)}, bf16[8,80,768]{2,1,0:T(8,128)(2,1)S(1)}) custom-call(bf16[512,768]{1,0:T(8,128)(2,1)S(1)} %copy-done.3, f32[1,768]{1,0:T(1,128)S(1)} %reshape.50.gain_ref, ...), custom_call_target="tpu_custom_call" | custom-call | flops 1811939328 | bytes 15728640 | tf_op jit(solution)/shard_map/project/pallas_call | solution.py:369
  33.7 1.6 copy-done.6
  35.3 0.8 convolution_convert_fusion.1.grad_own_ref
  37.4 22.1 %attend_forward.1 = (bf16[2048,192]{1,0:T(8,128)(2,1)S(1)}, f32[8,2048]{1,0:T(8,128)S(1)}) custom-call(s32[2048]{0:T(1024)S(1)} %bitcast.22, s32[1,2048]{1,0:T(1,128)S(1)} %copy-done.5, bf16[2048,192]{1,0:T(8,128)(2,1)S(1)} %get-tuple-element.26.q_ref, bf16[2048,192]{1,0:T(8,128)(2,1)S(1)} %get-tuple-element.27.k_ref, ...), custom_call_target="tpu_custom_call" | custom-call | flops 3221225472 | bytes 3145728 | tf_op jit(solution)/shard_map/attend_forward/pallas_call | solution.py:99
  59.5 1.0 copy-done.10
  60.5 0.9 copy-done.18
  61.4 129.6 %middle.1 = (bf16[2048,768]{1,0:T(8,128)(2,1)}, bf16[2048,192]{1,0:T(8,128)(2,1)}, f32[512,768]{1,0:T(8,128)}, bf16[512,768]{1,0:T(8,128)(2,1)}, bf16[1536,768]{1,0:T(8,128)(2,1)}, /*index=5*/bf16[192,768]{1,0:T(8,128)(2,1)}) custom-call(bf16[2048,192]{1,0:T(8,128)(2,1)} %copy-done.10, bf16[192,768]{1,0:T(8,128)(2,1)} %w_out_ref.1, ...), custom_call_target="tpu_custom_call" | custom-call | flops 19327352832 | bytes 31457280 | tf_op jit(solution)/shard_map/middle/pallas_call | solution.py:612
  191.0 2.9 convolution_convert_fusion
  193.9 5.2 %all-to-all-start = ((bf16[8,80,768]{2,1,0:T(8,128)(2,1)}), bf16[8,80,768]{2,1,0:T(8,128)(2,1)}, u32[]{:S(2)}, u32[]{:S(2)}) async-start(bf16[8,80,768]{2,1,0:T(8,128)(2,1)} %bitcast.7), calls=%async_computation | async-start | bytes 1966080 | tf_op jit(solution)/shard_map/all_to_all | solution.py:804
  199.1 3.4 %fusion.3 = (f32[3,1,256,768]{3,2,1,0:T(8,128)}, f32[3,1,256,768]{3,2,1,0:T(8,128)S(1)}) fusion(bf16[3,2,256,768]{3,2,1,0:T(8,128)(2,1)} %bitcast.25), kind=kLoop, calls=%fused_computation.12 | loop fusion | bytes 9437184 | tf_op jit(solution)/shard_map/slice | solution.py:801
  202.9 1.1 copy-done.13
  205.3 35.5 %attend_backward.1 = (bf16[2048,192]{1,0:T(8,128)(2,1)S(1)}, bf16[2048,192]{1,0:T(8,128)(2,1)S(1)}, bf16[2048,192]{1,0:T(8,128)(2,1)S(1)}) custom-call(s32[2048]{0:T(1024)S(1)} %bitcast.23, s32[1,2048]{1,0:T(1,128)S(1)} %copy-done.5, bf16[2048,192]{1,0:T(8,128)(2,1)S(1)} %get-tuple-element.26.q_ref, bf16[2048,192]{1,0:T(8,128)(2,1)S(1)} %get-tuple-element.27.k_ref, ...), custom_call_target="tpu_custom_call" | custom-call | flops 8053063680 | bytes 6291456 | tf_op jit(solution)/shard_map/attend_backward/pallas_call | solution.py:179
  240.8 59.4 %last.1 = (bf16[512,768]{1,0:T(8,128)(2,1)S(1)}, bf16[768,768]{1,0:T(8,128)(2,1)}, f32[8,768]{1,0:T(8,128)S(1)}) custom-call(bf16[2048,192]{1,0:T(8,128)(2,1)S(1)} %get-tuple-element.34.dq_ref, bf16[2048,192]{1,0:T(8,128)(2,1)S(1)} %get-tuple-element.35.dk_ref, bf16[2048,192]{1,0:T(8,128)(2,1)S(1)} %get-tuple-element.36.dv_ref, ...), custom_call_target="tpu_custom_call" | custom-call | flops 3623878656 | bytes 7864320 | tf_op jit(solution)/shard_map/last/pallas_call | solution.py:756
  300.2 1.9 slice.26
  302.1 1.3 slice.25
  303.4 0.6 slice_reduce_fusion
  304.0 2.2 copy.20
  306.3 0.9 copy.21
  (38 shorter events, 2.8 us)
Async XLA Ops:
  3.0 1.2 copy-start
  4.2 1.2 copy-start.1
  5.4 1.1 copy-start.3
  33.7 1.7 copy-start.6
  35.3 24.2 %copy-start.7 = (bf16[2048,192]{1,0:T(8,128)(2,1)}, bf16[2048,192]{1,0:T(8,128)(2,1)S(1)}, u32[]{:S(2)}) copy-start(bf16[2048,192]{1,0:T(8,128)(2,1)S(1)} %get-tuple-element.28.v_ref) | copy-start | bytes 2359300
  35.3 1.4 copy-start.16
  35.3 2.0 copy-start.5
  36.2 23.4 %copy-start.17 = (bf16[512,768]{1,0:T(8,128)(2,1)}, bf16[512,768]{1,0:T(8,128)(2,1)S(1)}, u32[]{:S(2)}) copy-start(bf16[512,768]{1,0:T(8,128)(2,1)S(1)} %convolution_convert_fusion.1.grad_own_ref) | copy-start | bytes 2359300
  36.2 24.3 %collective-permute-start = (bf16[512,768]{1,0:T(8,128)(2,1)S(1)}, bf16[512,768]{1,0:T(8,128)(2,1)S(1)}, u32[]{:S(2)}, u32[]{:S(2)}) collective-permute-start(bf16[512,768]{1,0:T(8,128)(2,1)S(1)} %convolution_convert_fusion.1.grad_own_ref), channel_id=1, source_target_pairs={{0,2},{1,3},{2,0},{3,1},{4,6},{5,7},{6,4},{7,5},{8,10},{9,11},{10,... | collective-permute-start | bytes 2359304 | tf_op jit(solution)/shard_map/ppermute | solution.py:793
  59.5 1.0 copy-start.10
  60.5 0.9 copy-start.18
  193.9 110.1 %all-to-all-start = ((bf16[8,80,768]{2,1,0:T(8,128)(2,1)}), bf16[8,80,768]{2,1,0:T(8,128)(2,1)}, u32[]{:S(2)}, u32[]{:S(2)}) async-start(bf16[8,80,768]{2,1,0:T(8,128)(2,1)} %bitcast.7), calls=%async_computation | async-start | bytes 1966080 | tf_op jit(solution)/shard_map/all_to_all | solution.py:804
  199.1 3.5 %copy-start.15 = (bf16[768,768]{1,0:T(8,128)(2,1)S(1)}, bf16[768,768]{1,0:T(8,128)(2,1)}, u32[]{:S(2)}) copy-start(bf16[768,768]{1,0:T(8,128)(2,1)} %w_up_ref.1) | copy-start | bytes 3538948
  202.6 1.4 copy-start.13
  202.6 2.0 copy-start.8
  202.6 2.4 copy-start.11
  202.6 2.7 copy-start.12
  205.3 35.5 %copy-start.2 = (bf16[3,768,192]{1,2,0:T(8,128)(2,1)S(1)}, bf16[3,768,192]{1,2,0:T(8,128)(2,1)}, u32[]{:S(2)}) copy-start(bf16[3,768,192]{1,2,0:T(8,128)(2,1)} %param.13) | copy-start | bytes 2654212
  205.3 35.5 %copy-start.4 = (bf16[512,768]{1,0:T(8,128)(2,1)S(1)}, bf16[512,768]{1,0:T(8,128)(2,1)}, u32[]{:S(2)}) copy-start(bf16[512,768]{1,0:T(8,128)(2,1)} %tokens_ref.5) | copy-start | bytes 2359300
  205.3 35.5 %copy-start.9 = (bf16[192,768]{1,0:T(8,128)(2,1)S(1)}, bf16[192,768]{1,0:T(8,128)(2,1)}, u32[]{:S(2)}) copy-start(bf16[192,768]{1,0:T(8,128)(2,1)} %get-tuple-element.39.d_out_ref) | copy-start | bytes 884740
  300.2 1.9 copy-start.14

commit v5 on v4

--- a/solution.py
+++ b/solution.py
@@ -8,7 +8,7 @@
 
 HEAD = 64
 TQ = 256
-TK = 256
+TK = 512
 NT = (((1,), (1,)), ((), ()))
 NN = (((1,), (0,)), ((), ()))
 TN = (((0,), (0,)), ((), ()))
@@ -106,7 +106,7 @@
             scratch_shapes=[pltpu.VMEM((width, n), jnp.bfloat16), pltpu.VMEM((n, 128), jnp.float32), pltpu.VMEM((heads, n, TQ), jnp.float32)],
         ),
         out_shape=[jax.ShapeDtypeStruct((n, width), jnp.bfloat16), jax.ShapeDtypeStruct((8, n), jnp.float32)],
-        compiler_params=pltpu.CompilerParams(vmem_limit_bytes=40 << 20),
+        compiler_params=pltpu.CompilerParams(vmem_limit_bytes=VMEM_BYTES),
         cost_estimate=pl.CostEstimate(flops=4 * heads * n * n * HEAD, bytes_accessed=8 * n * width, transcendentals=heads * n * n // 2),
         name="attend_forward",
     )(seg.reshape(-1), seg.reshape(1, -1), q, k, v)
@@ -186,7 +186,7 @@
             scratch_shapes=[pltpu.VMEM((width, n), jnp.bfloat16), pltpu.VMEM((n, 128), jnp.float32), pltpu.VMEM((n, width), jnp.float32), pltpu.VMEM((n, width), jnp.float32)],
         ),
         out_shape=[jax.ShapeDtypeStruct((n, width), jnp.bfloat16)] * 3,
-        compiler_params=pltpu.CompilerParams(vmem_limit_bytes=40 << 20),
+        compiler_params=pltpu.CompilerParams(vmem_limit_bytes=VMEM_BYTES),
         cost_estimate=pl.CostEstimate(flops=10 * heads * n * n * HEAD, bytes_accessed=16 * n * width, transcendentals=heads * n * n // 2),
         name="attend_backward",
     )(seg.reshape(-1), seg.reshape(1, -1), q, k, v, o, do, lse)
@@ -194,8 +194,10 @@
 
 MESH_ID = pl.DeviceIdType.MESH
 PARTS = 4
-MLP_CHUNKS = 3
-QKV_CHUNKS = 3
+VMEM_BYTES = 60 << 20
+MLP_CHUNKS = 6
+QKV_CHUNKS = 6
+NORM_TICKS = (5, 7, 9, 10)
 
 
 def remote(src, dst, send, recv, device):
@@ -232,7 +234,11 @@
     ]
 
 
-def sum_steps(stages, chunks, acc, came, send, recv, out):
+def left_bit(k, chunks):
+    return 0 if 2 * k < chunks else 1
+
+
+def sum_steps(stages, chunks, acc, came, send, recv, out, half=False):
     dp, mp = lax.axis_index("dp"), lax.axis_index("mp")
     chunk = acc.shape[0] // chunks
 
@@ -247,6 +253,11 @@
 
     def span(start, size):
         return pl.ds(pl.multiple_of(start, 16), size)
+
+    def placed(k, start):
+        if not half:
+            return start
+        return k * (chunk // 2) + bit(1 - left_bit(k, chunks)) * (chunk // 4) + start - held(k, 2)
 
     def halve(k, s):
         size = chunk >> (s + 1)
@@ -257,9 +268,17 @@
         )
 
     def double(k, s, mine=True):
+        if half and s == 1:
+            s = 1 - left_bit(k, chunks)
+            place = bit(s) if mine else 1 - bit(s)
+            rows = out.at[span(k * (chunk // 2) + place * (chunk // 4), chunk // 4)]
+            return remote(rows, rows, send.at[k, stages + 1], recv.at[k, stages + 1], (dp ^ (1 << s), mp))
         size = chunk >> (s + 1)
-        rows = out.at[span(held(k, s + 1) if mine else held(k, s) + (1 - bit(s)) * size, size)]
+        start = held(k, s + 1) if mine else held(k, s) + (1 - bit(s)) * size
+        rows = out.at[span(placed(k, start), size)]
         return remote(rows, rows, send.at[k, stages + s], recv.at[k, stages + s], (dp ^ (1 << s), mp))
+
+    final = 1 if half else 0
 
     def step(k, i):
         if i == 0:
@@ -273,27 +292,38 @@
                 acc[rows, :] = total.astype(jnp.bfloat16)
                 halve(k, i).start()
             else:
-                out[rows, :] = total.astype(jnp.bfloat16)
+                out[span(placed(k, held(k, i)), size), :] = total.astype(jnp.bfloat16)
                 double(k, stages - 1).start()
-        else:
+        elif 2 * stages - i >= final:
             s = 2 * stages - i
             double(k, s, False).wait_recv()
-            if s > 0:
+            if s > final:
                 double(k, s - 1).start()
 
     def drain():
         for k in range(chunks):
             for s in range(stages):
                 halve(k, s).wait_send()
-                double(k, s).wait_send()
+                if s >= final:
+                    double(k, s).wait_send()
 
     return step, drain
 
 
+def columns_of(row):
+    return jnp.concatenate(
+        [jnp.broadcast_to(row[:, t * 128:(t + 1) * 128], (128, 128)).T for t in range(row.shape[1] // 128)], axis=0
+    )
+
+
 def project_kernel(
-    dp_count, tokens_ref, gain_ref, w_ref, cot_ref, rows_ref, q_ref, k_ref, v_ref, returned_ref,
-    across_send, across_recv, pair_send, pair_recv, pass_send, pass_recv, slot_send, slot_recv, self_sem,
+    dp_count, tokens_hbm, gain_ref, w_hbm, cot_ref, owner_ref, rows_hbm, q_ref, k_ref, v_ref, grad_ref, place_ref,
+    tokens_ref, w_ref, rows_ref, load_sem, store_sem, returned_ref, across_send, across_recv, pair_send, pair_recv, pass_send, pass_recv, slot_send, slot_recv, self_sem,
 ):
+    load_tokens = pltpu.make_async_copy(tokens_hbm, tokens_ref, load_sem.at[0])
+    load_w = pltpu.make_async_copy(w_hbm, w_ref, load_sem.at[1])
+    load_tokens.start()
+    load_w.start()
     dp, mp = lax.axis_index("dp"), lax.axis_index("mp")
     pair, across, far = mp ^ 1, mp ^ 2, mp ^ 3
     own = tokens_ref.shape[0]
@@ -311,10 +341,15 @@
         other = lax.rem(dp + k, dp_count)
         return remote(cot_ref.at[other], returned_ref.at[dp], slot_send.at[k], slot_recv.at[k], (other, mp))
 
+    def store(i, owner):
+        rows = pl.ds(pl.multiple_of(owner * own, own), own)
+        return pltpu.make_async_copy(rows_ref.at[rows], rows_hbm.at[rows], store_sem.at[i])
+
+    load_tokens.wait()
     for c in range(PARTS):
         values = tokens_ref[c * part:(c + 1) * part, :].astype(jnp.float32)
         unit, _ = norm_unit(values)
-        rows_ref[spot(mp, c, part), :] = (unit * gain_ref[...]).astype(jnp.bfloat16)
+        rows_ref[spot(mp, c, part), :] = (unit * gain_ref[0:1, :]).astype(jnp.bfloat16)
         gather_copy(c, mp, (dp, across), across_send, across_recv).start()
         gather_copy(c, mp, (dp, pair), pair_send, pair_recv).start()
     for k in range(1, dp_count):
@@ -334,19 +369,35 @@
             return 0
         lax.fori_loop(0, 2, step, 0)
 
+    load_w.wait()
     both(mp)
+    store(0, mp).start()
+    capacity = cot_ref.shape[1]
+    owner_row = owner_ref[...].astype(jnp.float32)
+    owner_col = columns_of(owner_row)
+    earlier = lax.broadcasted_iota(jnp.int32, (own, own), 0) < lax.broadcasted_iota(jnp.int32, (own, own), 1)
+    same = jnp.concatenate([owner_col] * (own // 128), axis=1) == owner_row
+    rank_row = jnp.sum(jnp.where(same & earlier, 1.0, 0.0), axis=0, keepdims=True)
+    slot_row = owner_row * capacity + rank_row
+    slots = place_ref.shape[0]
+    place_ref[...] = jnp.where(
+        lax.broadcasted_iota(jnp.int32, (slots, own), 0).astype(jnp.float32) == slot_row, 1.0, 0.0
+    ).astype(jnp.bfloat16)
     for c in range(PARTS):
         gather_copy(c, pair, (dp, pair), pair_send, pair_recv).wait_recv()
     both(pair)
+    store(1, pair).start()
     for half in range(2):
         for c in range(half * PARTS // 2, (half + 1) * PARTS // 2):
             gather_copy(c, across, (dp, across), across_send, across_recv).wait_recv()
             gather_copy(c, across, (dp, pair), pass_send, pass_recv).start()
         product(across, half)
+    store(2, across).start()
     for half in range(2):
         for c in range(half * PARTS // 2, (half + 1) * PARTS // 2):
             gather_copy(c, far, (dp, pair), pass_send, pass_recv).wait_recv()
         product(far, half)
+    store(3, far).start()
     for c in range(PARTS):
         gather_copy(c, mp, (dp, across), across_send, across_recv).wait_send()
         gather_copy(c, mp, (dp, pair), pair_send, pair_recv).wait_send()
@@ -356,28 +407,45 @@
         slot_copy(k).wait_send()
         other = lax.rem(dp + dp_count - k, dp_count)
         remote(cot_ref.at[dp], returned_ref.at[other], slot_send.at[k], slot_recv.at[k], (other, mp)).wait_recv()
-
-
-def project(tokens, gain, w_qkv, cot):
+    for i, owner in enumerate((mp, pair, across, far)):
+        store(i, owner).wait()
+    if capacity % 16 == 0:
+        back = returned_ref[...].reshape(slots, cot_ref.shape[2])
+        grad_ref[...] = lax.dot_general(place_ref[...], back, TN, preferred_element_type=jnp.float32).astype(jnp.bfloat16)
+    else:
+        rank_col = columns_of(rank_row)[:, :capacity]
+        lane = lax.broadcasted_iota(jnp.int32, (own, capacity), 1).astype(jnp.float32)
+
+        def take(d, total):
+            pick = (owner_col[:, :capacity] == d.astype(jnp.float32)) & (rank_col == lane)
+            pick = jnp.where(pick, 1.0, 0.0).astype(jnp.bfloat16)
+            return total + jnp.dot(pick, returned_ref[d], preferred_element_type=jnp.float32)
+        grad_ref[...] = lax.fori_loop(0, dp_count, take, jnp.zeros(grad_ref.shape, jnp.float32)).astype(jnp.bfloat16)
+
+
+def project(tokens, gain, w_qkv, cot, owners):
     own, width = tokens.shape
     dp_count = cot.shape[0]
     total = own * 4
     cols = w_qkv.shape[1]
     vmem = pl.BlockSpec(memory_space=pltpu.VMEM)
-    hbm = pl.BlockSpec(memory_space=pl.ANY)
+    hbm = pl.BlockSpec(memory_space=pltpu.HBM)
     dma = pltpu.SemaphoreType.DMA
     return pl.pallas_call(
         functools.partial(project_kernel, dp_count),
         out_shape=[jax.ShapeDtypeStruct((total, width), jnp.bfloat16)]
         + [jax.ShapeDtypeStruct((total, cols), jnp.bfloat16)] * 3
-        + [jax.ShapeDtypeStruct(cot.shape, cot.dtype)],
-        in_specs=[vmem, vmem, vmem, hbm],
-        out_specs=[vmem] * 4 + [hbm],
-        scratch_shapes=[dma((PARTS,))] * 6 + [dma((dp_count,))] * 2 + [dma],
-        compiler_params=pltpu.CompilerParams(collective_id=1, has_side_effects=True, vmem_limit_bytes=40 << 20),
+        + [jax.ShapeDtypeStruct((own, width), jnp.bfloat16), jax.ShapeDtypeStruct((dp_count * cot.shape[1], own), jnp.bfloat16)],
+        in_specs=[hbm, vmem, hbm, hbm, vmem],
+        out_specs=[hbm] + [vmem] * 5,
+        scratch_shapes=[
+            pltpu.VMEM(tokens.shape, tokens.dtype), pltpu.VMEM(w_qkv.shape, w_qkv.dtype),
+            pltpu.VMEM((total, width), jnp.bfloat16), dma((2,)), dma((4,)), pltpu.VMEM(cot.shape, cot.dtype),
+        ] + [dma((PARTS,))] * 6 + [dma((dp_count,))] * 2 + [dma],
+        compiler_params=pltpu.CompilerParams(collective_id=1, has_side_effects=True, vmem_limit_bytes=VMEM_BYTES),
         cost_estimate=pl.CostEstimate(flops=6 * total * width * cols, bytes_accessed=10 * total * width, transcendentals=0),
         name="project",
-    )(tokens, gain, w_qkv, cot)
+    )(tokens, gain, w_qkv, cot, owners)
 
 
 def gelu_and_slope(values):
@@ -387,11 +455,30 @@
 
 
 def middle_kernel(
-    stages, merged_ref, w_out_ref, tokens_ref, gain_ref, w_up_ref, w_down_ref, grad_own_ref, grad_across_ref,
-    back_rows_ref, grad_merged_ref, grad_residual_ref, output_ref, d_mlp_ref, d_out_ref,
+    stages, merged_hbm, w_out_hbm, tokens_hbm, gain_ref, w_up_hbm, w_down_hbm, grad_own_hbm, grad_across_hbm, place_hbm,
+    back_rows_hbm, grad_merged_hbm, grad_residual_hbm, outgoing_hbm, first_hbm, second_hbm, gain_part_ref, d_out_ref,
+    merged_ref, w_out_ref, tokens_ref, w_up_ref, w_down_ref, grad_own_ref, grad_across_ref, place_ref,
+    back_rows_ref, grad_merged_ref, grad_residual_ref, outgoing_ref, d_mlp_ref, load_sem, store_sem,
     mlp_rows, grad_rows, active, grad_pre, residual, mine, bufs,
     sum_send, sum_recv, row_send, row_recv, grad_send, grad_recv, self_sem, acc, came, dp_send, dp_recv,
 ):
+    first_rows = first_hbm.shape[0]
+    loads = [
+        pltpu.make_async_copy(src, dst, load_sem.at[i])
+        for i, (src, dst) in enumerate((
+            (merged_hbm, merged_ref), (w_out_hbm, w_out_ref), (tokens_hbm, tokens_ref), (grad_own_hbm, grad_own_ref),
+            (grad_across_hbm, grad_across_ref), (w_up_hbm, w_up_ref), (w_down_hbm, w_down_ref), (place_hbm, place_ref),
+        ))
+    ]
+    for load in loads:
+        load.start()
+    stores = [
+        pltpu.make_async_copy(src, dst, store_sem.at[i])
+        for i, (src, dst) in enumerate((
+            (back_rows_ref, back_rows_hbm), (grad_merged_ref, grad_merged_hbm), (grad_residual_ref, grad_residual_hbm),
+            (outgoing_ref, outgoing_hbm), (d_mlp_ref.at[0:first_rows], first_hbm), (d_mlp_ref.at[first_rows:], second_hbm),
+        ))
+    ]
     low, full = jnp.bfloat16, jnp.float32
     dp, mp = lax.axis_index("dp"), lax.axis_index("mp")
     pair, across, far = mp ^ 1, mp ^ 2, mp ^ 3
@@ -399,7 +486,8 @@
     part = own // PARTS
     to_pair, to_across = (dp, pair), (dp, across)
     greet([to_pair, to_across] + [(dp ^ (1 << j), mp) for j in range(stages)])
-    add_step, add_drain = sum_steps(stages, MLP_CHUNKS, acc, came, dp_send, dp_recv, d_mlp_ref)
+    add_step, add_drain = sum_steps(stages, MLP_CHUNKS, acc, came, dp_send, dp_recv, d_mlp_ref, half=True)
+    target = acc if stages else d_mlp_ref
 
     def spot(owner, c=None):
         if c is None:
@@ -444,6 +532,8 @@
     def out_part(owner):
         return jnp.dot(merged_ref[spot(owner), :], w_out_ref[...], preferred_element_type=full)
 
+    loads[0].wait()
+    loads[1].wait()
     bufs[0, 0, FAR] = out_part(far).astype(low)
     each(PARTS, lambda c: sum_copy(0, FAR, c).start())
     mine[0] = out_part(across)
@@ -453,6 +543,8 @@
     each(PARTS, pass_across)
     bufs[0, 0, PAIR] = out_part(pair).astype(low)
     each(PARTS, lambda c: sum_copy(0, PAIR, c).start())
+    for load in loads[2:5]:
+        load.wait()
     for copy in local_copies:
         copy.start()
     grad_copy(0, mp, grad_own_ref).start()
@@ -463,6 +555,8 @@
     grad_copy(0, pair, grad_own_ref).wait_recv()
     grad_copy(1, far, grad_across_ref).wait_recv()
 
+    for load in loads[5:8]:
+        load.wait()
     blocks = w_up_ref.shape[1] // 256
     both = 2 * part
 
@@ -488,7 +582,7 @@
         values = mine[0, piece(c), :] + arrived(0, PAIR, c) + arrived(0, ACROSS, c)
         residual[piece(c), :] = values
         unit, _ = norm_unit(values)
-        mlp_rows[spot(mp, c), :] = (unit * gain_ref[...]).astype(low)
+        mlp_rows[spot(mp, c), :] = (unit * gain_ref[1:2, :]).astype(low)
         row_copy(0, 0, c, mp, mlp_rows).start()
         row_copy(0, 1, c, mp, mlp_rows).start()
         row_copy(0, 1, c, pair, mlp_rows).wait_recv()
@@ -506,17 +600,20 @@
         ship(1, ACROSS, c, got[part:] + arrived(1, FAR, c))
     each(PARTS, distant)
 
-    for b in range(MLP_CHUNKS):
+    size = width // MLP_CHUNKS
+    for b in range(3):
         cols = slice(b * 256, (b + 1) * 256)
-        target = acc if stages else d_mlp_ref
-        target[b * 512:b * 512 + 256, :] = lax.dot_general(
-            mlp_rows[:, cols], grad_pre[...], TN, preferred_element_type=full
-        ).astype(low)
-        target[b * 512 + 256:b * 512 + 512, :] = lax.dot_general(
-            grad_rows[:, cols], active[...], TN, preferred_element_type=full
-        ).astype(low)
-        if stages:
-            add_step(b, 0)
+        up = lax.dot_general(mlp_rows[:, cols], grad_pre[...], TN, preferred_element_type=full)
+        gain_col = jnp.sum(up * w_up_ref[cols, :].astype(full), axis=1, keepdims=True)
+        gain_part_ref[:, cols] = jnp.broadcast_to(gain_col, (256, 128)).T[0:8] / gain_ref[1:2, cols]
+        up = up.astype(low)
+        down = lax.dot_general(grad_rows[:, cols], active[...], TN, preferred_element_type=full).astype(low)
+        for j in range(256 // size):
+            k = b * (256 // size) + j
+            target[2 * k * size:(2 * k + 1) * size, :] = up[j * size:(j + 1) * size]
+            target[(2 * k + 1) * size:(2 * k + 2) * size, :] = down[j * size:(j + 1) * size]
+            if stages:
+                add_step(k, 0)
 
     def add(*steps):
         if stages:
@@ -534,7 +631,7 @@
     def back_norm(c):
         grad = mine[1, piece(c), :] + arrived(1, PAIR, c) + arrived(1, ACROSS, c)
         unit, inverse = norm_unit(residual[piece(c), :])
-        scaled = grad * gain_ref[...]
+        scaled = grad * gain_ref[1:2, :]
         first_mean = jnp.mean(scaled, axis=-1, keepdims=True)
         second_mean = jnp.mean(scaled * unit, axis=-1, keepdims=True)
         total = inverse * (scaled - first_mean - unit * second_mean) + grad_own_ref[piece(c), :].astype(full)
@@ -542,16 +639,21 @@
         back_rows_ref[spot(mp, c), :] = total.astype(low)
         row_copy(1, 0, c, mp, back_rows_ref).start()
         row_copy(1, 1, c, mp, back_rows_ref).start()
+    def tick(t):
+        add(*[(t - i, i) for i in range(2 * stages, 0, -1) if 0 <= t - i < MLP_CHUNKS])
+
     each(2, back_norm)
-    add((0, 1))
-    each(2, lambda c: back_norm(c + 2))
+    tick(1)
+    each(1, lambda c: back_norm(c + 2))
+    tick(2)
+    each(1, lambda c: back_norm(c + 3))
 
     mine[1] = down_part(across)
 
     def pass_output(c):
         ship(2, ACROSS, c, mine[1, piece(c), :] + arrived(2, FAR, c))
     each(PARTS, pass_output)
-    add((0, 2), (1, 1))
+    tick(3)
     mine[0] = residual[...] + down_part(mp)
 
     def merged_part(owner):
@@ -566,26 +668,30 @@
     def hand_on(c):
         row_copy(1, 0, c, across, back_rows_ref).wait_recv()
         row_copy(1, 2, c, across, back_rows_ref).start()
-    each(2, hand_on)
-    add((0, 3), (1, 2))
-    each(1, lambda c: hand_on(c + 2))
-    add((2, 1))
-    each(1, lambda c: hand_on(c + 3))
-    add((0, 4), (1, 3), (2, 2))
+    for c in range(PARTS):
+        each(1, lambda i: hand_on(i + c))
+        tick(4 + c)
     merged_part(across)
     each(PARTS, lambda c: row_copy(1, 2, c, far, back_rows_ref).wait_recv())
     merged_part(far)
+    stores[0].start()
+    stores[1].start()
+    stores[2].start()
     d_out_ref[...] = lax.dot_general(merged_ref[...], back_rows_ref[...], TN, preferred_element_type=full).astype(low)
-    add((0, 5), (1, 4), (2, 3))
 
     def finish(c):
-        output_ref[piece(c), :] = (mine[0, piece(c), :] + arrived(2, PAIR, c) + arrived(2, ACROSS, c)).astype(low)
-    each(2, finish)
-    add((1, 5), (2, 4))
-    each(2, lambda c: finish(c + 2))
-    add((2, 5), (0, 6), (1, 6), (2, 6))
+        mine[0, piece(c), :] = mine[0, piece(c), :] + arrived(2, PAIR, c) + arrived(2, ACROSS, c)
+    for c in range(PARTS):
+        each(1, lambda i: finish(i + c))
+        tick(8 + c)
+    stores[4].start()
+    stores[5].start()
+    outgoing_ref[...] = jnp.dot(place_ref[...], mine[0].astype(low), preferred_element_type=full).astype(low)
+    stores[3].start()
     if stages:
         add_drain()
+    for store in stores:
+        store.wait()
 
     def drain(c):
         for which in range(3):
@@ -600,42 +706,55 @@
     grad_copy(1, across, grad_across_ref).wait_send()
 
 
-def middle(dp_count, merged, w_out, tokens, gain, w_up, w_down, grad_own, grad_across):
+def middle(dp_count, merged, w_out, tokens, gain, w_up, w_down, grad_own, grad_across, place):
     stages = sum_stages(2 * w_up.shape[0], MLP_CHUNKS, dp_count)
+    d_rows = w_up.shape[0] * (1 if stages else 2)
     total, cols = merged.shape
     own, width = tokens.shape
     hidden = w_up.shape[1]
+    slots = place.shape[0]
     low, full = jnp.bfloat16, jnp.float32
     vmem = pl.BlockSpec(memory_space=pltpu.VMEM)
+    hbm = pl.BlockSpec(memory_space=pl.ANY)
     dma = pltpu.SemaphoreType.DMA
-    shape = jax.ShapeDtypeStruct
+    shape, room = jax.ShapeDtypeStruct, pltpu.VMEM
     return pl.pallas_call(
         functools.partial(middle_kernel, stages),
         out_shape=[
-            shape((total, width), low), shape((total, cols), low), shape((own, width), full), shape((own, width), low),
-            shape((2 * width, hidden), low), shape((cols, width), low),
+            shape((total, width), low), shape((total, cols), low), shape((own, width), full), shape((slots, width), low),
+            shape((d_rows // 2, hidden), low), shape((d_rows // 2, hidden), low), shape((8, width), full), shape((cols, width), low),
         ],
-        in_specs=[vmem] * 8,
-        out_specs=[vmem] * 6,
+        in_specs=[hbm] * 3 + [vmem] + [hbm] * 5,
+        out_specs=[hbm] * 6 + [vmem] * 2,
         scratch_shapes=[
-            pltpu.VMEM((total, width), low), pltpu.VMEM((total, width), low),
-            pltpu.VMEM((total, hidden), low), pltpu.VMEM((total, hidden), low),
-            pltpu.VMEM((own, width), full), pltpu.VMEM((2, own, width), full),
-            pltpu.VMEM((3, 2, 3, own, width), low),
+            room((total, cols), low), room(w_out.shape, low), room((own, width), low), room(w_up.shape, low),
+            room(w_down.shape, low), room((own, width), low), room((own, width), low), room(place.shape, low),
+            room((total, width), low), room((total, cols), low), room((own, width), full), room((slots, width), low),
+            room((d_rows, hidden), low), dma((8,)), dma((6,)),
+            room((total, width), low), room((total, width), low),
+            room((total, hidden), low), room((total, hidden), low),
+            room((own, width), full), room((2, own, width), full),
+            room((3, 2, 3, own, width), low),
             dma((3, 3, PARTS)), dma((3, 3, PARTS)), dma((2, 3, PARTS)), dma((2, 3, PARTS)), dma((2,)), dma((2,)), dma((2,)),
         ]
         + sum_scratch(2 * width, hidden, MLP_CHUNKS, stages),
-        compiler_params=pltpu.CompilerParams(collective_id=2, has_side_effects=True, vmem_limit_bytes=56 << 20),
+        compiler_params=pltpu.CompilerParams(collective_id=2, has_side_effects=True, vmem_limit_bytes=VMEM_BYTES),
         cost_estimate=pl.CostEstimate(flops=16 * total * width * hidden, bytes_accessed=20 * total * width, transcendentals=0),
         name="middle",
-    )(merged, w_out, tokens, gain, w_up, w_down, grad_own, grad_across)
+    )(merged, w_out, tokens, gain, w_up, w_down, grad_own, grad_across, place)
 
 
 def last_kernel(
-    stages, dq_ref, dk_ref, dv_ref, w_ref, rows_ref, grad_residual_ref, tokens_ref, gain_ref, d_out_ref, gain_part_ref,
+    dp_count, stages, dq_ref, dk_ref, dv_ref, w_hbm, rows_hbm, grad_residual_hbm, tokens_hbm, gain_ref, gain_part_ref, d_out_ref,
     grad_tokens_ref, d_sum_ref, gains_ref,
-    mine, bufs, gain_all, sum_send, sum_recv, gain_send, gain_recv, acc, came, dp_send, dp_recv,
+    w_ref, rows_ref, grad_residual_ref, tokens_ref, load_sem, mine, bufs, gain_mine, gain_came, sum_send, sum_recv, gain_send, gain_recv, acc, came, dp_send, dp_recv,
 ):
+    load_w = pltpu.make_async_copy(w_hbm, w_ref, load_sem.at[0])
+    load_rows = pltpu.make_async_copy(rows_hbm, rows_ref, load_sem.at[1])
+    load_residual = pltpu.make_async_copy(grad_residual_hbm, grad_residual_ref, load_sem.at[2])
+    load_tokens = pltpu.make_async_copy(tokens_hbm, tokens_ref, load_sem.at[3])
+    for load in (load_w, load_rows, load_residual, load_tokens):
+        load.start()
     low, full = jnp.bfloat16, jnp.float32
     dp, mp = lax.axis_index("dp"), lax.axis_index("mp")
     pair, across, far = mp ^ 1, mp ^ 2, mp ^ 3
@@ -643,7 +762,8 @@
     part = own // PARTS
     cols = dq_ref.shape[1]
     to_pair, to_across = (dp, pair), (dp, across)
-    greet([to_pair, to_across, (dp, far)] + [(dp ^ (1 << j), mp) for j in range(stages)])
+    links = [to_pair, to_across] + [(dp ^ (1 << j), mp) for j in range(dp_count.bit_length() - 1)]
+    greet(links)
     add_step, add_drain = sum_steps(stages, QKV_CHUNKS, acc, came, dp_send, dp_recv, d_sum_ref)
     target = acc if stages else d_sum_ref
     chunk = target.shape[0] // QKV_CHUNKS
@@ -652,7 +772,11 @@
     def add(*steps):
         if stages:
             for k, i in steps:
-                add_step(k, i)
+                if 0 <= k < QKV_CHUNKS:
+                    add_step(k, i)
+
+    def tick(t):
+        add(*[(t - i, i) for i in range(2 * stages, 0, -1)])
 
     def piece(c):
         return pl.ds(pl.multiple_of(c * part, part), part)
@@ -671,73 +795,81 @@
         sum_copy(kind, c).wait_recv()
         return bufs[1, kind, piece(c), :].astype(full)
 
-    target[0:cols, :] = d_out_ref[...]
-    started = 0
-    for p, ref in enumerate((dq_ref, dk_ref, dv_ref)):
-        target[(p + 1) * cols:(p + 2) * cols, :] = lax.dot_general(
-            ref[...], rows_ref[...], TN, preferred_element_type=full
-        ).astype(low)
-        while started < QKV_CHUNKS and (started + 1) * chunk <= (p + 2) * cols:
-            add((started, 0))
-            started += 1
-
     def in_part(owner):
         where = pl.ds(pl.multiple_of(owner * own, own), own)
         total = jnp.dot(dq_ref[where, :], w_ref[0], preferred_element_type=full)
         total = total + jnp.dot(dk_ref[where, :], w_ref[1], preferred_element_type=full)
         return total + jnp.dot(dv_ref[where, :], w_ref[2], preferred_element_type=full)
 
+    def ready(low_row, high_row):
+        add(*[(k, 0) for k in range(QKV_CHUNKS) if low_row < (k + 1) * chunk <= high_row])
+
+    target[0:cols, :] = d_out_ref[...]
+    ready(0, cols)
+
+    def weight_grad(p, ref, gain_row):
+        grad = lax.dot_general(ref[...], rows_ref[...], TN, preferred_element_type=full)
+        target[(p + 1) * cols:(p + 2) * cols, :] = grad.astype(low)
+        ready((p + 1) * cols, (p + 2) * cols)
+        return gain_row + jnp.sum(grad * w_ref[p].astype(full), axis=0, keepdims=True)
+
+    load_w.wait()
     bufs[0, FAR] = in_part(far).astype(low)
     each(PARTS, lambda c: sum_copy(FAR, c).start())
+    load_rows.wait()
+    gain_row = weight_grad(0, dq_ref, jnp.zeros((1, width), full))
     mine[...] = in_part(across)
 
     def pass_across(c):
         bufs[0, ACROSS, piece(c), :] = (mine[piece(c), :] + arrived(FAR, c)).astype(low)
         sum_copy(ACROSS, c).start()
     each(PARTS, pass_across)
+    gain_row = weight_grad(1, dk_ref, gain_row)
+    gain_row = weight_grad(2, dv_ref, gain_row)
     bufs[0, PAIR] = in_part(pair).astype(low)
     each(PARTS, lambda c: sum_copy(PAIR, c).start())
+
+    def gain_copy(i):
+        return remote(gain_mine.at[i], gain_came.at[i], gain_send.at[i], gain_recv.at[i], links[i])
+
+    def gain_step(i):
+        gain_copy(i).wait_recv()
+        gain_mine[i + 1] = gain_mine[i] + gain_came[i]
+        if i + 1 < len(links):
+            gain_copy(i + 1).start()
+
+    row = lax.broadcasted_iota(jnp.int32, (8, width), 0)
+    gain_mine[0] = jnp.where(row == 0, gain_part_ref[...], jnp.where(row == 1, gain_row / gain_ref[0:1, :], 0.0))
+    gain_copy(0).start()
     mine[...] = in_part(mp)
-    add((0, 1))
+    load_residual.wait()
+    load_tokens.wait()
 
     def back_norm(c):
         grad = mine[piece(c), :] + arrived(PAIR, c) + arrived(ACROSS, c)
         unit, inverse = norm_unit(tokens_ref[piece(c), :].astype(full))
-        scaled = grad * gain_ref[...]
+        scaled = grad * gain_ref[0:1, :]
         first_mean = jnp.mean(scaled, axis=-1, keepdims=True)
         second_mean = jnp.mean(scaled * unit, axis=-1, keepdims=True)
         total = inverse * (scaled - first_mean - unit * second_mean) + grad_residual_ref[piece(c), :]
         grad_tokens_ref[piece(c), :] = total.astype(low)
 
-    each(1, back_norm)
-    add((0, 2), (1, 1))
-    each(1, lambda c: back_norm(c + 1))
-    add((0, 3), (1, 2), (2, 1))
-    each(1, lambda c: back_norm(c + 2))
-    add((0, 4), (1, 3), (2, 2))
-    each(1, lambda c: back_norm(c + 3))
-    add((0, 5), (1, 4), (2, 3), (1, 5), (2, 4), (2, 5), (0, 6), (1, 6), (2, 6))
+    for t in range(1, QKV_CHUNKS + 2 * stages if stages else 1):
+        tick(t)
+        for c, when in enumerate(NORM_TICKS):
+            if t == when:
+                each(1, lambda i: back_norm(i + c))
+        if 2 <= t < 2 + len(links):
+            gain_step(t - 2)
+    if not stages:
+        each(PARTS, back_norm)
+        for i in range(len(links)):
+            gain_step(i)
+    gains_ref[...] = gain_mine[len(links)]
     if stages:
         add_drain()
-
-    total = jnp.zeros((1, width), full)
-    for p in range(3):
-        prod = w_ref[p].astype(full) * d_sum_ref[(p + 1) * cols:(p + 2) * cols, :].astype(full)
-        total = total + jnp.sum(prod, axis=0, keepdims=True)
-    row = lax.broadcasted_iota(jnp.int32, (8, width), 0)
-    gain_all[mp] = jnp.where(row == 0, gain_part_ref[...], jnp.where(row == 1, total / gain_ref[...], 0.0))
-
-    def gain_copy(i, owner, other):
-        return remote(gain_all.at[owner], gain_all.at[owner], gain_send.at[i], gain_recv.at[i], (dp, other))
-
-    others = (pair, across, far)
-    for i, other in enumerate(others):
-        gain_copy(i, mp, other).start()
-    for i, other in enumerate(others):
-        gain_copy(i, other, other).wait_recv()
-    gains_ref[...] = (gain_all[0] + gain_all[1]) + (gain_all[2] + gain_all[3])
-    for i, other in enumerate(others):
-        gain_copy(i, mp, other).wait_send()
+    for i in range(len(links)):
+        gain_copy(i).wait_send()
 
     def drain(c):
         for kind in range(3):
@@ -745,28 +877,35 @@
     each(PARTS, drain)
 
 
-def last(dp_count, dq, dk, dv, w_qkv, rows, grad_residual, tokens, gain, d_out, gain_part):
+def last(dp_count, dq, dk, dv, w_qkv, rows, grad_residual, tokens, gain, gain_part, d_out):
     own, width = tokens.shape
     cols = dq.shape[1]
-    stages = sum_stages(4 * cols, QKV_CHUNKS, dp_count)
+    d_rows = 4 * cols
+    stages = sum_stages(d_rows, QKV_CHUNKS, dp_count)
     low, full = jnp.bfloat16, jnp.float32
+    count = 2 + dp_count.bit_length() - 1
+    hbm = pl.BlockSpec(memory_space=pltpu.HBM)
     vmem = pl.BlockSpec(memory_space=pltpu.VMEM)
     dma = pltpu.SemaphoreType.DMA
     shape = jax.ShapeDtypeStruct
-    return pl.pallas_call(
-        functools.partial(last_kernel, stages),
-        out_shape=[shape((own, width), low), shape((4 * cols, width), low), shape((8, width), full)],
-        in_specs=[vmem] * 10,
+    grad_tokens, d_sum, gains = pl.pallas_call(
+        functools.partial(last_kernel, dp_count, stages),
+        out_shape=[shape((own, width), low), shape((d_rows, width), low), shape((8, width), full)],
+        in_specs=[vmem] * 3 + [hbm] * 4 + [vmem] * 3,
         out_specs=[vmem] * 3,
         scratch_shapes=[
-            pltpu.VMEM((own, width), full), pltpu.VMEM((2, 3, own, width), low), pltpu.VMEM((4, 8, width), full),
-            dma((3, PARTS)), dma((3, PARTS)), dma((3,)), dma((3,)),
+            pltpu.VMEM(w_qkv.shape, low), pltpu.VMEM(rows.shape, low), pltpu.VMEM((own, width), full),
+            pltpu.VMEM((own, width), low), dma((4,)),
+            pltpu.VMEM((own, width), full), pltpu.VMEM((2, 3, own, width), low),
+            pltpu.VMEM((count + 1, 8, width), full), pltpu.VMEM((count, 8, width), full),
+            dma((3, PARTS)), dma((3, PARTS)), dma((count,)), dma((count,)),
         ]
-        + sum_scratch(4 * cols, width, QKV_CHUNKS, stages),
-        compiler_params=pltpu.CompilerParams(collective_id=3, has_side_effects=True, vmem_limit_bytes=48 << 20),
+        + sum_scratch(d_rows, width, QKV_CHUNKS, stages),
+        compiler_params=pltpu.CompilerParams(collective_id=3, has_side_effects=True, vmem_limit_bytes=VMEM_BYTES),
         cost_estimate=pl.CostEstimate(flops=12 * 4 * own * width * cols, bytes_accessed=20 * own * width, transcendentals=0),
         name="last",
-    )(dq, dk, dv, w_qkv, rows, grad_residual, tokens, gain, d_out, gain_part)
+    )(dq, dk, dv, w_qkv, rows, grad_residual, tokens, gain, gain_part, d_out)
+    return grad_tokens, d_sum if stages else lax.psum(d_sum, "dp"), gains
 
 
 def local(
@@ -775,50 +914,54 @@
     width = tokens.shape[1]
     dp_count = lax.axis_size("dp")
     capacity = cotangent.shape[0] // dp_count
-    own_rows = tokens.shape[0]
-    contract_first = (((0,), (0,)), ((), ()))
-    low = jnp.bfloat16
-
-    owners = gene_owner[:, 0]
-    place = jnp.arange(own_rows, dtype=jnp.int32)
-    earlier = (owners[:, None] == owners[None, :]) & (place[None, :] < place[:, None])
-    slots = owners * capacity + jnp.sum(earlier.astype(jnp.int32), axis=1)
-    onehot = (slots[:, None] == jnp.arange(dp_count * capacity, dtype=jnp.int32)[None, :]).astype(low)
-
+    low, full = jnp.bfloat16, jnp.float32
     w_rows = jnp.swapaxes(w_qkv, 1, 2)
-    gain_one = gain_attn.reshape(1, -1)
-    attn_in, *projected, returned = project(tokens, gain_one, w_rows, cotangent.reshape(dp_count, capacity, width))
-    returned = returned.reshape(dp_count * capacity, width)
-    grad_block = jnp.dot(onehot, returned, preferred_element_type=jnp.float32).astype(low)
+    gains_in = jnp.stack([gain_attn, gain_mlp])
+    attn_in, *projected, grad_block, place = project(
+        tokens, gains_in, w_rows, cotangent.reshape(dp_count, capacity, width), gene_owner.reshape(1, -1)
+    )
     grad_across = lax.ppermute(grad_block, "mp", [(i, i ^ 2) for i in range(lax.axis_size("mp"))])
     merged, log_sums = attend_forward(segment_ids, *projected)
-    residual_rows, grad_merged, grad_residual, output, mlp_sum, d_out = middle(
-        dp_count, merged, w_attn_out, tokens, gain_mlp.reshape(1, -1), w_up, w_down, grad_block, grad_across
+    residual_rows, grad_merged, grad_residual, outgoing, first, second, gain_part, d_out = middle(
+        dp_count, merged, w_attn_out, tokens, gains_in, w_up, w_down, grad_block, grad_across, place
     )
-    if not sum_stages(2 * width, MLP_CHUNKS, dp_count):
-        mlp_sum = lax.psum(mlp_sum, "dp")
-    mlp_sum = mlp_sum.reshape(MLP_CHUNKS, 2, width // MLP_CHUNKS, w_up.shape[1]).astype(jnp.float32)
-    up_sum, down_sum = (mlp_sum[:, i].reshape(w_up.shape) for i in range(2))
-    gain_part = (jnp.sum(w_up.astype(jnp.float32) * up_sum, axis=1) / gain_mlp).reshape(1, -1)
-    outgoing = lax.dot_general(onehot, output, contract_first, preferred_element_type=jnp.float32).astype(low)
+    cols = w_qkv.shape[2]
+    if sum_stages(2 * width, MLP_CHUNKS, dp_count):
+        size = width // MLP_CHUNKS
+        place_y = lax.rem(lax.axis_index("dp"), 2) == 0
+        place_z = lax.rem(lax.axis_index("dp") // 2, 2) == 0
+        count = sum(left_bit(k, MLP_CHUNKS) == 0 for k in range(MLP_CHUNKS))
+        first_came = lax.ppermute(first, "dp", [(i, i ^ 1) for i in range(dp_count)])
+        second_came = lax.ppermute(second, "dp", [(i, i ^ 2) for i in range(dp_count)])
+        gain_part, first_came, second_came = lax.optimization_barrier((gain_part, first_came, second_came))
+        first = [jnp.where(place_y, first, first_came), jnp.where(place_y, first_came, first)]
+        second = jnp.stack(
+            [
+                one.reshape(MLP_CHUNKS - count, 2, size // 2, width)
+                for one in (jnp.where(place_z, second, second_came), jnp.where(place_z, second_came, second))
+            ],
+            axis=2,
+        )
+        up_sum, down_sum = (
+            jnp.concatenate([first[i], second[:, i].reshape(-1, width)]).astype(full) for i in range(2)
+        )
+    else:
+        d_sum = lax.psum(jnp.concatenate([first, second]), "dp").reshape(MLP_CHUNKS, 2, -1, width).astype(full)
+        up_sum, down_sum = (d_sum[:, i].reshape(-1, width) for i in range(2))
     relaid = lax.all_to_all(
         outgoing.reshape(dp_count, capacity, width), "dp", split_axis=0, concat_axis=0, tiled=True
     ).reshape(dp_count * capacity, width)
     grad_proj = attend_backward(segment_ids, *projected, merged, grad_merged, log_sums)
     grad_tokens, weight_sum, gains = last(
-        dp_count, *grad_proj, w_rows, attn_in, grad_residual, tokens, gain_one, d_out, gain_part
+        dp_count, *grad_proj, w_rows, attn_in, grad_residual, tokens, gains_in, gain_part, d_out
     )
-    cols = w_qkv.shape[2]
-    if not sum_stages(4 * cols, QKV_CHUNKS, dp_count):
-        weight_sum = lax.psum(weight_sum, "dp")
-        products = w_rows.astype(jnp.float32) * weight_sum[cols:].reshape(w_rows.shape).astype(jnp.float32)
-        gains = gains.at[1].set(lax.psum(jnp.sum(products, axis=(0, 1)) / gain_attn, "mp"))
-    weight_sum = weight_sum.astype(jnp.float32)
+    qkv_sum = weight_sum[cols:].reshape(3, cols, width).astype(full)
+    attn_sum = weight_sum[:cols].astype(full)
     return (
         relaid,
         grad_tokens,
-        jnp.swapaxes(weight_sum[cols:].reshape(3, cols, width), 1, 2),
-        weight_sum[:cols],
+        jnp.swapaxes(qkv_sum, 1, 2),
+        attn_sum,
         up_sum,
         down_sum,
         gains[1],

time: 307 us -> 279 us (0.909)
  Pallas kernels: 274 us -> 256 us
  local copies, waits for them, and re-layouts: 21 us -> 6.83 us
  other arithmetic: 2 us -> 7.19 us
  matrix products: 3.71 us -> 0 us
    pallas_call x1, Pallas kernels: 130 us -> 110 us  [middle(): pl.pallas_call(functools.partial(middle_kernel, stages), out_shape=[shape...]
    unnamed x40 -> x10, local copies, waits for them, and re-layouts: 12.5 us -> 2.71 us
    slice x3, local copies, waits for them, and re-layouts: 6.68 us -> 1.31 us  [the longest x1 1.23 us: local(): qkv_sum = weight_sum[cols:].reshape(3, cols, width).astype(full)]
    convert_element_type x0 -> x3, other arithmetic: none -> 4.97 us  [the longest x2 3.15 us: local(): jnp.concatenate([first[i], second[:, i].reshape(-1, width)]).astype(full)]
    pallas_call x1, Pallas kernels: 35.5 us -> 31 us  [attend_backward(): pl.pallas_call(functools.partial(bwd_kernel, n, heads), grid_spec=pltpu.P...]
    pallas_call x1, Pallas kernels: 59.4 us -> 63.4 us  [last(): pl.pallas_call(functools.partial(last_kernel, dp_count, stages), out_shap...]
    dot_general x2 -> x0, matrix products: 3.71 us -> none  [the longest x1 2.89 us: local(): lax.dot_general(onehot, output, contract_first, preferred_element_type=jn...]
    ppermute x0 -> x2, starting transfers between devices: none -> 3.48 us  [the longest x1 2.02 us: local(): lax.ppermute(first, 'dp', [(i, i ^ 1) for i in range(dp_count)])]
  transfers between devices with their start and end apart: 2 -> 4, of which waited for: 0 -> 0; matrix products, arithmetic and copies ran while one was open for 3% -> 3% of each run, Pallas kernels for 38% -> 41%
where the time goes in v5:
time: 279 us
  Pallas kernels  256 us (92%)
  starting transfers between devices  8.25 us (3%)
  other arithmetic  7.19 us (3%)
  local copies, waits for them, and re-layouts  6.83 us (2%)
    pallas_call x1, Pallas kernels, middle(): pl.pallas_call(functools.partial(middle_kernel, stages), out_shape=[shape...  110 us
    pallas_call x1, Pallas kernels, last(): pl.pallas_call(functools.partial(last_kernel, dp_count, stages), out_shap...  63.4 us
    pallas_call x1, Pallas kernels, attend_backward(): pl.pallas_call(functools.partial(bwd_kernel, n, heads), grid_spec=pltpu.P...  31 us
    pallas_call x1, Pallas kernels, project(): pl.pallas_call(functools.partial(project_kernel, dp_count), out_shape=[ja...  30.3 us
    pallas_call x1, Pallas kernels, attend_forward(): pl.pallas_call(functools.partial(fwd_kernel, n, heads), grid_spec=pltpu.P...  20.9 us
  transfers between devices with their start and end apart: 4, of which 0 were waited for; matrix products, arithmetic and copies ran while one was open for 3% of the time, Pallas kernels for 41%

profile of v5, /device:TPU:0, one launch (start us, length us, event | category | flops | bytes accessed | tf_op | source)
XLA Modules:
  0.0 278.9 jit_solution(7620590224351286576)
XLA Ops:
  0.6 0.7 stack.13
  1.3 0.7 stack.12
  2.0 0.6 pad_maximum_fusion.1.gain_ref
  2.6 30.3 %project.1 = (bf16[2048,768]{1,0:T(8,128)(2,1)}, bf16[2048,192]{1,0:T(8,128)(2,1)}, bf16[2048,192]{1,0:T(8,128)(2,1)}, bf16[2048,192]{1,0:T(8,128)(2,1)}, bf16[5...) custom-call(bf16[512,768]{1,0:T(8,128)(2,1)} %tokens_hbm.5, f32[2,768]{1,0:T(2,128)} %pad_maximum_fusion.1.gain_ref, ...), custom_call_target="tpu_custom_call" | custom-call | flops 1811939328 | bytes 15728640 | tf_op jit(solution)/shard_map/project/pallas_call | solution.py:434
  32.9 0.6 collective-permute-start
  33.6 20.9 %attend_forward.1 = (bf16[2048,192]{1,0:T(8,128)(2,1)}, f32[8,2048]{1,0:T(8,128)}) custom-call(s32[2048]{0:T(1024)} %bitcast.24, s32[1,2048]{1,0:T(1,128)} %segv_ref.3, bf16[2048,192]{1,0:T(8,128)(2,1)} %get-tuple-element.32.q_ref, bf16[2048,192]{1,0:T(8,128)(2,1)} %get-tuple-element.33.k_ref, bf16[2048,192]{1,0:T(8,128)(2,1)} %get-tuple-element.34.v_ref), custom_call_target="tpu_custom_call" | custom-call | flops 3221225472 | bytes 3145728 | tf_op jit(solution)/shard_map/attend_forward/pallas_call | solution.py:99
  54.5 0.9 copy-done.3
  55.3 110.2 %middle.1 = (bf16[2048,768]{1,0:T(8,128)(2,1)}, bf16[2048,192]{1,0:T(8,128)(2,1)}, f32[512,768]{1,0:T(8,128)}, bf16[640,768]{1,0:T(8,128)(2,1)}, bf16[384,768]{1...) custom-call(bf16[2048,192]{1,0:T(8,128)(2,1)} %get-tuple-element.35.merged_hbm.o_ref, ...), custom_call_target="tpu_custom_call" | custom-call | flops 19327352832 | bytes 31457280 | tf_op jit(solution)/shard_map/middle/pallas_call | solution.py:721
  165.6 4.1 %all-to-all-start = ((bf16[8,80,768]{2,1,0:T(8,128)(2,1)}), bf16[8,80,768]{2,1,0:T(8,128)(2,1)S(1)}, u32[]{:S(2)}, u32[]{:S(2)}) async-start(bf16[8,80,768]{2,1,0:T(8,128)(2,1)} %bitcast.20), calls=%async_computation | async-start | bytes 1966080 | tf_op jit(solution)/shard_map/all_to_all | solution.py:951
  169.7 2.0 collective-permute-start.1
  171.8 1.5 collective-permute-start.2
  173.2 31.0 %attend_backward.1 = (bf16[2048,192]{1,0:T(8,128)(2,1)}, bf16[2048,192]{1,0:T(8,128)(2,1)}, bf16[2048,192]{1,0:T(8,128)(2,1)}) custom-call(s32[2048]{0:T(1024)} %bitcast.25, s32[1,2048]{1,0:T(1,128)} %segv_ref.3, bf16[2048,192]{1,0:T(8,128)(2,1)} %get-tuple-element.32.q_ref, bf16[2048,192]{1,0:T(8,128)(2,1)} %get-tuple-element.33.k_ref, ...), custom_call_target="tpu_custom_call" | custom-call | flops 8053063680 | bytes 6291456 | tf_op jit(solution)/shard_map/attend_backward/pallas_call | solution.py:179
  204.3 0.0 collective-permute-done.1
  204.3 63.4 %last.1 = (bf16[512,768]{1,0:T(8,128)(2,1)}, bf16[768,768]{1,0:T(8,128)(2,1)}, f32[8,768]{1,0:T(8,128)}) custom-call(bf16[2048,192]{1,0:T(8,128)(2,1)} %get-tuple-element.41.dq_ref, bf16[2048,192]{1,0:T(8,128)(2,1)} %get-tuple-element.42.dk_ref, bf16[2048,192]{1,0:T(8,128)(2,1)} %get-tuple-element.43.dv_ref, bf16[3,192,768]{2,1,0:T(8,128)(2,1)} %bitcast.23, ...), custom_call_target="tpu_custom_call" | custom-call | flops 3623878656 | bytes 7864320 | tf_op jit(solution)/shard_map/last/pallas_call | solution.py:891
  267.7 1.2 slice.18
  268.9 0.2 broadcast_select_fusion
  269.1 0.1 pad_maximum_fusion
  269.3 1.4 slice_reduce_fusion
  270.8 1.6 maximum_convert_fusion
  272.3 1.6 maximum_convert_fusion.1
  273.9 1.8 slice_convert_fusion
  275.7 1.4 convert_bitcast_fusion
  277.1 0.9 copy.22
  278.0 0.9 copy.23
  (12 shorter events, 0.1 us)
Async XLA Ops:
  32.9 21.5 %collective-permute-start = (bf16[512,768]{1,0:T(8,128)(2,1)}, bf16[512,768]{1,0:T(8,128)(2,1)S(1)}, u32[]{:S(2)}, u32[]{:S(2)}) collective-permute-start(bf16[512,768]{1,0:T(8,128)(2,1)} %get-tuple-element.36.grad_own_hbm), channel_id=1, source_target_pairs={{0,2},{1,3},{2,0},{3,1},{4,6},{5,7},{6,4},{7,5},{8,10},{9,11},{10,... | collective-permute-start | bytes 2359304 | tf_op jit(solution)/shard_map/ppermute | solution.py:923
  54.5 0.9 copy-start.3
  165.6 4.2 %copy-start.1 = (bf16[384,768]{1,0:T(8,128)(2,1)S(1)}, bf16[384,768]{1,0:T(8,128)(2,1)}, u32[]{:S(2)}) copy-start(bf16[384,768]{1,0:T(8,128)(2,1)} %get-tuple-element.47) | copy-start | bytes 1769476
  165.6 6.2 %copy-start.2 = (bf16[384,768]{1,0:T(8,128)(2,1)S(1)}, bf16[384,768]{1,0:T(8,128)(2,1)}, u32[]{:S(2)}) copy-start(bf16[384,768]{1,0:T(8,128)(2,1)} %get-tuple-element.48) | copy-start | bytes 1769476
  165.6 111.5 %all-to-all-start = ((bf16[8,80,768]{2,1,0:T(8,128)(2,1)}), bf16[8,80,768]{2,1,0:T(8,128)(2,1)S(1)}, u32[]{:S(2)}, u32[]{:S(2)}) async-start(bf16[8,80,768]{2,1,0:T(8,128)(2,1)} %bitcast.20), calls=%async_computation | async-start | bytes 1966080 | tf_op jit(solution)/shard_map/all_to_all | solution.py:951
  169.7 34.5 %collective-permute-start.1 = (bf16[384,768]{1,0:T(8,128)(2,1)S(1)}, bf16[384,768]{1,0:T(8,128)(2,1)S(1)}, u32[]{:S(2)}, u32[]{:S(2)}) collective-permute-start(bf16[384,768]{1,0:T(8,128)(2,1)S(1)} %copy-done.1), channel_id=1, source_target_pairs={{0,4},{4,0},{8,12},{12,8},{16,20},{20,16},{24,28},{28,24},{1,5},{5... | collective-permute-start | bytes 1769480 | tf_op jit(solution)/shard_map/ppermute | solution.py:934
  171.8 32.5 %collective-permute-start.2 = (bf16[384,768]{1,0:T(8,128)(2,1)S(1)}, bf16[384,768]{1,0:T(8,128)(2,1)S(1)}, u32[]{:S(2)}, u32[]{:S(2)}) collective-permute-start(bf16[384,768]{1,0:T(8,128)(2,1)S(1)} %copy-done.2), channel_id=1, source_target_pairs={{0,8},{4,12},{8,0},{12,4},{16,24},{20,28},{24,16},{28,20},{1,9},{5... | collective-permute-start | bytes 1769480 | tf_op jit(solution)/shard_map/ppermute | solution.py:935
  275.7 2.3 copy-start

commit v6 on v5

--- a/solution.py
+++ b/solution.py
@@ -14,6 +14,10 @@
 TN = (((0,), (0,)), ((), ()))
 MASKED = -1e30
 epsilon = 1e-05
+
+
+def local_copies(pairs, sems):
+    return [pltpu.make_async_copy(src, dst, sems.at[i]) for i, (src, dst) in enumerate(pairs)]
 
 
 def lower_bound(seg, n, value):
@@ -196,8 +200,7 @@
 PARTS = 4
 VMEM_BYTES = 60 << 20
 MLP_CHUNKS = 6
-QKV_CHUNKS = 6
-NORM_TICKS = (5, 7, 9, 10)
+QKV_CHUNKS = 3
 
 
 def remote(src, dst, send, recv, device):
@@ -234,8 +237,12 @@
     ]
 
 
-def left_bit(k, chunks):
-    return 0 if 2 * k < chunks else 1
+def left_bit(k):
+    return k % 2
+
+
+def packed(k, chunks):
+    return k // 2 if k % 2 == 0 else (chunks + 1) // 2 + k // 2
 
 
 def sum_steps(stages, chunks, acc, came, send, recv, out, half=False):
@@ -257,7 +264,7 @@
     def placed(k, start):
         if not half:
             return start
-        return k * (chunk // 2) + bit(1 - left_bit(k, chunks)) * (chunk // 4) + start - held(k, 2)
+        return packed(k, chunks) * (chunk // 2) + bit(1 - left_bit(k)) * (chunk // 4) + start - held(k, 2)
 
     def halve(k, s):
         size = chunk >> (s + 1)
@@ -269,9 +276,9 @@
 
     def double(k, s, mine=True):
         if half and s == 1:
-            s = 1 - left_bit(k, chunks)
+            s = 1 - left_bit(k)
             place = bit(s) if mine else 1 - bit(s)
-            rows = out.at[span(k * (chunk // 2) + place * (chunk // 4), chunk // 4)]
+            rows = out.at[span(packed(k, chunks) * (chunk // 2) + place * (chunk // 4), chunk // 4)]
             return remote(rows, rows, send.at[k, stages + 1], recv.at[k, stages + 1], (dp ^ (1 << s), mp))
         size = chunk >> (s + 1)
         start = held(k, s + 1) if mine else held(k, s) + (1 - bit(s)) * size
@@ -317,13 +324,17 @@
 
 
 def project_kernel(
-    dp_count, tokens_hbm, gain_ref, w_hbm, cot_ref, owner_ref, rows_hbm, q_ref, k_ref, v_ref, grad_ref, place_ref,
-    tokens_ref, w_ref, rows_ref, load_sem, store_sem, returned_ref, across_send, across_recv, pair_send, pair_recv, pass_send, pass_recv, slot_send, slot_recv, self_sem,
+    dp_count, tokens_hbm, gain_hbm, w_hbm, cot_ref, owner_hbm, rows_hbm, q_hbm, k_hbm, v_hbm, grad_hbm, place_hbm,
+    tokens_ref, gain_ref, w_ref, owner_ref, rows_ref, q_ref, k_ref, v_ref, grad_ref, place_ref, load_sem, store_sem, out_sem, returned_ref, across_send, across_recv, pair_send, pair_recv, pass_send, pass_recv, slot_send, slot_recv, self_sem,
 ):
-    load_tokens = pltpu.make_async_copy(tokens_hbm, tokens_ref, load_sem.at[0])
-    load_w = pltpu.make_async_copy(w_hbm, w_ref, load_sem.at[1])
-    load_tokens.start()
-    load_w.start()
+    load_tokens, load_gain, load_w, load_owner = loads = local_copies(
+        ((tokens_hbm, tokens_ref), (gain_hbm, gain_ref), (w_hbm, w_ref), (owner_hbm, owner_ref)), load_sem
+    )
+    for load in loads:
+        load.start()
+    stores = local_copies(
+        ((q_ref, q_hbm), (k_ref, k_hbm), (v_ref, v_hbm), (place_ref, place_hbm), (grad_ref, grad_hbm)), out_sem
+    )
     dp, mp = lax.axis_index("dp"), lax.axis_index("mp")
     pair, across, far = mp ^ 1, mp ^ 2, mp ^ 3
     own = tokens_ref.shape[0]
@@ -345,18 +356,18 @@
         rows = pl.ds(pl.multiple_of(owner * own, own), own)
         return pltpu.make_async_copy(rows_ref.at[rows], rows_hbm.at[rows], store_sem.at[i])
 
+    for k in range(1, dp_count):
+        slot_copy(k).start()
+    self_copy = pltpu.make_async_copy(cot_ref.at[dp], returned_ref.at[dp], self_sem)
+    self_copy.start()
     load_tokens.wait()
+    load_gain.wait()
     for c in range(PARTS):
         values = tokens_ref[c * part:(c + 1) * part, :].astype(jnp.float32)
         unit, _ = norm_unit(values)
         rows_ref[spot(mp, c, part), :] = (unit * gain_ref[0:1, :]).astype(jnp.bfloat16)
         gather_copy(c, mp, (dp, across), across_send, across_recv).start()
         gather_copy(c, mp, (dp, pair), pair_send, pair_recv).start()
-    for k in range(1, dp_count):
-        slot_copy(k).start()
-    self_copy = pltpu.make_async_copy(cot_ref.at[dp], returned_ref.at[dp], self_sem)
-    self_copy.start()
-
     def product(owner, half):
         where = spot(owner, half, own // 2)
         rows = rows_ref[where, :]
@@ -370,6 +381,7 @@
         lax.fori_loop(0, 2, step, 0)
 
     load_w.wait()
+    load_owner.wait()
     both(mp)
     store(0, mp).start()
     capacity = cot_ref.shape[1]
@@ -383,6 +395,7 @@
     place_ref[...] = jnp.where(
         lax.broadcasted_iota(jnp.int32, (slots, own), 0).astype(jnp.float32) == slot_row, 1.0, 0.0
     ).astype(jnp.bfloat16)
+    stores[3].start()
     for c in range(PARTS):
         gather_copy(c, pair, (dp, pair), pair_send, pair_recv).wait_recv()
     both(pair)
@@ -398,6 +411,8 @@
             gather_copy(c, far, (dp, pair), pass_send, pass_recv).wait_recv()
         product(far, half)
     store(3, far).start()
+    for out in stores[:3]:
+        out.start()
     for c in range(PARTS):
         gather_copy(c, mp, (dp, across), across_send, across_recv).wait_send()
         gather_copy(c, mp, (dp, pair), pair_send, pair_recv).wait_send()
@@ -421,6 +436,9 @@
             pick = jnp.where(pick, 1.0, 0.0).astype(jnp.bfloat16)
             return total + jnp.dot(pick, returned_ref[d], preferred_element_type=jnp.float32)
         grad_ref[...] = lax.fori_loop(0, dp_count, take, jnp.zeros(grad_ref.shape, jnp.float32)).astype(jnp.bfloat16)
+    stores[4].start()
+    for out in stores:
+        out.wait()
 
 
 def project(tokens, gain, w_qkv, cot, owners):
@@ -436,12 +454,12 @@
         out_shape=[jax.ShapeDtypeStruct((total, width), jnp.bfloat16)]
         + [jax.ShapeDtypeStruct((total, cols), jnp.bfloat16)] * 3
         + [jax.ShapeDtypeStruct((own, width), jnp.bfloat16), jax.ShapeDtypeStruct((dp_count * cot.shape[1], own), jnp.bfloat16)],
-        in_specs=[hbm, vmem, hbm, hbm, vmem],
-        out_specs=[hbm] + [vmem] * 5,
-        scratch_shapes=[
-            pltpu.VMEM(tokens.shape, tokens.dtype), pltpu.VMEM(w_qkv.shape, w_qkv.dtype),
-            pltpu.VMEM((total, width), jnp.bfloat16), dma((2,)), dma((4,)), pltpu.VMEM(cot.shape, cot.dtype),
-        ] + [dma((PARTS,))] * 6 + [dma((dp_count,))] * 2 + [dma],
+        in_specs=[hbm] * 5,
+        out_specs=[hbm] * 6,
+        scratch_shapes=[pltpu.VMEM(one.shape, one.dtype) for one in (tokens, gain, w_qkv, owners)]
+        + [pltpu.VMEM((total, width), jnp.bfloat16)] + [pltpu.VMEM((total, cols), jnp.bfloat16)] * 3
+        + [pltpu.VMEM((own, width), jnp.bfloat16), pltpu.VMEM((dp_count * cot.shape[1], own), jnp.bfloat16)]
+        + [dma((4,)), dma((4,)), dma((5,)), pltpu.VMEM(cot.shape, cot.dtype)] + [dma((PARTS,))] * 6 + [dma((dp_count,))] * 2 + [dma],
         compiler_params=pltpu.CompilerParams(collective_id=1, has_side_effects=True, vmem_limit_bytes=VMEM_BYTES),
         cost_estimate=pl.CostEstimate(flops=6 * total * width * cols, bytes_accessed=10 * total * width, transcendentals=0),
         name="project",
@@ -455,30 +473,32 @@
 
 
 def middle_kernel(
-    stages, merged_hbm, w_out_hbm, tokens_hbm, gain_ref, w_up_hbm, w_down_hbm, grad_own_hbm, grad_across_hbm, place_hbm,
-    back_rows_hbm, grad_merged_hbm, grad_residual_hbm, outgoing_hbm, first_hbm, second_hbm, gain_part_ref, d_out_ref,
-    merged_ref, w_out_ref, tokens_ref, w_up_ref, w_down_ref, grad_own_ref, grad_across_ref, place_ref,
+    stages, merged_hbm, w_out_hbm, tokens_hbm, gain_hbm, w_up_hbm, w_down_hbm, grad_own_hbm, grad_across_hbm, place_hbm,
+    back_rows_hbm, grad_merged_hbm, grad_residual_hbm, outgoing_hbm, first_hbm, second_hbm, gain_part_hbm, d_out_hbm,
+    merged_ref, w_out_ref, tokens_ref, gain_ref, gain_part_ref, d_out_ref, w_up_ref, w_down_ref, grad_own_ref, grad_across_ref, place_ref,
     back_rows_ref, grad_merged_ref, grad_residual_ref, outgoing_ref, d_mlp_ref, load_sem, store_sem,
     mlp_rows, grad_rows, active, grad_pre, residual, mine, bufs,
     sum_send, sum_recv, row_send, row_recv, grad_send, grad_recv, self_sem, acc, came, dp_send, dp_recv,
 ):
     first_rows = first_hbm.shape[0]
-    loads = [
-        pltpu.make_async_copy(src, dst, load_sem.at[i])
-        for i, (src, dst) in enumerate((
+    loads = local_copies(
+        (
             (merged_hbm, merged_ref), (w_out_hbm, w_out_ref), (tokens_hbm, tokens_ref), (grad_own_hbm, grad_own_ref),
             (grad_across_hbm, grad_across_ref), (w_up_hbm, w_up_ref), (w_down_hbm, w_down_ref), (place_hbm, place_ref),
-        ))
-    ]
+            (gain_hbm, gain_ref),
+        ),
+        load_sem,
+    )
     for load in loads:
         load.start()
-    stores = [
-        pltpu.make_async_copy(src, dst, store_sem.at[i])
-        for i, (src, dst) in enumerate((
+    stores = local_copies(
+        (
             (back_rows_ref, back_rows_hbm), (grad_merged_ref, grad_merged_hbm), (grad_residual_ref, grad_residual_hbm),
             (outgoing_ref, outgoing_hbm), (d_mlp_ref.at[0:first_rows], first_hbm), (d_mlp_ref.at[first_rows:], second_hbm),
-        ))
-    ]
+            (gain_part_ref, gain_part_hbm), (d_out_ref, d_out_hbm),
+        ),
+        store_sem,
+    )
     low, full = jnp.bfloat16, jnp.float32
     dp, mp = lax.axis_index("dp"), lax.axis_index("mp")
     pair, across, far = mp ^ 1, mp ^ 2, mp ^ 3
@@ -500,7 +520,7 @@
     def grad_copy(i, owner, src):
         return remote(src, grad_rows.at[spot(owner)], grad_send.at[i], grad_recv.at[i], to_pair)
 
-    local_copies = [
+    grad_loads = [
         pltpu.make_async_copy(grad_own_ref, grad_rows.at[spot(mp)], self_sem.at[0]),
         pltpu.make_async_copy(grad_across_ref, grad_rows.at[spot(across)], self_sem.at[1]),
     ]
@@ -545,17 +565,17 @@
     each(PARTS, lambda c: sum_copy(0, PAIR, c).start())
     for load in loads[2:5]:
         load.wait()
-    for copy in local_copies:
+    for copy in grad_loads:
         copy.start()
     grad_copy(0, mp, grad_own_ref).start()
     grad_copy(1, across, grad_across_ref).start()
     mine[0] = out_part(mp) + tokens_ref[...].astype(full)
-    for copy in local_copies:
+    for copy in grad_loads:
         copy.wait()
     grad_copy(0, pair, grad_own_ref).wait_recv()
     grad_copy(1, far, grad_across_ref).wait_recv()
 
-    for load in loads[5:8]:
+    for load in loads[5:]:
         load.wait()
     blocks = w_up_ref.shape[1] // 256
     both = 2 * part
@@ -640,7 +660,7 @@
         row_copy(1, 0, c, mp, back_rows_ref).start()
         row_copy(1, 1, c, mp, back_rows_ref).start()
     def tick(t):
-        add(*[(t - i, i) for i in range(2 * stages, 0, -1) if 0 <= t - i < MLP_CHUNKS])
+        add(*[(t - i, i) for i in range(1, 2 * stages + 1) if 0 <= t - i < MLP_CHUNKS])
 
     each(2, back_norm)
     tick(1)
@@ -671,19 +691,24 @@
     for c in range(PARTS):
         each(1, lambda i: hand_on(i + c))
         tick(4 + c)
+    tick(8)
     merged_part(across)
     each(PARTS, lambda c: row_copy(1, 2, c, far, back_rows_ref).wait_recv())
+    tick(9)
     merged_part(far)
     stores[0].start()
     stores[1].start()
     stores[2].start()
     d_out_ref[...] = lax.dot_general(merged_ref[...], back_rows_ref[...], TN, preferred_element_type=full).astype(low)
+    stores[6].start()
+    stores[7].start()
+
+    tick(10)
 
     def finish(c):
         mine[0, piece(c), :] = mine[0, piece(c), :] + arrived(2, PAIR, c) + arrived(2, ACROSS, c)
     for c in range(PARTS):
         each(1, lambda i: finish(i + c))
-        tick(8 + c)
     stores[4].start()
     stores[5].start()
     outgoing_ref[...] = jnp.dot(place_ref[...], mine[0].astype(low), preferred_element_type=full).astype(low)
@@ -724,13 +749,14 @@
             shape((total, width), low), shape((total, cols), low), shape((own, width), full), shape((slots, width), low),
             shape((d_rows // 2, hidden), low), shape((d_rows // 2, hidden), low), shape((8, width), full), shape((cols, width), low),
         ],
-        in_specs=[hbm] * 3 + [vmem] + [hbm] * 5,
-        out_specs=[hbm] * 6 + [vmem] * 2,
+        in_specs=[hbm] * 9,
+        out_specs=[hbm] * 8,
         scratch_shapes=[
-            room((total, cols), low), room(w_out.shape, low), room((own, width), low), room(w_up.shape, low),
+            room((total, cols), low), room(w_out.shape, low), room((own, width), low), room(gain.shape, full),
+            room((8, width), full), room((cols, width), low), room(w_up.shape, low),
             room(w_down.shape, low), room((own, width), low), room((own, width), low), room(place.shape, low),
             room((total, width), low), room((total, cols), low), room((own, width), full), room((slots, width), low),
-            room((d_rows, hidden), low), dma((8,)), dma((6,)),
+            room((d_rows, hidden), low), dma((9,)), dma((8,)),
             room((total, width), low), room((total, width), low),
             room((total, hidden), low), room((total, hidden), low),
             room((own, width), full), room((2, own, width), full),
@@ -744,17 +770,106 @@
     )(merged, w_out, tokens, gain, w_up, w_down, grad_own, grad_across, place)
 
 
+def direct_fits(rows, chunks, dp_count):
+    return dp_count % 2 == 0 and rows % (16 * chunks * dp_count) == 0
+
+
+def direct_steps(dp_count, chunks, acc, came, send, recv, out, out_hbm, keep_sem):
+    dp, mp = lax.axis_index("dp"), lax.axis_index("mp")
+    chunk = acc.shape[0] // chunks
+    group = dp_count // 2
+    half, slot = chunk // 2, chunk // dp_count
+    y, z = lax.rem(dp, 2), dp // 2
+    beside = (dp + 1 - 2 * y, mp)
+    others = sorted(range(1, group), key=lambda j: -min(j, group - j))
+
+    def span(start, size):
+        return pl.ds(pl.multiple_of(start, 16), size)
+
+    def low(k, side, g=0):
+        return k * chunk + side * half + g * slot
+
+    def member(j):
+        return lax.rem(z + j, group)
+
+    def slot_of(k, j):
+        return span(k * chunk + half + (j - 1) * slot, slot)
+
+    def halve(k):
+        return remote(acc.at[span(low(k, 1 - y), half)], came.at[span(k * chunk, half)], send.at[k, 0], recv.at[k, 0], beside)
+
+    def scatter(k, j):
+        piece = acc.at[span(low(k, y, member(j)), slot)]
+        return remote(piece, came.at[slot_of(k, j)], send.at[k, j], recv.at[k, j], (y + 2 * member(j), mp))
+
+    def gather(k, j, mine=True):
+        rows = out.at[span(low(k, y, z if mine else member(group - j)), slot)]
+        return remote(rows, rows, send.at[k, group + j - 1], recv.at[k, group + j - 1], (y + 2 * member(j), mp))
+
+    def double(k, mine=True):
+        rows = span(low(k, y if mine else 1 - y), half)
+        return remote(out.at[rows], out_hbm.at[rows], send.at[k, 2 * group - 1], recv.at[k, 2 * group - 1], beside)
+
+    def keep(k):
+        rows = span(low(k, y), half)
+        return pltpu.make_async_copy(out.at[rows], out_hbm.at[rows], keep_sem.at[k])
+
+    def step(k, i):
+        if i == 0:
+            halve(k).start()
+        elif i == 1:
+            halve(k).wait_recv()
+            rows = span(low(k, y), half)
+            total = acc[rows, :].astype(jnp.float32) + came[span(k * chunk, half), :].astype(jnp.float32)
+            acc[rows, :] = total.astype(jnp.bfloat16)
+            for j in others:
+                scatter(k, j).start()
+        elif i == 2:
+            rows = span(low(k, y, z), slot)
+            total = acc[rows, :].astype(jnp.float32)
+            for j in others:
+                scatter(k, j).wait_recv()
+                total = total + came[slot_of(k, j), :].astype(jnp.float32)
+            out[rows, :] = total.astype(jnp.bfloat16)
+            for j in others:
+                gather(k, j).start()
+        elif i == 3:
+            for j in others:
+                gather(k, j, False).wait_recv()
+            double(k).start()
+            keep(k).start()
+        else:
+            double(k, False).wait_recv()
+
+    def drain():
+        for k in range(chunks):
+            halve(k).wait_send()
+            for j in others:
+                scatter(k, j).wait_send()
+                gather(k, j).wait_send()
+            double(k).wait_send()
+            keep(k).wait()
+
+    return step, drain
+
+
 def last_kernel(
-    dp_count, stages, dq_ref, dk_ref, dv_ref, w_hbm, rows_hbm, grad_residual_hbm, tokens_hbm, gain_ref, gain_part_ref, d_out_ref,
-    grad_tokens_ref, d_sum_ref, gains_ref,
-    w_ref, rows_ref, grad_residual_ref, tokens_ref, load_sem, mine, bufs, gain_mine, gain_came, sum_send, sum_recv, gain_send, gain_recv, acc, came, dp_send, dp_recv,
+    dp_count, fits, dq_hbm, dk_hbm, dv_hbm, w_hbm, rows_hbm, grad_residual_hbm, tokens_hbm, gain_hbm, gain_part_hbm, d_out_hbm,
+    grad_tokens_hbm, d_sum_hbm, gains_hbm,
+    dq_ref, dk_ref, dv_ref, w_ref, rows_ref, grad_residual_ref, tokens_ref, gain_ref, gain_part_ref, d_out_ref,
+    grad_tokens_ref, gains_ref, load_sem, store_sem, mine, bufs, gain_dp, gain_mp,
+    sum_send, sum_recv, dp_gain_send, dp_gain_recv, mp_gain_send, mp_gain_recv, acc, came, out, dp_send, dp_recv, keep_sem,
 ):
-    load_w = pltpu.make_async_copy(w_hbm, w_ref, load_sem.at[0])
-    load_rows = pltpu.make_async_copy(rows_hbm, rows_ref, load_sem.at[1])
-    load_residual = pltpu.make_async_copy(grad_residual_hbm, grad_residual_ref, load_sem.at[2])
-    load_tokens = pltpu.make_async_copy(tokens_hbm, tokens_ref, load_sem.at[3])
-    for load in (load_w, load_rows, load_residual, load_tokens):
+    loads = local_copies(
+        (
+            (dq_hbm, dq_ref), (rows_hbm, rows_ref), (w_hbm, w_ref), (d_out_hbm, d_out_ref), (dk_hbm, dk_ref), (dv_hbm, dv_ref),
+            (gain_hbm, gain_ref), (gain_part_hbm, gain_part_ref), (grad_residual_hbm, grad_residual_ref), (tokens_hbm, tokens_ref),
+        ),
+        load_sem,
+    )
+    for load in loads:
         load.start()
+    store_tokens, store_gains = local_copies(((grad_tokens_ref, grad_tokens_hbm), (gains_ref, gains_hbm)), store_sem)
     low, full = jnp.bfloat16, jnp.float32
     dp, mp = lax.axis_index("dp"), lax.axis_index("mp")
     pair, across, far = mp ^ 1, mp ^ 2, mp ^ 3
@@ -762,21 +877,14 @@
     part = own // PARTS
     cols = dq_ref.shape[1]
     to_pair, to_across = (dp, pair), (dp, across)
-    links = [to_pair, to_across] + [(dp ^ (1 << j), mp) for j in range(dp_count.bit_length() - 1)]
-    greet(links)
-    add_step, add_drain = sum_steps(stages, QKV_CHUNKS, acc, came, dp_send, dp_recv, d_sum_ref)
-    target = acc if stages else d_sum_ref
-    chunk = target.shape[0] // QKV_CHUNKS
+    greet([to_pair, to_across, (dp, far)] + [(lax.rem(dp + k, dp_count), mp) for k in range(1, dp_count)])
+    add_step, add_drain = direct_steps(dp_count, QKV_CHUNKS, acc, came, dp_send, dp_recv, out, d_sum_hbm, keep_sem)
     FAR, ACROSS, PAIR = 0, 1, 2
 
     def add(*steps):
-        if stages:
+        if fits:
             for k, i in steps:
-                if 0 <= k < QKV_CHUNKS:
-                    add_step(k, i)
-
-    def tick(t):
-        add(*[(t - i, i) for i in range(2 * stages, 0, -1)])
+                add_step(k, i)
 
     def piece(c):
         return pl.ds(pl.multiple_of(c * part, part), part)
@@ -801,49 +909,63 @@
         total = total + jnp.dot(dk_ref[where, :], w_ref[1], preferred_element_type=full)
         return total + jnp.dot(dv_ref[where, :], w_ref[2], preferred_element_type=full)
 
-    def ready(low_row, high_row):
-        add(*[(k, 0) for k in range(QKV_CHUNKS) if low_row < (k + 1) * chunk <= high_row])
-
-    target[0:cols, :] = d_out_ref[...]
-    ready(0, cols)
-
-    def weight_grad(p, ref, gain_row):
+    def weight_grad(p, ref):
         grad = lax.dot_general(ref[...], rows_ref[...], TN, preferred_element_type=full)
-        target[(p + 1) * cols:(p + 2) * cols, :] = grad.astype(low)
-        ready((p + 1) * cols, (p + 2) * cols)
-        return gain_row + jnp.sum(grad * w_ref[p].astype(full), axis=0, keepdims=True)
-
-    load_w.wait()
+        acc[(p + 1) * cols:(p + 2) * cols, :] = grad.astype(low)
+        return jnp.sum(grad * w_ref[p].astype(full), axis=0, keepdims=True)
+
+    for load in loads[:4]:
+        load.wait()
+    acc[0:cols, :] = d_out_ref[...]
+    gain_row = weight_grad(0, dq_ref)
+    add((0, 0))
+    for load in loads[4:]:
+        load.wait()
     bufs[0, FAR] = in_part(far).astype(low)
     each(PARTS, lambda c: sum_copy(FAR, c).start())
-    load_rows.wait()
-    gain_row = weight_grad(0, dq_ref, jnp.zeros((1, width), full))
+    gain_row = gain_row + weight_grad(1, dk_ref)
+    add((1, 0))
     mine[...] = in_part(across)
 
     def pass_across(c):
         bufs[0, ACROSS, piece(c), :] = (mine[piece(c), :] + arrived(FAR, c)).astype(low)
         sum_copy(ACROSS, c).start()
     each(PARTS, pass_across)
-    gain_row = weight_grad(1, dk_ref, gain_row)
-    gain_row = weight_grad(2, dv_ref, gain_row)
+    gain_row = gain_row + weight_grad(2, dv_ref)
+    add((2, 0))
+
+    row = lax.broadcasted_iota(jnp.int32, (8, width), 0)
+    gain_dp[dp] = jnp.where(row == 0, gain_part_ref[...], jnp.where(row == 1, gain_row / gain_ref[0:1, :], 0.0))
+
+    def gain_over_dp(k, owner):
+        return remote(gain_dp.at[owner], gain_dp.at[owner], dp_gain_send.at[k], dp_gain_recv.at[k], (lax.rem(dp + k, dp_count), mp))
+
+    def gain_over_mp(i, owner):
+        other = (pair, across, far)[i]
+        return remote(gain_mp.at[owner], gain_mp.at[owner], mp_gain_send.at[i], mp_gain_recv.at[i], (dp, other))
+
+    for k in range(1, dp_count):
+        gain_over_dp(k, dp).start()
+
+    def turn_gains():
+        for k in range(1, dp_count):
+            gain_over_dp(k, lax.rem(dp + dp_count - k, dp_count)).wait_recv()
+        total = gain_dp[0]
+        for k in range(1, dp_count):
+            total = total + gain_dp[k]
+        gain_mp[mp] = total
+        for i in range(3):
+            gain_over_mp(i, mp).start()
+
+    def end_gains():
+        for i, owner in enumerate((pair, across, far)):
+            gain_over_mp(i, owner).wait_recv()
+        gains_ref[...] = (gain_mp[0] + gain_mp[1]) + (gain_mp[2] + gain_mp[3])
+        store_gains.start()
+
     bufs[0, PAIR] = in_part(pair).astype(low)
     each(PARTS, lambda c: sum_copy(PAIR, c).start())
-
-    def gain_copy(i):
-        return remote(gain_mine.at[i], gain_came.at[i], gain_send.at[i], gain_recv.at[i], links[i])
-
-    def gain_step(i):
-        gain_copy(i).wait_recv()
-        gain_mine[i + 1] = gain_mine[i] + gain_came[i]
-        if i + 1 < len(links):
-            gain_copy(i + 1).start()
-
-    row = lax.broadcasted_iota(jnp.int32, (8, width), 0)
-    gain_mine[0] = jnp.where(row == 0, gain_part_ref[...], jnp.where(row == 1, gain_row / gain_ref[0:1, :], 0.0))
-    gain_copy(0).start()
     mine[...] = in_part(mp)
-    load_residual.wait()
-    load_tokens.wait()
 
     def back_norm(c):
         grad = mine[piece(c), :] + arrived(PAIR, c) + arrived(ACROSS, c)
@@ -854,58 +976,69 @@
         total = inverse * (scaled - first_mean - unit * second_mean) + grad_residual_ref[piece(c), :]
         grad_tokens_ref[piece(c), :] = total.astype(low)
 
-    for t in range(1, QKV_CHUNKS + 2 * stages if stages else 1):
-        tick(t)
-        for c, when in enumerate(NORM_TICKS):
-            if t == when:
-                each(1, lambda i: back_norm(i + c))
-        if 2 <= t < 2 + len(links):
-            gain_step(t - 2)
-    if not stages:
-        each(PARTS, back_norm)
-        for i in range(len(links)):
-            gain_step(i)
-    gains_ref[...] = gain_mine[len(links)]
-    if stages:
+    def norm(c):
+        each(1, lambda i: back_norm(i + c))
+
+    add((0, 1))
+    norm(0)
+    add((1, 1), (0, 2))
+    norm(1)
+    add((2, 1), (1, 2), (0, 3))
+    norm(2)
+    turn_gains()
+    add((2, 2), (1, 3))
+    norm(3)
+    store_tokens.start()
+    add((0, 4), (2, 3))
+    end_gains()
+    add((1, 4), (2, 4))
+    if fits:
         add_drain()
-    for i in range(len(links)):
-        gain_copy(i).wait_send()
+    else:
+        whole = pltpu.make_async_copy(acc, d_sum_hbm, keep_sem.at[0])
+        whole.start()
+        whole.wait()
+    for k in range(1, dp_count):
+        gain_over_dp(k, dp).wait_send()
+    for i in range(3):
+        gain_over_mp(i, mp).wait_send()
 
     def drain(c):
         for kind in range(3):
             sum_copy(kind, c).wait_send()
     each(PARTS, drain)
+    store_tokens.wait()
+    store_gains.wait()
 
 
 def last(dp_count, dq, dk, dv, w_qkv, rows, grad_residual, tokens, gain, gain_part, d_out):
     own, width = tokens.shape
     cols = dq.shape[1]
     d_rows = 4 * cols
-    stages = sum_stages(d_rows, QKV_CHUNKS, dp_count)
+    fits = direct_fits(d_rows, QKV_CHUNKS, dp_count)
     low, full = jnp.bfloat16, jnp.float32
-    count = 2 + dp_count.bit_length() - 1
-    hbm = pl.BlockSpec(memory_space=pltpu.HBM)
-    vmem = pl.BlockSpec(memory_space=pltpu.VMEM)
+    hbm = pl.BlockSpec(memory_space=pl.ANY)
     dma = pltpu.SemaphoreType.DMA
-    shape = jax.ShapeDtypeStruct
+    shape, room = jax.ShapeDtypeStruct, pltpu.VMEM
+    operands = (dq, dk, dv, w_qkv, rows, grad_residual, tokens, gain, gain_part, d_out)
     grad_tokens, d_sum, gains = pl.pallas_call(
-        functools.partial(last_kernel, dp_count, stages),
+        functools.partial(last_kernel, dp_count, fits),
         out_shape=[shape((own, width), low), shape((d_rows, width), low), shape((8, width), full)],
-        in_specs=[vmem] * 3 + [hbm] * 4 + [vmem] * 3,
-        out_specs=[vmem] * 3,
-        scratch_shapes=[
-            pltpu.VMEM(w_qkv.shape, low), pltpu.VMEM(rows.shape, low), pltpu.VMEM((own, width), full),
-            pltpu.VMEM((own, width), low), dma((4,)),
-            pltpu.VMEM((own, width), full), pltpu.VMEM((2, 3, own, width), low),
-            pltpu.VMEM((count + 1, 8, width), full), pltpu.VMEM((count, 8, width), full),
-            dma((3, PARTS)), dma((3, PARTS)), dma((count,)), dma((count,)),
-        ]
-        + sum_scratch(d_rows, width, QKV_CHUNKS, stages),
+        in_specs=[hbm] * 10,
+        out_specs=[hbm] * 3,
+        scratch_shapes=[room(one.shape, one.dtype) for one in operands]
+        + [
+            room((own, width), low), room((8, width), full), dma((10,)), dma((2,)),
+            room((own, width), full), room((2, 3, own, width), low), room((dp_count, 8, width), full), room((4, 8, width), full),
+            dma((3, PARTS)), dma((3, PARTS)), dma((dp_count,)), dma((dp_count,)), dma((3,)), dma((3,)),
+            room((d_rows, width), low), room((d_rows, width), low), room((d_rows, width), low),
+            dma((QKV_CHUNKS, dp_count)), dma((QKV_CHUNKS, dp_count)), dma((QKV_CHUNKS,)),
+        ],
         compiler_params=pltpu.CompilerParams(collective_id=3, has_side_effects=True, vmem_limit_bytes=VMEM_BYTES),
         cost_estimate=pl.CostEstimate(flops=12 * 4 * own * width * cols, bytes_accessed=20 * own * width, transcendentals=0),
         name="last",
-    )(dq, dk, dv, w_qkv, rows, grad_residual, tokens, gain, gain_part, d_out)
-    return grad_tokens, d_sum if stages else lax.psum(d_sum, "dp"), gains
+    )(*operands)
+    return grad_tokens, d_sum if fits else lax.psum(d_sum, "dp"), gains
 
 
 def local(
@@ -930,20 +1063,23 @@
         size = width // MLP_CHUNKS
         place_y = lax.rem(lax.axis_index("dp"), 2) == 0
         place_z = lax.rem(lax.axis_index("dp") // 2, 2) == 0
-        count = sum(left_bit(k, MLP_CHUNKS) == 0 for k in range(MLP_CHUNKS))
         first_came = lax.ppermute(first, "dp", [(i, i ^ 1) for i in range(dp_count)])
         second_came = lax.ppermute(second, "dp", [(i, i ^ 2) for i in range(dp_count)])
         gain_part, first_came, second_came = lax.optimization_barrier((gain_part, first_came, second_came))
-        first = [jnp.where(place_y, first, first_came), jnp.where(place_y, first_came, first)]
+        first = [
+            one.reshape(-1, size, width)
+            for one in (jnp.where(place_y, first, first_came), jnp.where(place_y, first_came, first))
+        ]
         second = jnp.stack(
             [
-                one.reshape(MLP_CHUNKS - count, 2, size // 2, width)
+                one.reshape(-1, 2, size // 2, width)
                 for one in (jnp.where(place_z, second, second_came), jnp.where(place_z, second_came, second))
             ],
             axis=2,
         )
         up_sum, down_sum = (
-            jnp.concatenate([first[i], second[:, i].reshape(-1, width)]).astype(full) for i in range(2)
+            jnp.stack([first[i], second[:, i].reshape(-1, size, width)], axis=1).reshape(-1, width).astype(full)
+            for i in range(2)
         )
     else:
         d_sum = lax.psum(jnp.concatenate([first, second]), "dp").reshape(MLP_CHUNKS, 2, -1, width).astype(full)

time: 279 us -> 263 us (0.943)
  Pallas kernels: 256 us -> 238 us
  local copies, waits for them, and re-layouts: 6.83 us -> 10.7 us
  other arithmetic: 7.19 us -> 4.35 us
    pallas_call x1, Pallas kernels: 63.4 us -> 47.7 us  [last(): pl.pallas_call(functools.partial(last_kernel, dp_count, fits), out_shape=...]
    pallas_call x1, Pallas kernels: 110 us -> 98.2 us  [middle(): pl.pallas_call(functools.partial(middle_kernel, stages), out_shape=[shape...]
    pallas_call x1, Pallas kernels: 31 us -> 37.6 us  [attend_backward(): pl.pallas_call(functools.partial(bwd_kernel, n, heads), grid_spec=pltpu.P...]
    pallas_call x1, Pallas kernels: 20.9 us -> 25.1 us  [attend_forward(): pl.pallas_call(functools.partial(fwd_kernel, n, heads), grid_spec=pltpu.P...]
    convert_element_type x0 -> x2, local copies, waits for them, and re-layouts: none -> 3.32 us  [local(): jnp.stack([first[i], second[:, i].reshape(-1, size, width)], axis=1)]
    convert_element_type x2, other arithmetic: 3.15 us -> 0.31 us  [local(): jnp.stack([first[i], second[:, i].reshape(-1, size, width)], axis=1)]
  transfers between devices with their start and end apart: 4 -> 4, of which waited for: 0 -> 0; matrix products, arithmetic and copies ran while one was open for 3% -> 4% of each run, Pallas kernels for 41% -> 42%
where the time goes in v6:
time: 263 us
  Pallas kernels  238 us (90%)
  local copies, waits for them, and re-layouts  10.7 us (4%)
  starting transfers between devices  9.31 us (4%)
  other arithmetic  4.35 us (2%)
    pallas_call x1, Pallas kernels, middle(): pl.pallas_call(functools.partial(middle_kernel, stages), out_shape=[shape...  98.2 us
    pallas_call x1, Pallas kernels, last(): pl.pallas_call(functools.partial(last_kernel, dp_count, fits), out_shape=...  47.7 us
    pallas_call x1, Pallas kernels, attend_backward(): pl.pallas_call(functools.partial(bwd_kernel, n, heads), grid_spec=pltpu.P...  37.6 us
    pallas_call x1, Pallas kernels, project(): pl.pallas_call(functools.partial(project_kernel, dp_count), out_shape=[ja...  29.3 us
    pallas_call x1, Pallas kernels, attend_forward(): pl.pallas_call(functools.partial(fwd_kernel, n, heads), grid_spec=pltpu.P...  25.1 us
  transfers between devices with their start and end apart: 4, of which 0 were waited for; matrix products, arithmetic and copies ran while one was open for 4% of the time, Pallas kernels for 42%

profile of v6, /device:TPU:0, one launch (start us, length us, event | category | flops | bytes accessed | tf_op | source)
XLA Modules:
  0.0 262.9 jit_solution(14781182509817677830)
XLA Ops:
  0.6 0.7 stack.19
  1.3 0.7 stack.18
  2.0 0.6 pad_maximum_fusion.1.gain_hbm
  2.6 29.3 %project.1 = (bf16[2048,768]{1,0:T(8,128)(2,1)}, bf16[2048,192]{1,0:T(8,128)(2,1)}, bf16[2048,192]{1,0:T(8,128)(2,1)}, bf16[2048,192]{1,0:T(8,128)(2,1)}, bf16[5...) custom-call(bf16[512,768]{1,0:T(8,128)(2,1)} %tokens_hbm.5, f32[2,768]{1,0:T(2,128)} %pad_maximum_fusion.1.gain_hbm, ...), custom_call_target="tpu_custom_call" | custom-call | flops 1811939328 | bytes 15728640 | tf_op jit(solution)/shard_map/project/pallas_call | solution.py:452
  31.9 0.6 collective-permute-start
  32.6 25.1 %attend_forward.1 = (bf16[2048,192]{1,0:T(8,128)(2,1)}, f32[8,2048]{1,0:T(8,128)}) custom-call(s32[2048]{0:T(1024)} %bitcast.32, s32[1,2048]{1,0:T(1,128)} %segv_ref.3, bf16[2048,192]{1,0:T(8,128)(2,1)} %get-tuple-element.32.q_ref, bf16[2048,192]{1,0:T(8,128)(2,1)} %get-tuple-element.33.k_ref, bf16[2048,192]{1,0:T(8,128)(2,1)} %get-tuple-element.34.v_ref), custom_call_target="tpu_custom_call" | custom-call | flops 3221225472 | bytes 3145728 | tf_op jit(solution)/shard_map/attend_forward/pallas_call | solution.py:103
  57.7 0.9 copy-done.3
  58.5 98.2 %middle.1 = (bf16[2048,768]{1,0:T(8,128)(2,1)}, bf16[2048,192]{1,0:T(8,128)(2,1)}, f32[512,768]{1,0:T(8,128)}, bf16[640,768]{1,0:T(8,128)(2,1)}, bf16[384,768]{1...) custom-call(bf16[2048,192]{1,0:T(8,128)(2,1)} %get-tuple-element.35.merged_hbm.o_ref, ...), custom_call_target="tpu_custom_call" | custom-call | flops 19327352832 | bytes 31457280 | tf_op jit(solution)/shard_map/middle/pallas_call | solution.py:746
  156.7 5.2 %all-to-all-start = ((bf16[8,80,768]{2,1,0:T(8,128)(2,1)}), bf16[8,80,768]{2,1,0:T(8,128)(2,1)S(1)}, u32[]{:S(2)}, u32[]{:S(2)}) async-start(bf16[8,80,768]{2,1,0:T(8,128)(2,1)} %bitcast.28), calls=%async_computation | async-start | bytes 1966080 | tf_op jit(solution)/shard_map/all_to_all | solution.py:1087
  161.9 2.0 collective-permute-start.1
  163.9 1.5 collective-permute-start.2
  165.4 37.6 %attend_backward.1 = (bf16[2048,192]{1,0:T(8,128)(2,1)}, bf16[2048,192]{1,0:T(8,128)(2,1)}, bf16[2048,192]{1,0:T(8,128)(2,1)}) custom-call(s32[2048]{0:T(1024)} %bitcast.33, s32[1,2048]{1,0:T(1,128)} %segv_ref.3, bf16[2048,192]{1,0:T(8,128)(2,1)} %get-tuple-element.32.q_ref, bf16[2048,192]{1,0:T(8,128)(2,1)} %get-tuple-element.33.k_ref, ...), custom_call_target="tpu_custom_call" | custom-call | flops 8053063680 | bytes 6291456 | tf_op jit(solution)/shard_map/attend_backward/pallas_call | solution.py:183
  203.0 47.7 %last.1 = (bf16[512,768]{1,0:T(8,128)(2,1)}, bf16[768,768]{1,0:T(8,128)(2,1)}, f32[8,768]{1,0:T(8,128)}) custom-call(bf16[2048,192]{1,0:T(8,128)(2,1)} %get-tuple-element.41.dq_hbm, bf16[2048,192]{1,0:T(8,128)(2,1)} %get-tuple-element.42.dk_hbm, bf16[2048,192]{1,0:T(8,128)(2,1)} %get-tuple-element.43.dv_hbm, bf16[3,192,768]{2,1,0:T(8,128)(2,1)} %bitcast.31, ...), custom_call_target="tpu_custom_call" | custom-call | flops 3623878656 | bytes 7864320 | tf_op jit(solution)/shard_map/last/pallas_call | solution.py:1024
  250.7 1.2 slice.18
  252.0 0.2 broadcast_select_fusion
  252.3 0.2 maximum_convert_fusion
  252.5 1.7 copy.24
  254.3 1.7 copy.25
  256.0 1.4 slice_reduce_fusion
  257.4 1.8 slice_convert_fusion
  259.2 1.4 convert_bitcast_fusion
  260.6 0.9 copy.31
  261.5 0.5 copy-done
  262.1 0.9 copy.32
  (14 shorter events, 0.4 us)
Async XLA Ops:
  31.9 25.7 %collective-permute-start = (bf16[512,768]{1,0:T(8,128)(2,1)}, bf16[512,768]{1,0:T(8,128)(2,1)S(1)}, u32[]{:S(2)}, u32[]{:S(2)}) collective-permute-start(bf16[512,768]{1,0:T(8,128)(2,1)} %get-tuple-element.36.grad_own_hbm), channel_id=1, source_target_pairs={{0,2},{1,3},{2,0},{3,1},{4,6},{5,7},{6,4},{7,5},{8,10},{9,11},{10,... | collective-permute-start | bytes 2359304 | tf_op jit(solution)/shard_map/ppermute | solution.py:1056
  57.6 0.9 copy-start.3
  156.7 5.2 %copy-start.1 = (bf16[384,768]{1,0:T(8,128)(2,1)S(1)}, bf16[384,768]{1,0:T(8,128)(2,1)}, u32[]{:S(2)}) copy-start(bf16[384,768]{1,0:T(8,128)(2,1)} %get-tuple-element.47) | copy-start | bytes 1769476
  156.7 7.2 %copy-start.2 = (bf16[384,768]{1,0:T(8,128)(2,1)S(1)}, bf16[384,768]{1,0:T(8,128)(2,1)}, u32[]{:S(2)}) copy-start(bf16[384,768]{1,0:T(8,128)(2,1)} %get-tuple-element.48) | copy-start | bytes 1769476
  156.7 103.9 %all-to-all-start = ((bf16[8,80,768]{2,1,0:T(8,128)(2,1)}), bf16[8,80,768]{2,1,0:T(8,128)(2,1)S(1)}, u32[]{:S(2)}, u32[]{:S(2)}) async-start(bf16[8,80,768]{2,1,0:T(8,128)(2,1)} %bitcast.28), calls=%async_computation | async-start | bytes 1966080 | tf_op jit(solution)/shard_map/all_to_all | solution.py:1087
  161.9 41.1 %collective-permute-start.1 = (bf16[384,768]{1,0:T(8,128)(2,1)S(1)}, bf16[384,768]{1,0:T(8,128)(2,1)S(1)}, u32[]{:S(2)}, u32[]{:S(2)}) collective-permute-start(bf16[384,768]{1,0:T(8,128)(2,1)S(1)} %copy-done.1), channel_id=1, source_target_pairs={{0,4},{4,0},{8,12},{12,8},{16,20},{20,16},{24,28},{28,24},{1,5},{5... | collective-permute-start | bytes 1769480 | tf_op jit(solution)/shard_map/ppermute | solution.py:1066
  163.9 39.0 %collective-permute-start.2 = (bf16[384,768]{1,0:T(8,128)(2,1)S(1)}, bf16[384,768]{1,0:T(8,128)(2,1)S(1)}, u32[]{:S(2)}, u32[]{:S(2)}) collective-permute-start(bf16[384,768]{1,0:T(8,128)(2,1)S(1)} %copy-done.2), channel_id=1, source_target_pairs={{0,8},{4,12},{8,0},{12,4},{16,24},{20,28},{24,16},{28,20},{1,9},{5... | collective-permute-start | bytes 1769480 | tf_op jit(solution)/shard_map/ppermute | solution.py:1067
  260.6 1.5 copy-start

commit v7 on v6

--- a/solution.py
+++ b/solution.py
@@ -8,7 +8,7 @@
 
 HEAD = 64
 TQ = 256
-TK = 512
+TK = 256
 NT = (((1,), (1,)), ((), ()))
 NN = (((1,), (0,)), ((), ()))
 TN = (((0,), (0,)), ((), ()))
@@ -20,21 +20,30 @@
     return [pltpu.make_async_copy(src, dst, sems.at[i]) for i, (src, dst) in enumerate(pairs)]
 
 
-def lower_bound(seg, n, value):
-    def step(_, c):
-        lo, hi = c
-        mid = (lo + hi) // 2
-        less = seg[jnp.minimum(mid, n - 1)] < value
-        go = lo < hi
-        return (jnp.where(go & less, mid + 1, lo), jnp.where(go & ~less, mid, hi))
-    lo, hi = lax.fori_loop(0, n.bit_length(), step, (jnp.int32(0), jnp.int32(n)))
-    return lo
-
-
-def key_range(seg, n, tile):
-    first = lower_bound(seg, n, seg[tile * TQ])
-    end = lower_bound(seg, n, seg[tile * TQ + TQ - 1] + 1)
-    return first // TK, (end + TK - 1) // TK
+def key_ranges(seg, tiles):
+    n = seg.shape[1]
+    lane = lax.broadcasted_iota(jnp.int32, (tiles, n), 1)
+    row = lax.broadcasted_iota(jnp.int32, (tiles, n), 0)
+    ids = jnp.broadcast_to(seg.astype(jnp.float32), (tiles, n))
+
+    def total(mask, values):
+        return jnp.sum(jnp.where(mask, values, 0.0), axis=1, keepdims=True)
+
+    first = total(lane == row * TQ, ids)
+    last = total(lane == row * TQ + TQ - 1, ids)
+    start = jnp.floor(total(ids < first, 1.0) * (1.0 / TK))
+    end = jnp.floor((total(ids <= last, 1.0) + (TK - 1.0)) * (1.0 / TK))
+    lane = lax.broadcasted_iota(jnp.int32, (tiles, 128), 1)
+    return jnp.where(lane == 0, start, jnp.where(lane == 1, end, 0.0)).astype(jnp.int32)
+
+
+def over_blocks(ranges, tile, body, state):
+    lo, hi = ranges[tile, 0], ranges[tile, 1]
+    pairs = (hi - lo) // 2
+    state = lax.fori_loop(
+        0, pairs, lambda i, one: body(pl.multiple_of((lo + 2 * i) * TK, TK), 2 * TK, one), state
+    )
+    return lax.fori_loop(lo + 2 * pairs, hi, lambda i, one: body(pl.multiple_of(i * TK, TK), TK, one), state)
 
 
 def head_masks(width, heads):
@@ -48,7 +57,7 @@
         cols[t * 128:(t + 1) * 128, :] = jnp.broadcast_to(row, (128, 128)).T
 
 
-def fwd_kernel(n, heads, seg, segv_ref, q_ref, k_ref, v_ref, o_ref, lse_ref, vt, cols, scores):
+def fwd_kernel(n, heads, ranges, segv_ref, q_ref, k_ref, v_ref, o_ref, lse_ref, vt, cols, scores):
     tile = pl.program_id(0)
     width = heads * HEAD
 
@@ -58,45 +67,42 @@
         for t in range(n // TK):
             vt[:, t * TK:(t + 1) * TK] = v_ref[t * TK:(t + 1) * TK, :].astype(jnp.float32).T.astype(jnp.bfloat16)
 
-    lo, hi = key_range(seg, n, tile)
     q0 = pl.multiple_of(tile * TQ, TQ)
     q = q_ref[...] * jnp.bfloat16(HEAD ** -0.5)
     masks = head_masks(width, heads)
     qm = [jnp.where(m, q, jnp.bfloat16(0)) for m in masks]
     seg_row = segv_ref[0:1, pl.ds(q0, TQ)].astype(jnp.float32)
 
-    def first(b, tops):
-        k0 = pl.multiple_of(b * TK, TK)
-        keys = k_ref[pl.ds(k0, TK), :]
-        col = cols[pl.ds(k0, TK), :]
+    def first(k0, size, tops):
+        keys = k_ref[pl.ds(k0, size), :]
+        col = cols[pl.ds(k0, size), :]
         same = jnp.concatenate([col] * (TQ // 128), axis=1) == seg_row
         out = []
         for h in range(heads):
             s = lax.dot_general(keys, qm[h], NT, preferred_element_type=jnp.float32)
             s = jnp.where(same, s, MASKED)
-            scores[h, pl.ds(k0, TK), :] = s
+            scores[h, pl.ds(k0, size), :] = s
             out.append(jnp.maximum(tops[h], jnp.max(s, axis=0, keepdims=True)))
         return tuple(out)
 
-    tops = lax.fori_loop(lo, hi, first, tuple(jnp.full((1, TQ), MASKED, jnp.float32) for _ in range(heads)))
-
-    def second(b, acc):
-        k0 = pl.multiple_of(b * TK, TK)
+    tops = over_blocks(ranges, tile, first, tuple(jnp.full((1, TQ), MASKED, jnp.float32) for _ in range(heads)))
+
+    def second(k0, size, acc):
         out = []
         for h in range(heads):
-            p = jnp.exp(scores[h, pl.ds(k0, TK), :] - tops[h])
+            p = jnp.exp(scores[h, pl.ds(k0, size), :] - tops[h])
             total = acc[h][1] + jnp.sum(p, axis=0, keepdims=True)
-            part = lax.dot_general(vt[h * HEAD:(h + 1) * HEAD, pl.ds(k0, TK)], p.astype(jnp.bfloat16), NN, preferred_element_type=jnp.float32)
+            part = lax.dot_general(vt[h * HEAD:(h + 1) * HEAD, pl.ds(k0, size)], p.astype(jnp.bfloat16), NN, preferred_element_type=jnp.float32)
             out.append((acc[h][0] + part, total))
         return tuple(out)
 
-    acc = lax.fori_loop(lo, hi, second, tuple((jnp.zeros((HEAD, TQ), jnp.float32), jnp.zeros((1, TQ), jnp.float32)) for _ in range(heads)))
+    acc = over_blocks(ranges, tile, second, tuple((jnp.zeros((HEAD, TQ), jnp.float32), jnp.zeros((1, TQ), jnp.float32)) for _ in range(heads)))
     ot = jnp.concatenate([acc[h][0] / acc[h][1] for h in range(heads)], axis=0)
     o_ref[...] = ot.T.astype(jnp.bfloat16)
     lse_ref[...] = jnp.concatenate([tops[h] + jnp.log(acc[h][1]) for h in range(heads)] + [jnp.zeros((8 - heads, TQ), jnp.float32)], axis=0)
 
 
-def attend_forward(seg, q, k, v):
+def attend_forward(ranges, seg, q, k, v):
     n, width = q.shape
     heads = width // HEAD
     whole = pl.BlockSpec(memory_space=pltpu.VMEM)
@@ -113,10 +119,10 @@
         compiler_params=pltpu.CompilerParams(vmem_limit_bytes=VMEM_BYTES),
         cost_estimate=pl.CostEstimate(flops=4 * heads * n * n * HEAD, bytes_accessed=8 * n * width, transcendentals=heads * n * n // 2),
         name="attend_forward",
-    )(seg.reshape(-1), seg.reshape(1, -1), q, k, v)
-
-
-def bwd_kernel(n, heads, seg, segv_ref, q_ref, k_ref, v_ref, o_ref, do_ref, lse_ref, dq_ref, dk_ref, dv_ref, kt, cols, dk_acc, dv_acc):
+    )(ranges, seg, q, k, v)
+
+
+def bwd_kernel(n, heads, ranges, segv_ref, q_ref, k_ref, v_ref, o_ref, do_ref, lse_ref, dq_ref, dk_ref, dv_ref, kt, cols, dk_acc, dv_acc):
     tile = pl.program_id(0)
     width = heads * HEAD
 
@@ -128,7 +134,6 @@
         dk_acc[...] = jnp.zeros_like(dk_acc)
         dv_acc[...] = jnp.zeros_like(dv_acc)
 
-    lo, hi = key_range(seg, n, tile)
     q0 = pl.multiple_of(tile * TQ, TQ)
     masks = head_masks(width, heads)
     q = q_ref[...] * jnp.bfloat16(HEAD ** -0.5)
@@ -145,15 +150,14 @@
     delta = lax.dot_general(pick, high, NT, preferred_element_type=jnp.float32) + lax.dot_general(pick, rest, NT, preferred_element_type=jnp.float32)
     lse = lse_ref[...]
 
-    def body(b, acc):
-        k0 = pl.multiple_of(b * TK, TK)
-        keys = k_ref[pl.ds(k0, TK), :]
-        vals = v_ref[pl.ds(k0, TK), :]
-        col = cols[pl.ds(k0, TK), :]
+    def body(k0, size, acc):
+        keys = k_ref[pl.ds(k0, size), :]
+        vals = v_ref[pl.ds(k0, size), :]
+        col = cols[pl.ds(k0, size), :]
         same = jnp.concatenate([col] * (TQ // 128), axis=1) == seg_row
         out = []
-        dks = jnp.zeros((TK, width), jnp.float32)
-        dvs = jnp.zeros((TK, width), jnp.float32)
+        dks = jnp.zeros((size, width), jnp.float32)
+        dvs = jnp.zeros((size, width), jnp.float32)
         for h in range(heads):
             s = lax.dot_general(keys, qm[h], NT, preferred_element_type=jnp.float32)
             p = jnp.where(same, jnp.exp(s - lse[h:h + 1, :]), 0.0)
@@ -161,12 +165,12 @@
             ds = (p * (dp - delta[h:h + 1, :])).astype(jnp.bfloat16)
             dvs = dvs + lax.dot_general(p.astype(jnp.bfloat16), dm[h], NN, preferred_element_type=jnp.float32)
             dks = dks + lax.dot_general(ds, qm[h], NN, preferred_element_type=jnp.float32)
-            out.append(acc[h] + lax.dot_general(kt[h * HEAD:(h + 1) * HEAD, pl.ds(k0, TK)], ds, NN, preferred_element_type=jnp.float32))
-        dk_acc[pl.ds(k0, TK), :] += dks
-        dv_acc[pl.ds(k0, TK), :] += dvs
+            out.append(acc[h] + lax.dot_general(kt[h * HEAD:(h + 1) * HEAD, pl.ds(k0, size)], ds, NN, preferred_element_type=jnp.float32))
+        dk_acc[pl.ds(k0, size), :] += dks
+        dv_acc[pl.ds(k0, size), :] += dvs
         return tuple(out)
 
-    acc = lax.fori_loop(lo, hi, body, tuple(jnp.zeros((HEAD, TQ), jnp.float32) for _ in range(heads)))
+    acc = over_blocks(ranges, tile, body, tuple(jnp.zeros((HEAD, TQ), jnp.float32) for _ in range(heads)))
     dq_ref[...] = (jnp.concatenate(acc, axis=0).T * HEAD ** -0.5).astype(jnp.bfloat16)
 
     @pl.when(tile == n // TQ - 1)
@@ -175,7 +179,7 @@
         dv_ref[...] = dv_acc[...].astype(jnp.bfloat16)
 
 
-def attend_backward(seg, q, k, v, o, do, lse):
+def attend_backward(ranges, seg, q, k, v, o, do, lse):
     n, width = q.shape
     heads = width // HEAD
     whole = pl.BlockSpec(memory_space=pltpu.VMEM)
@@ -193,7 +197,7 @@
         compiler_params=pltpu.CompilerParams(vmem_limit_bytes=VMEM_BYTES),
         cost_estimate=pl.CostEstimate(flops=10 * heads * n * n * HEAD, bytes_accessed=16 * n * width, transcendentals=heads * n * n // 2),
         name="attend_backward",
-    )(seg.reshape(-1), seg.reshape(1, -1), q, k, v, o, do, lse)
+    )(ranges, seg, q, k, v, o, do, lse)
 
 
 MESH_ID = pl.DeviceIdType.MESH
@@ -324,11 +328,11 @@
 
 
 def project_kernel(
-    dp_count, tokens_hbm, gain_hbm, w_hbm, cot_ref, owner_hbm, rows_hbm, q_hbm, k_hbm, v_hbm, grad_hbm, place_hbm,
-    tokens_ref, gain_ref, w_ref, owner_ref, rows_ref, q_ref, k_ref, v_ref, grad_ref, place_ref, load_sem, store_sem, out_sem, returned_ref, across_send, across_recv, pair_send, pair_recv, pass_send, pass_recv, slot_send, slot_recv, self_sem,
+    dp_count, tokens_hbm, gain_hbm, w_hbm, cot_ref, owner_hbm, seg_hbm, rows_hbm, q_hbm, k_hbm, v_hbm, grad_hbm, place_hbm, ranges_ref,
+    tokens_ref, gain_ref, w_ref, owner_ref, seg_ref, rows_ref, q_ref, k_ref, v_ref, grad_ref, place_ref, load_sem, store_sem, out_sem, returned_ref, across_send, across_recv, pair_send, pair_recv, pass_send, pass_recv, slot_send, slot_recv, self_sem,
 ):
-    load_tokens, load_gain, load_w, load_owner = loads = local_copies(
-        ((tokens_hbm, tokens_ref), (gain_hbm, gain_ref), (w_hbm, w_ref), (owner_hbm, owner_ref)), load_sem
+    load_tokens, load_gain, load_w, load_owner, load_seg = loads = local_copies(
+        ((tokens_hbm, tokens_ref), (gain_hbm, gain_ref), (w_hbm, w_ref), (owner_hbm, owner_ref), (seg_hbm, seg_ref)), load_sem
     )
     for load in loads:
         load.start()
@@ -365,7 +369,7 @@
     for c in range(PARTS):
         values = tokens_ref[c * part:(c + 1) * part, :].astype(jnp.float32)
         unit, _ = norm_unit(values)
-        rows_ref[spot(mp, c, part), :] = (unit * gain_ref[0:1, :]).astype(jnp.bfloat16)
+        rows_ref[spot(mp, c, part), :] = (unit * gain_ref[...].reshape(1, -1)).astype(jnp.bfloat16)
         gather_copy(c, mp, (dp, across), across_send, across_recv).start()
         gather_copy(c, mp, (dp, pair), pair_send, pair_recv).start()
     def product(owner, half):
@@ -382,7 +386,9 @@
 
     load_w.wait()
     load_owner.wait()
+    load_seg.wait()
     both(mp)
+    ranges_ref[...] = key_ranges(seg_ref[...], ranges_ref.shape[0])
     store(0, mp).start()
     capacity = cot_ref.shape[1]
     owner_row = owner_ref[...].astype(jnp.float32)
@@ -441,7 +447,7 @@
         out.wait()
 
 
-def project(tokens, gain, w_qkv, cot, owners):
+def project(tokens, gain, w_qkv, cot, owners, seg):
     own, width = tokens.shape
     dp_count = cot.shape[0]
     total = own * 4
@@ -453,17 +459,18 @@
         functools.partial(project_kernel, dp_count),
         out_shape=[jax.ShapeDtypeStruct((total, width), jnp.bfloat16)]
         + [jax.ShapeDtypeStruct((total, cols), jnp.bfloat16)] * 3
-        + [jax.ShapeDtypeStruct((own, width), jnp.bfloat16), jax.ShapeDtypeStruct((dp_count * cot.shape[1], own), jnp.bfloat16)],
-        in_specs=[hbm] * 5,
-        out_specs=[hbm] * 6,
-        scratch_shapes=[pltpu.VMEM(one.shape, one.dtype) for one in (tokens, gain, w_qkv, owners)]
+        + [jax.ShapeDtypeStruct((own, width), jnp.bfloat16), jax.ShapeDtypeStruct((dp_count * cot.shape[1], own), jnp.bfloat16)]
+        + [jax.ShapeDtypeStruct((seg.shape[1] // TQ, 128), jnp.int32)],
+        in_specs=[hbm] * 6,
+        out_specs=[hbm] * 6 + [vmem],
+        scratch_shapes=[pltpu.VMEM(one.shape, one.dtype) for one in (tokens, gain, w_qkv, owners, seg)]
         + [pltpu.VMEM((total, width), jnp.bfloat16)] + [pltpu.VMEM((total, cols), jnp.bfloat16)] * 3
         + [pltpu.VMEM((own, width), jnp.bfloat16), pltpu.VMEM((dp_count * cot.shape[1], own), jnp.bfloat16)]
-        + [dma((4,)), dma((4,)), dma((5,)), pltpu.VMEM(cot.shape, cot.dtype)] + [dma((PARTS,))] * 6 + [dma((dp_count,))] * 2 + [dma],
+        + [dma((5,)), dma((4,)), dma((5,)), pltpu.VMEM(cot.shape, cot.dtype)] + [dma((PARTS,))] * 6 + [dma((dp_count,))] * 2 + [dma],
         compiler_params=pltpu.CompilerParams(collective_id=1, has_side_effects=True, vmem_limit_bytes=VMEM_BYTES),
         cost_estimate=pl.CostEstimate(flops=6 * total * width * cols, bytes_accessed=10 * total * width, transcendentals=0),
         name="project",
-    )(tokens, gain, w_qkv, cot, owners)
+    )(tokens, gain, w_qkv, cot, owners, seg)
 
 
 def gelu_and_slope(values):
@@ -602,7 +609,7 @@
         values = mine[0, piece(c), :] + arrived(0, PAIR, c) + arrived(0, ACROSS, c)
         residual[piece(c), :] = values
         unit, _ = norm_unit(values)
-        mlp_rows[spot(mp, c), :] = (unit * gain_ref[1:2, :]).astype(low)
+        mlp_rows[spot(mp, c), :] = (unit * gain_ref[...].reshape(1, -1)).astype(low)
         row_copy(0, 0, c, mp, mlp_rows).start()
         row_copy(0, 1, c, mp, mlp_rows).start()
         row_copy(0, 1, c, pair, mlp_rows).wait_recv()
@@ -625,7 +632,7 @@
         cols = slice(b * 256, (b + 1) * 256)
         up = lax.dot_general(mlp_rows[:, cols], grad_pre[...], TN, preferred_element_type=full)
         gain_col = jnp.sum(up * w_up_ref[cols, :].astype(full), axis=1, keepdims=True)
-        gain_part_ref[:, cols] = jnp.broadcast_to(gain_col, (256, 128)).T[0:8] / gain_ref[1:2, cols]
+        gain_part_ref[:, cols] = jnp.broadcast_to(gain_col, (256, 128)).T[0:8] / gain_ref[cols].reshape(1, -1)
         up = up.astype(low)
         down = lax.dot_general(grad_rows[:, cols], active[...], TN, preferred_element_type=full).astype(low)
         for j in range(256 // size):
@@ -651,7 +658,7 @@
     def back_norm(c):
         grad = mine[1, piece(c), :] + arrived(1, PAIR, c) + arrived(1, ACROSS, c)
         unit, inverse = norm_unit(residual[piece(c), :])
-        scaled = grad * gain_ref[1:2, :]
+        scaled = grad * gain_ref[...].reshape(1, -1)
         first_mean = jnp.mean(scaled, axis=-1, keepdims=True)
         second_mean = jnp.mean(scaled * unit, axis=-1, keepdims=True)
         total = inverse * (scaled - first_mean - unit * second_mean) + grad_own_ref[piece(c), :].astype(full)
@@ -935,7 +942,7 @@
     add((2, 0))
 
     row = lax.broadcasted_iota(jnp.int32, (8, width), 0)
-    gain_dp[dp] = jnp.where(row == 0, gain_part_ref[...], jnp.where(row == 1, gain_row / gain_ref[0:1, :], 0.0))
+    gain_dp[dp] = jnp.where(row == 0, gain_part_ref[...], jnp.where(row == 1, gain_row / gain_ref[...].reshape(1, -1), 0.0))
 
     def gain_over_dp(k, owner):
         return remote(gain_dp.at[owner], gain_dp.at[owner], dp_gain_send.at[k], dp_gain_recv.at[k], (lax.rem(dp + k, dp_count), mp))
@@ -970,7 +977,7 @@
     def back_norm(c):
         grad = mine[piece(c), :] + arrived(PAIR, c) + arrived(ACROSS, c)
         unit, inverse = norm_unit(tokens_ref[piece(c), :].astype(full))
-        scaled = grad * gain_ref[0:1, :]
+        scaled = grad * gain_ref[...].reshape(1, -1)
         first_mean = jnp.mean(scaled, axis=-1, keepdims=True)
         second_mean = jnp.mean(scaled * unit, axis=-1, keepdims=True)
         total = inverse * (scaled - first_mean - unit * second_mean) + grad_residual_ref[piece(c), :]
@@ -1041,6 +1048,80 @@
     return grad_tokens, d_sum if fits else lax.psum(d_sum, "dp"), gains
 
 
+def finish_kernel(
+    first_ref, first_came_ref, second_ref, second_came_ref, attn_ref, qkv_ref, gains_ref, tokens_hbm, relaid_hbm,
+    up_ref, down_ref, attn_out_ref, qkv_out_ref, gain_attn_ref, gain_mlp_ref, tokens_out_hbm, relaid_out_hbm, tokens_ref, relaid_ref, load_sem, store_sem,
+):
+    loads = local_copies(((tokens_hbm, tokens_ref), (relaid_hbm, relaid_ref)), load_sem)
+    stores = local_copies(((tokens_ref, tokens_out_hbm), (relaid_ref, relaid_out_hbm)), store_sem)
+
+    @pl.when(pl.program_id(0) == 0)
+    def _():
+        for load in loads:
+            load.start()
+
+    @pl.when(pl.program_id(0) == 1)
+    def _():
+        for load, store in zip(loads, stores):
+            load.wait()
+            store.start()
+
+    full = jnp.float32
+    dp = lax.axis_index("dp")
+    size = first_ref.shape[0]
+    mine, came = first_ref[...].astype(full), first_came_ref[...].astype(full)
+    even = lax.rem(dp, 2) == 0
+    up_ref[0:size, :] = jnp.where(even, mine, came)
+    down_ref[0:size, :] = jnp.where(even, came, mine)
+    mine, came = second_ref[...].astype(full), second_came_ref[...].astype(full)
+    even = lax.rem(dp // 2, 2) == 0
+    low, high = jnp.where(even, mine, came), jnp.where(even, came, mine)
+    half = size // 2
+    up_ref[size:size + half, :] = low[:half]
+    up_ref[size + half:, :] = high[:half]
+    down_ref[size:size + half, :] = low[half:]
+    down_ref[size + half:, :] = high[half:]
+    attn_out_ref[...] = attn_ref[...].astype(full)
+    qkv_out_ref[...] = qkv_ref[...].astype(full)
+    gain_mlp_ref[...] = gains_ref[0]
+    gain_attn_ref[...] = gains_ref[1]
+
+    @pl.when(pl.program_id(0) == pl.num_programs(0) - 1)
+    def _():
+        for store in stores:
+            store.wait()
+
+
+def finish(first, first_came, second, second_came, weight_sum, gains, grad_tokens, relaid):
+    steps = MLP_CHUNKS // 2
+    size = first.shape[0] // steps
+    rows, width = weight_sum.shape
+    cols = rows // 4
+    full = jnp.float32
+    hbm = pl.BlockSpec(memory_space=pl.ANY)
+    vmem = pl.BlockSpec(memory_space=pltpu.VMEM)
+    shape = jax.ShapeDtypeStruct
+
+    def block(count, ahead=0):
+        return pl.BlockSpec((count, width), lambda i: (i + ahead, 0))
+
+    return pl.pallas_call(
+        finish_kernel,
+        grid=(steps,),
+        out_shape=[
+            shape((2 * steps * size, width), full), shape((2 * steps * size, width), full), shape((cols, width), full),
+            shape((3 * cols, width), full), shape((width,), full), shape((width,), full), shape(grad_tokens.shape, grad_tokens.dtype), shape(relaid.shape, relaid.dtype),
+        ],
+        in_specs=[block(size)] * 4 + [block(cols // 3), block(cols, 1), vmem, hbm, hbm],
+        out_specs=[block(2 * size)] * 2 + [block(cols // 3), block(cols), vmem, vmem, hbm, hbm],
+        scratch_shapes=[pltpu.VMEM(one.shape, one.dtype) for one in (grad_tokens, relaid)]
+        + [pltpu.SemaphoreType.DMA((2,)), pltpu.SemaphoreType.DMA((2,))],
+        compiler_params=pltpu.CompilerParams(vmem_limit_bytes=VMEM_BYTES),
+        cost_estimate=pl.CostEstimate(flops=0, bytes_accessed=14 * rows * width, transcendentals=0),
+        name="finish",
+    )(first, first_came, second, second_came, weight_sum, weight_sum, gains, grad_tokens, relaid)
+
+
 def local(
     tokens, segment_ids, gene_owner, w_qkv, w_attn_out, w_up, w_down, gain_attn, gain_mlp, cotangent
 ):
@@ -1049,50 +1130,37 @@
     capacity = cotangent.shape[0] // dp_count
     low, full = jnp.bfloat16, jnp.float32
     w_rows = jnp.swapaxes(w_qkv, 1, 2)
-    gains_in = jnp.stack([gain_attn, gain_mlp])
-    attn_in, *projected, grad_block, place = project(
-        tokens, gains_in, w_rows, cotangent.reshape(dp_count, capacity, width), gene_owner.reshape(1, -1)
+    attn_in, *projected, grad_block, place, ranges = project(
+        tokens, gain_attn, w_rows, cotangent.reshape(dp_count, capacity, width), gene_owner.reshape(1, -1), segment_ids
     )
     grad_across = lax.ppermute(grad_block, "mp", [(i, i ^ 2) for i in range(lax.axis_size("mp"))])
-    merged, log_sums = attend_forward(segment_ids, *projected)
+    merged, log_sums = attend_forward(ranges, segment_ids, *projected)
     residual_rows, grad_merged, grad_residual, outgoing, first, second, gain_part, d_out = middle(
-        dp_count, merged, w_attn_out, tokens, gains_in, w_up, w_down, grad_block, grad_across, place
+        dp_count, merged, w_attn_out, tokens, gain_mlp, w_up, w_down, grad_block, grad_across, place
     )
     cols = w_qkv.shape[2]
-    if sum_stages(2 * width, MLP_CHUNKS, dp_count):
-        size = width // MLP_CHUNKS
-        place_y = lax.rem(lax.axis_index("dp"), 2) == 0
-        place_z = lax.rem(lax.axis_index("dp") // 2, 2) == 0
+    whole = sum_stages(2 * width, MLP_CHUNKS, dp_count) == 0
+    if not whole:
         first_came = lax.ppermute(first, "dp", [(i, i ^ 1) for i in range(dp_count)])
         second_came = lax.ppermute(second, "dp", [(i, i ^ 2) for i in range(dp_count)])
         gain_part, first_came, second_came = lax.optimization_barrier((gain_part, first_came, second_came))
-        first = [
-            one.reshape(-1, size, width)
-            for one in (jnp.where(place_y, first, first_came), jnp.where(place_y, first_came, first))
-        ]
-        second = jnp.stack(
-            [
-                one.reshape(-1, 2, size // 2, width)
-                for one in (jnp.where(place_z, second, second_came), jnp.where(place_z, second_came, second))
-            ],
-            axis=2,
-        )
-        up_sum, down_sum = (
-            jnp.stack([first[i], second[:, i].reshape(-1, size, width)], axis=1).reshape(-1, width).astype(full)
-            for i in range(2)
-        )
-    else:
-        d_sum = lax.psum(jnp.concatenate([first, second]), "dp").reshape(MLP_CHUNKS, 2, -1, width).astype(full)
-        up_sum, down_sum = (d_sum[:, i].reshape(-1, width) for i in range(2))
     relaid = lax.all_to_all(
         outgoing.reshape(dp_count, capacity, width), "dp", split_axis=0, concat_axis=0, tiled=True
     ).reshape(dp_count * capacity, width)
-    grad_proj = attend_backward(segment_ids, *projected, merged, grad_merged, log_sums)
+    grad_proj = attend_backward(ranges, segment_ids, *projected, merged, grad_merged, log_sums)
     grad_tokens, weight_sum, gains = last(
-        dp_count, *grad_proj, w_rows, attn_in, grad_residual, tokens, gains_in, gain_part, d_out
-    )
-    qkv_sum = weight_sum[cols:].reshape(3, cols, width).astype(full)
-    attn_sum = weight_sum[:cols].astype(full)
+        dp_count, *grad_proj, w_rows, attn_in, grad_residual, tokens, gain_attn, gain_part, d_out
+    )
+    if whole:
+        d_sum = lax.psum(jnp.concatenate([first, second]), "dp").reshape(MLP_CHUNKS, 2, -1, width).astype(full)
+        up_sum, down_sum = (d_sum[:, i].reshape(-1, width) for i in range(2))
+        attn_sum, qkv_sum = weight_sum[:cols].astype(full), weight_sum[cols:].astype(full)
+        gain_one, gain_two = gains[1], gains[0]
+    else:
+        up_sum, down_sum, attn_sum, qkv_sum, gain_one, gain_two, grad_tokens, relaid = finish(
+            first, first_came, second, second_came, weight_sum, gains, grad_tokens, relaid
+        )
+    qkv_sum = qkv_sum.reshape(3, cols, width)
     return (
         relaid,
         grad_tokens,
@@ -1100,8 +1168,8 @@
         attn_sum,
         up_sum,
         down_sum,
-        gains[1],
-        gains[0],
+        gain_one,
+        gain_two,
     )
 
 

time: 263 us -> 248 us (0.943)
  local copies, waits for them, and re-layouts: 10.7 us -> 1.84 us
  other arithmetic: 4.35 us -> 0 us
    pallas_call x0 -> x1, Pallas kernels: none -> 6.19 us  [finish(): pl.pallas_call(finish_kernel, grid=(steps,), out_shape=[shape((2 * steps...]
    pallas_call x1, Pallas kernels: 37.6 us -> 32.5 us  [attend_backward(): pl.pallas_call(functools.partial(bwd_kernel, n, heads), grid_spec=pltpu.P...]
    pallas_call x1, Pallas kernels: 25.1 us -> 20.5 us  [attend_forward(): pl.pallas_call(functools.partial(fwd_kernel, n, heads), grid_spec=pltpu.P...]
    convert_element_type x2 -> x0, local copies, waits for them, and re-layouts: 3.32 us -> none  [local(): jnp.stack([first[i], second[:, i].reshape(-1, size, width)], axis=1)]
    slice x2 -> x0, local copies, waits for them, and re-layouts: 2.65 us -> none  [the longest x1 1.43 us: local(): gains[0]]
  transfers between devices with their start and end apart: 4 -> 4, of which waited for: 0 -> 0; matrix products, arithmetic and copies ran while one was open for 4% -> 0% of each run, Pallas kernels for 42% -> 41%
where the time goes in v7:
time: 248 us
  Pallas kernels  236 us (95%)
  starting transfers between devices  9.29 us (4%)
    pallas_call x1, Pallas kernels, middle(): pl.pallas_call(functools.partial(middle_kernel, stages), out_shape=[shape...  99.1 us
    pallas_call x1, Pallas kernels, last(): pl.pallas_call(functools.partial(last_kernel, dp_count, fits), out_shape=...  47.9 us
    pallas_call x1, Pallas kernels, attend_backward(): pl.pallas_call(functools.partial(bwd_kernel, n, heads), grid_spec=pltpu.P...  32.5 us
    pallas_call x1, Pallas kernels, project(): pl.pallas_call(functools.partial(project_kernel, dp_count), out_shape=[ja...  29.9 us
    pallas_call x1, Pallas kernels, attend_forward(): pl.pallas_call(functools.partial(fwd_kernel, n, heads), grid_spec=pltpu.P...  20.5 us
    pallas_call x1, Pallas kernels, finish(): pl.pallas_call(finish_kernel, grid=(steps,), out_shape=[shape((2 * steps...  6.19 us
    all_to_all x1, starting transfers between devices, local(): lax.all_to_all(outgoing.reshape(dp_count, capacity, width), 'dp', split_a...  5.18 us
  transfers between devices with their start and end apart: 4, of which 0 were waited for; matrix products, arithmetic and copies ran while one was open for 0% of the time, Pallas kernels for 41%

profile of v7, /device:TPU:0, one launch (start us, length us, event | category | flops | bytes accessed | tf_op | source)
XLA Modules:
  0.0 248.3 jit_solution(7865714780151083781)
XLA Ops:
  0.6 29.9 %project.1 = (bf16[2048,768]{1,0:T(8,128)(2,1)}, bf16[2048,192]{1,0:T(8,128)(2,1)}, bf16[2048,192]{1,0:T(8,128)(2,1)}, bf16[2048,192]{1,0:T(8,128)(2,1)}, bf16[5...) custom-call(bf16[512,768]{1,0:T(8,128)(2,1)} %tokens_hbm.5, f32[768]{0:T(1024)} %gain_hbm.5, ...), custom_call_target="tpu_custom_call" | custom-call | flops 1811939328 | bytes 15728640 | tf_op jit(solution)/shard_map/project/pallas_call | solution.py:458
  30.6 0.6 collective-permute-start
  31.2 20.5 %attend_forward.1 = (bf16[2048,192]{1,0:T(8,128)(2,1)}, f32[8,2048]{1,0:T(8,128)}) custom-call(s32[8,128]{1,0:T(8,128)} %get-tuple-element.41.ranges, s32[1,2048]{1,0:T(1,128)} %segv_ref.3, bf16[2048,192]{1,0:T(8,128)(2,1)} %get-tuple-element.42.q_ref, bf16[2048,192]{1,0:T(8,128)(2,1)} %get-tuple-element.43.k_ref, bf16[2048,192]{1,0:T(8,128)(2,1)} %get-tuple-element.44.v_ref), custom_call_target="tpu_custom_call" | custom-call | flops 3221225472 | bytes 3145728 | tf_op jit(solution)/shard_map/attend_forward/pallas_call | solution.py:109
  51.7 0.0 collective-permute-done.grad_across_hbm
  51.7 0.9 copy-done.5
  52.6 99.1 %middle.1 = (bf16[2048,768]{1,0:T(8,128)(2,1)}, bf16[2048,192]{1,0:T(8,128)(2,1)}, f32[512,768]{1,0:T(8,128)}, bf16[640,768]{1,0:T(8,128)(2,1)}, bf16[384,768]{1...) custom-call(bf16[2048,192]{1,0:T(8,128)(2,1)} %get-tuple-element.45.merged_hbm.o_ref, ...), custom_call_target="tpu_custom_call" | custom-call | flops 19327352832 | bytes 31457280 | tf_op jit(solution)/shard_map/middle/pallas_call | solution.py:753
  151.7 0.0 copy-start.1
  151.8 0.0 copy-start.2
  151.8 5.2 %all-to-all-start = ((bf16[8,80,768]{2,1,0:T(8,128)(2,1)}), bf16[8,80,768]{2,1,0:T(8,128)(2,1)S(1)}, u32[]{:S(2)}, u32[]{:S(2)}) async-start(bf16[8,80,768]{2,1,0:T(8,128)(2,1)} %bitcast.9), calls=%async_computation | async-start | bytes 1966080 | tf_op jit(solution)/shard_map/all_to_all | solution.py:1147
  156.9 0.0 copy-done.1
  156.9 2.0 collective-permute-start.1
  159.0 0.0 copy-done.2
  159.0 1.5 collective-permute-start.2
  160.4 32.5 %attend_backward.1 = (bf16[2048,192]{1,0:T(8,128)(2,1)}, bf16[2048,192]{1,0:T(8,128)(2,1)}, bf16[2048,192]{1,0:T(8,128)(2,1)}) custom-call(s32[8,128]{1,0:T(8,128)} %get-tuple-element.41.ranges, s32[1,2048]{1,0:T(1,128)} %segv_ref.3, bf16[2048,192]{1,0:T(8,128)(2,1)} %get-tuple-element.42.q_ref, bf16[2048,192]{1,0:T(8,128)(2,1)} %get-tuple-element.43.k_ref, ...), custom_call_target="tpu_custom_call" | custom-call | flops 8053063680 | bytes 6291456 | tf_op jit(solution)/shard_map/attend_backward/pallas_call | solution.py:187
  193.0 0.0 collective-permute-done.1.first_came_ref
  193.0 0.0 copy-start.3
  193.0 0.0 collective-permute-done.2.second_came_ref
  193.0 0.0 copy-start.4
  193.0 47.9 %last.1 = (bf16[512,768]{1,0:T(8,128)(2,1)}, bf16[768,768]{1,0:T(8,128)(2,1)}, f32[8,768]{1,0:T(8,128)}) custom-call(bf16[2048,192]{1,0:T(8,128)(2,1)} %get-tuple-element.55.dq_hbm, bf16[2048,192]{1,0:T(8,128)(2,1)} %get-tuple-element.56.dk_hbm, bf16[2048,192]{1,0:T(8,128)(2,1)} %get-tuple-element.57.dv_hbm, bf16[3,192,768]{2,1,0:T(8,128)(2,1)} %bitcast.13, ...), custom_call_target="tpu_custom_call" | custom-call | flops 3623878656 | bytes 7864320 | tf_op jit(solution)/shard_map/last/pallas_call | solution.py:1031
  241.0 0.0 copy-done.3
  241.0 0.0 all-to-all-done
  241.0 0.0 copy-start
  241.0 0.9 copy-done
  242.0 6.2 %finish.1 = (f32[768,768]{1,0:T(8,128)}, f32[768,768]{1,0:T(8,128)}, f32[192,768]{1,0:T(8,128)}, f32[576,768]{1,0:T(8,128)}, f32[768]{0:T(1024)}, /*index=5*/f32...) custom-call(bf16[384,768]{1,0:T(8,128)(2,1)} %get-tuple-element.48.first_ref, bf16[384,768]{1,0:T(8,128)(2,1)} %copy-done.3, ...), custom_call_target="tpu_custom_call" | custom-call | bytes 8257536 | tf_op jit(solution)/shard_map/finish/pallas_call | solution.py:1108
  (2 shorter events, 0.0 us)
Async XLA Ops:
  30.6 21.1 %collective-permute-start = (bf16[512,768]{1,0:T(8,128)(2,1)}, bf16[512,768]{1,0:T(8,128)(2,1)S(1)}, u32[]{:S(2)}, u32[]{:S(2)}) collective-permute-start(bf16[512,768]{1,0:T(8,128)(2,1)} %get-tuple-element.46.grad_own_hbm), channel_id=1, source_target_pairs={{0,2},{1,3},{2,0},{3,1},{4,6},{5,7},{6,4},{7,5},{8,10},{9,11},{10,... | collective-permute-start | bytes 2359304 | tf_op jit(solution)/shard_map/ppermute | solution.py:1136
  51.7 0.9 copy-start.5
  151.7 5.2 %copy-start.1 = (bf16[384,768]{1,0:T(8,128)(2,1)S(1)}, bf16[384,768]{1,0:T(8,128)(2,1)}, u32[]{:S(2)}) copy-start(bf16[384,768]{1,0:T(8,128)(2,1)} %get-tuple-element.48.first_ref) | copy-start | bytes 1769476
  151.8 7.2 %copy-start.2 = (bf16[384,768]{1,0:T(8,128)(2,1)S(1)}, bf16[384,768]{1,0:T(8,128)(2,1)}, u32[]{:S(2)}) copy-start(bf16[384,768]{1,0:T(8,128)(2,1)} %get-tuple-element.50.second_ref) | copy-start | bytes 1769476
  151.8 89.2 %all-to-all-start = ((bf16[8,80,768]{2,1,0:T(8,128)(2,1)}), bf16[8,80,768]{2,1,0:T(8,128)(2,1)S(1)}, u32[]{:S(2)}, u32[]{:S(2)}) async-start(bf16[8,80,768]{2,1,0:T(8,128)(2,1)} %bitcast.9), calls=%async_computation | async-start | bytes 1966080 | tf_op jit(solution)/shard_map/all_to_all | solution.py:1147
  156.9 36.0 %collective-permute-start.1 = (bf16[384,768]{1,0:T(8,128)(2,1)S(1)}, bf16[384,768]{1,0:T(8,128)(2,1)S(1)}, u32[]{:S(2)}, u32[]{:S(2)}) collective-permute-start(bf16[384,768]{1,0:T(8,128)(2,1)S(1)} %copy-done.1), channel_id=1, source_target_pairs={{0,4},{4,0},{8,12},{12,8},{16,20},{20,16},{24,28},{28,24},{1,5},{5... | collective-permute-start | bytes 1769480 | tf_op jit(solution)/shard_map/ppermute | solution.py:1144
  159.0 34.0 %collective-permute-start.2 = (bf16[384,768]{1,0:T(8,128)(2,1)S(1)}, bf16[384,768]{1,0:T(8,128)(2,1)S(1)}, u32[]{:S(2)}, u32[]{:S(2)}) collective-permute-start(bf16[384,768]{1,0:T(8,128)(2,1)S(1)} %copy-done.2), channel_id=1, source_target_pairs={{0,8},{4,12},{8,0},{12,4},{16,24},{20,28},{24,16},{28,20},{1,9},{5... | collective-permute-start | bytes 1769480 | tf_op jit(solution)/shard_map/ppermute | solution.py:1145
  193.0 48.0 %copy-start.3 = (bf16[384,768]{1,0:T(8,128)(2,1)}, bf16[384,768]{1,0:T(8,128)(2,1)S(1)}, u32[]{:S(2)}) copy-start(bf16[384,768]{1,0:T(8,128)(2,1)S(1)} %collective-permute-done.1.first_came_ref) | copy-start | bytes 1769476
  193.0 48.0 %copy-start.4 = (bf16[384,768]{1,0:T(8,128)(2,1)}, bf16[384,768]{1,0:T(8,128)(2,1)S(1)}, u32[]{:S(2)}) copy-start(bf16[384,768]{1,0:T(8,128)(2,1)S(1)} %collective-permute-done.2.second_came_ref) | copy-start | bytes 1769476
  241.0 1.0 copy-start

commit v8 on v7

--- a/solution.py
+++ b/solution.py
@@ -13,6 +13,7 @@
 NN = (((1,), (0,)), ((), ()))
 TN = (((0,), (0,)), ((), ()))
 MASKED = -1e30
+TALL = HEAD + 16
 epsilon = 1e-05
 
 
@@ -65,7 +66,10 @@
     def _():
         seg_columns(segv_ref, cols, n)
         for t in range(n // TK):
-            vt[:, t * TK:(t + 1) * TK] = v_ref[t * TK:(t + 1) * TK, :].astype(jnp.float32).T.astype(jnp.bfloat16)
+            turned = v_ref[t * TK:(t + 1) * TK, :].astype(jnp.float32).T.astype(jnp.bfloat16)
+            for h in range(heads):
+                vt[h * TALL:h * TALL + HEAD, t * TK:(t + 1) * TK] = turned[h * HEAD:(h + 1) * HEAD]
+                vt[h * TALL + HEAD:(h + 1) * TALL, t * TK:(t + 1) * TK] = jnp.ones((TALL - HEAD, TK), jnp.bfloat16)
 
     q0 = pl.multiple_of(tile * TQ, TQ)
     q = q_ref[...] * jnp.bfloat16(HEAD ** -0.5)
@@ -90,16 +94,17 @@
     def second(k0, size, acc):
         out = []
         for h in range(heads):
-            p = jnp.exp(scores[h, pl.ds(k0, size), :] - tops[h])
-            total = acc[h][1] + jnp.sum(p, axis=0, keepdims=True)
-            part = lax.dot_general(vt[h * HEAD:(h + 1) * HEAD, pl.ds(k0, size)], p.astype(jnp.bfloat16), NN, preferred_element_type=jnp.float32)
-            out.append((acc[h][0] + part, total))
+            p = jnp.exp(scores[h, pl.ds(k0, size), :] - tops[h]).astype(jnp.bfloat16)
+            out.append(acc[h] + jnp.dot(vt[h * TALL:(h + 1) * TALL, pl.ds(k0, size)], p, preferred_element_type=jnp.float32))
         return tuple(out)
 
-    acc = over_blocks(ranges, tile, second, tuple((jnp.zeros((HEAD, TQ), jnp.float32), jnp.zeros((1, TQ), jnp.float32)) for _ in range(heads)))
-    ot = jnp.concatenate([acc[h][0] / acc[h][1] for h in range(heads)], axis=0)
+    acc = over_blocks(ranges, tile, second, tuple(jnp.zeros((TALL, TQ), jnp.float32) for _ in range(heads)))
+    totals = [one[HEAD:HEAD + 1] for one in acc]
+    ot = jnp.concatenate([acc[h][:HEAD] / totals[h] for h in range(heads)], axis=0)
     o_ref[...] = ot.T.astype(jnp.bfloat16)
-    lse_ref[...] = jnp.concatenate([tops[h] + jnp.log(acc[h][1]) for h in range(heads)] + [jnp.zeros((8 - heads, TQ), jnp.float32)], axis=0)
+    lse_ref[...] = jnp.concatenate(
+        [tops[h] + jnp.log(totals[h]) for h in range(heads)] + [jnp.zeros((8 - heads, TQ), jnp.float32)], axis=0
+    )
 
 
 def attend_forward(ranges, seg, q, k, v):
@@ -113,7 +118,7 @@
             grid=(n // TQ,),
             in_specs=[whole, pl.BlockSpec((TQ, width), lambda t, s: (t, 0)), whole, whole],
             out_specs=[pl.BlockSpec((TQ, width), lambda t, s: (t, 0)), pl.BlockSpec((8, TQ), lambda t, s: (0, t))],
-            scratch_shapes=[pltpu.VMEM((width, n), jnp.bfloat16), pltpu.VMEM((n, 128), jnp.float32), pltpu.VMEM((heads, n, TQ), jnp.float32)],
+            scratch_shapes=[pltpu.VMEM((heads * TALL, n), jnp.bfloat16), pltpu.VMEM((n, 128), jnp.float32), pltpu.VMEM((heads, n, TQ), jnp.float32)],
         ),
         out_shape=[jax.ShapeDtypeStruct((n, width), jnp.bfloat16), jax.ShapeDtypeStruct((8, n), jnp.float32)],
         compiler_params=pltpu.CompilerParams(vmem_limit_bytes=VMEM_BYTES),
@@ -122,52 +127,51 @@
     )(ranges, seg, q, k, v)
 
 
-def bwd_kernel(n, heads, ranges, segv_ref, q_ref, k_ref, v_ref, o_ref, do_ref, lse_ref, dq_ref, dk_ref, dv_ref, kt, cols, dk_acc, dv_acc):
+def bwd_kernel(
+    n, heads, ranges, segv_ref, q_ref, k_ref, v_ref, o_ref, do_ref, lse_ref, dq_ref, dk_ref, dv_ref,
+    kt, kh, vh, cols, dk_acc, dv_acc,
+):
     tile = pl.program_id(0)
-    width = heads * HEAD
+
+    def head_cols(h):
+        return slice(h * HEAD, (h + 1) * HEAD)
 
     @pl.when(tile == 0)
     def _():
+        dk_acc[...] = jnp.zeros_like(dk_acc)
+        dv_acc[...] = jnp.zeros_like(dv_acc)
         seg_columns(segv_ref, cols, n)
+        for h in range(heads):
+            kh[h] = k_ref[:, head_cols(h)]
+            vh[h] = v_ref[:, head_cols(h)]
         for t in range(n // TK):
             kt[:, t * TK:(t + 1) * TK] = k_ref[t * TK:(t + 1) * TK, :].astype(jnp.float32).T.astype(jnp.bfloat16)
-        dk_acc[...] = jnp.zeros_like(dk_acc)
-        dv_acc[...] = jnp.zeros_like(dv_acc)
 
     q0 = pl.multiple_of(tile * TQ, TQ)
-    masks = head_masks(width, heads)
     q = q_ref[...] * jnp.bfloat16(HEAD ** -0.5)
     do = do_ref[...]
-    qm = [jnp.where(m, q, jnp.bfloat16(0)) for m in masks]
-    dm = [jnp.where(m, do, jnp.bfloat16(0)) for m in masks]
     seg_row = segv_ref[0:1, pl.ds(q0, TQ)].astype(jnp.float32)
-    prod = do.astype(jnp.float32) * o_ref[...].astype(jnp.float32)
-    high = prod.astype(jnp.bfloat16)
-    rest = (prod - high.astype(jnp.float32)).astype(jnp.bfloat16)
-    row = lax.broadcasted_iota(jnp.int32, (16, width), 0)
-    lane = lax.broadcasted_iota(jnp.int32, (16, width), 1)
-    pick = jnp.where(lane // HEAD == row, 1.0, 0.0).astype(jnp.bfloat16)
-    delta = lax.dot_general(pick, high, NT, preferred_element_type=jnp.float32) + lax.dot_general(pick, rest, NT, preferred_element_type=jnp.float32)
+    do_wide = do.astype(jnp.float32)
+    products = (do_wide * o_ref[...].astype(jnp.float32)).T
+    q_turned = q.astype(jnp.float32).T.astype(jnp.bfloat16)
+    do_turned = do_wide.T.astype(jnp.bfloat16)
     lse = lse_ref[...]
+    deltas = [jnp.sum(products[head_cols(h)], axis=0, keepdims=True) for h in range(heads)]
+    q_heads = [q[:, head_cols(h)] for h in range(heads)]
+    do_heads = [do[:, head_cols(h)] for h in range(heads)]
 
     def body(k0, size, acc):
-        keys = k_ref[pl.ds(k0, size), :]
-        vals = v_ref[pl.ds(k0, size), :]
-        col = cols[pl.ds(k0, size), :]
-        same = jnp.concatenate([col] * (TQ // 128), axis=1) == seg_row
+        where = pl.ds(k0, size)
+        same = jnp.concatenate([cols[where, :]] * (TQ // 128), axis=1) == seg_row
         out = []
-        dks = jnp.zeros((size, width), jnp.float32)
-        dvs = jnp.zeros((size, width), jnp.float32)
         for h in range(heads):
-            s = lax.dot_general(keys, qm[h], NT, preferred_element_type=jnp.float32)
+            s = jnp.dot(kh[h, where, :], q_turned[head_cols(h)], preferred_element_type=jnp.float32)
             p = jnp.where(same, jnp.exp(s - lse[h:h + 1, :]), 0.0)
-            dp = lax.dot_general(vals, dm[h], NT, preferred_element_type=jnp.float32)
-            ds = (p * (dp - delta[h:h + 1, :])).astype(jnp.bfloat16)
-            dvs = dvs + lax.dot_general(p.astype(jnp.bfloat16), dm[h], NN, preferred_element_type=jnp.float32)
-            dks = dks + lax.dot_general(ds, qm[h], NN, preferred_element_type=jnp.float32)
-            out.append(acc[h] + lax.dot_general(kt[h * HEAD:(h + 1) * HEAD, pl.ds(k0, size)], ds, NN, preferred_element_type=jnp.float32))
-        dk_acc[pl.ds(k0, size), :] += dks
-        dv_acc[pl.ds(k0, size), :] += dvs
+            dp = jnp.dot(vh[h, where, :], do_turned[head_cols(h)], preferred_element_type=jnp.float32)
+            ds = (p * (dp - deltas[h])).astype(jnp.bfloat16)
+            dv_acc[h, where, :] += jnp.dot(p.astype(jnp.bfloat16), do_heads[h], preferred_element_type=jnp.float32)
+            dk_acc[h, where, :] += jnp.dot(ds, q_heads[h], preferred_element_type=jnp.float32)
+            out.append(acc[h] + jnp.dot(kt[head_cols(h), where], ds, preferred_element_type=jnp.float32))
         return tuple(out)
 
     acc = over_blocks(ranges, tile, body, tuple(jnp.zeros((HEAD, TQ), jnp.float32) for _ in range(heads)))
@@ -175,8 +179,9 @@
 
     @pl.when(tile == n // TQ - 1)
     def _():
-        dk_ref[...] = dk_acc[...].astype(jnp.bfloat16)
-        dv_ref[...] = dv_acc[...].astype(jnp.bfloat16)
+        for h in range(heads):
+            dk_ref[:, head_cols(h)] = dk_acc[h].astype(jnp.bfloat16)
+            dv_ref[:, head_cols(h)] = dv_acc[h].astype(jnp.bfloat16)
 
 
 def attend_backward(ranges, seg, q, k, v, o, do, lse):
@@ -191,7 +196,8 @@
             grid=(n // TQ,),
             in_specs=[whole, rows, whole, whole, rows, rows, pl.BlockSpec((8, TQ), lambda t, s: (0, t))],
             out_specs=[rows, whole, whole],
-            scratch_shapes=[pltpu.VMEM((width, n), jnp.bfloat16), pltpu.VMEM((n, 128), jnp.float32), pltpu.VMEM((n, width), jnp.float32), pltpu.VMEM((n, width), jnp.float32)],
+            scratch_shapes=[pltpu.VMEM((width, n), jnp.bfloat16)] + [pltpu.VMEM((heads, n, HEAD), jnp.bfloat16)] * 2
+            + [pltpu.VMEM((n, 128), jnp.float32)] + [pltpu.VMEM((heads, n, HEAD), jnp.float32)] * 2,
         ),
         out_shape=[jax.ShapeDtypeStruct((n, width), jnp.bfloat16)] * 3,
         compiler_params=pltpu.CompilerParams(vmem_limit_bytes=VMEM_BYTES),
@@ -204,7 +210,7 @@
 PARTS = 4
 VMEM_BYTES = 60 << 20
 MLP_CHUNKS = 6
-QKV_CHUNKS = 3
+QKV_CHUNKS = (128,) * 6
 
 
 def remote(src, dst, send, recv, device):
@@ -360,7 +366,7 @@
         rows = pl.ds(pl.multiple_of(owner * own, own), own)
         return pltpu.make_async_copy(rows_ref.at[rows], rows_hbm.at[rows], store_sem.at[i])
 
-    for k in range(1, dp_count):
+    for k in sorted(range(1, dp_count), key=lambda k: -min(k, dp_count - k)):
         slot_copy(k).start()
     self_copy = pltpu.make_async_copy(cot_ref.at[dp], returned_ref.at[dp], self_sem)
     self_copy.start()
@@ -778,14 +784,15 @@
 
 
 def direct_fits(rows, chunks, dp_count):
-    return dp_count % 2 == 0 and rows % (16 * chunks * dp_count) == 0
+    return dp_count % 2 == 0 and rows == sum(chunks) and all(one % (16 * dp_count) == 0 for one in chunks)
 
 
 def direct_steps(dp_count, chunks, acc, came, send, recv, out, out_hbm, keep_sem):
     dp, mp = lax.axis_index("dp"), lax.axis_index("mp")
-    chunk = acc.shape[0] // chunks
     group = dp_count // 2
-    half, slot = chunk // 2, chunk // dp_count
+    starts = [sum(chunks[:k]) for k in range(len(chunks))]
+    halves = [one // 2 for one in chunks]
+    slots = [one // dp_count for one in chunks]
     y, z = lax.rem(dp, 2), dp // 2
     beside = (dp + 1 - 2 * y, mp)
     others = sorted(range(1, group), key=lambda j: -min(j, group - j))
@@ -794,31 +801,31 @@
         return pl.ds(pl.multiple_of(start, 16), size)
 
     def low(k, side, g=0):
-        return k * chunk + side * half + g * slot
+        return starts[k] + side * halves[k] + g * slots[k]
 
     def member(j):
         return lax.rem(z + j, group)
 
     def slot_of(k, j):
-        return span(k * chunk + half + (j - 1) * slot, slot)
+        return span(starts[k] + halves[k] + (j - 1) * slots[k], slots[k])
 
     def halve(k):
-        return remote(acc.at[span(low(k, 1 - y), half)], came.at[span(k * chunk, half)], send.at[k, 0], recv.at[k, 0], beside)
+        return remote(acc.at[span(low(k, 1 - y), halves[k])], came.at[span(starts[k], halves[k])], send.at[k, 0], recv.at[k, 0], beside)
 
     def scatter(k, j):
-        piece = acc.at[span(low(k, y, member(j)), slot)]
+        piece = acc.at[span(low(k, y, member(j)), slots[k])]
         return remote(piece, came.at[slot_of(k, j)], send.at[k, j], recv.at[k, j], (y + 2 * member(j), mp))
 
     def gather(k, j, mine=True):
-        rows = out.at[span(low(k, y, z if mine else member(group - j)), slot)]
+        rows = out.at[span(low(k, y, z if mine else member(group - j)), slots[k])]
         return remote(rows, rows, send.at[k, group + j - 1], recv.at[k, group + j - 1], (y + 2 * member(j), mp))
 
     def double(k, mine=True):
-        rows = span(low(k, y if mine else 1 - y), half)
+        rows = span(low(k, y if mine else 1 - y), halves[k])
         return remote(out.at[rows], out_hbm.at[rows], send.at[k, 2 * group - 1], recv.at[k, 2 * group - 1], beside)
 
     def keep(k):
-        rows = span(low(k, y), half)
+        rows = span(low(k, y), halves[k])
         return pltpu.make_async_copy(out.at[rows], out_hbm.at[rows], keep_sem.at[k])
 
     def step(k, i):
@@ -826,13 +833,13 @@
             halve(k).start()
         elif i == 1:
             halve(k).wait_recv()
-            rows = span(low(k, y), half)
-            total = acc[rows, :].astype(jnp.float32) + came[span(k * chunk, half), :].astype(jnp.float32)
+            rows = span(low(k, y), halves[k])
+            total = acc[rows, :].astype(jnp.float32) + came[span(starts[k], halves[k]), :].astype(jnp.float32)
             acc[rows, :] = total.astype(jnp.bfloat16)
             for j in others:
                 scatter(k, j).start()
         elif i == 2:
-            rows = span(low(k, y, z), slot)
+            rows = span(low(k, y, z), slots[k])
             total = acc[rows, :].astype(jnp.float32)
             for j in others:
                 scatter(k, j).wait_recv()
@@ -849,7 +856,7 @@
             double(k, False).wait_recv()
 
     def drain():
-        for k in range(chunks):
+        for k in range(len(chunks)):
             halve(k).wait_send()
             for j in others:
                 scatter(k, j).wait_send()
@@ -869,7 +876,7 @@
 ):
     loads = local_copies(
         (
-            (dq_hbm, dq_ref), (rows_hbm, rows_ref), (w_hbm, w_ref), (d_out_hbm, d_out_ref), (dk_hbm, dk_ref), (dv_hbm, dv_ref),
+            (d_out_hbm, d_out_ref), (dq_hbm, dq_ref), (rows_hbm, rows_ref), (w_hbm, w_ref), (dk_hbm, dk_ref), (dv_hbm, dv_ref),
             (gain_hbm, gain_ref), (gain_part_hbm, gain_part_ref), (grad_residual_hbm, grad_residual_ref), (tokens_hbm, tokens_ref),
         ),
         load_sem,
@@ -916,30 +923,43 @@
         total = total + jnp.dot(dk_ref[where, :], w_ref[1], preferred_element_type=full)
         return total + jnp.dot(dv_ref[where, :], w_ref[2], preferred_element_type=full)
 
+    ends = [sum(QKV_CHUNKS[:k + 1]) for k in range(len(QKV_CHUNKS))]
+
+    def ready(low_row, high_row):
+        add(*[(k, 0) for k, end in enumerate(ends) if low_row < end <= high_row])
+
     def weight_grad(p, ref):
         grad = lax.dot_general(ref[...], rows_ref[...], TN, preferred_element_type=full)
         acc[(p + 1) * cols:(p + 2) * cols, :] = grad.astype(low)
+        ready((p + 1) * cols, (p + 2) * cols)
         return jnp.sum(grad * w_ref[p].astype(full), axis=0, keepdims=True)
 
-    for load in loads[:4]:
+    count = len(QKV_CHUNKS)
+
+    def tick(t):
+        add(*[(t - i, i) for i in range(1, 5) if 0 <= t - i < count])
+
+    loads[0].wait()
+    acc[0:cols, :] = d_out_ref[...]
+    ready(0, cols)
+    for load in loads[1:4]:
         load.wait()
-    acc[0:cols, :] = d_out_ref[...]
     gain_row = weight_grad(0, dq_ref)
-    add((0, 0))
     for load in loads[4:]:
         load.wait()
     bufs[0, FAR] = in_part(far).astype(low)
     each(PARTS, lambda c: sum_copy(FAR, c).start())
+    tick(1)
     gain_row = gain_row + weight_grad(1, dk_ref)
-    add((1, 0))
     mine[...] = in_part(across)
 
     def pass_across(c):
         bufs[0, ACROSS, piece(c), :] = (mine[piece(c), :] + arrived(FAR, c)).astype(low)
         sum_copy(ACROSS, c).start()
     each(PARTS, pass_across)
+    tick(2)
     gain_row = gain_row + weight_grad(2, dv_ref)
-    add((2, 0))
+    tick(3)
 
     row = lax.broadcasted_iota(jnp.int32, (8, width), 0)
     gain_dp[dp] = jnp.where(row == 0, gain_part_ref[...], jnp.where(row == 1, gain_row / gain_ref[...].reshape(1, -1), 0.0))
@@ -986,19 +1006,15 @@
     def norm(c):
         each(1, lambda i: back_norm(i + c))
 
-    add((0, 1))
-    norm(0)
-    add((1, 1), (0, 2))
-    norm(1)
-    add((2, 1), (1, 2), (0, 3))
-    norm(2)
-    turn_gains()
-    add((2, 2), (1, 3))
-    norm(3)
-    store_tokens.start()
-    add((0, 4), (2, 3))
-    end_gains()
-    add((1, 4), (2, 4))
+    for t in range(4, max(count + 4, 5 + PARTS)):
+        tick(t)
+        if t < 4 + PARTS:
+            norm(t - 4)
+        if t == 5:
+            turn_gains()
+        if t == 4 + PARTS:
+            store_tokens.start()
+            end_gains()
     if fits:
         add_drain()
     else:
@@ -1039,7 +1055,7 @@
             room((own, width), full), room((2, 3, own, width), low), room((dp_count, 8, width), full), room((4, 8, width), full),
             dma((3, PARTS)), dma((3, PARTS)), dma((dp_count,)), dma((dp_count,)), dma((3,)), dma((3,)),
             room((d_rows, width), low), room((d_rows, width), low), room((d_rows, width), low),
-            dma((QKV_CHUNKS, dp_count)), dma((QKV_CHUNKS, dp_count)), dma((QKV_CHUNKS,)),
+            dma((len(QKV_CHUNKS), dp_count)), dma((len(QKV_CHUNKS), dp_count)), dma((len(QKV_CHUNKS),)),
         ],
         compiler_params=pltpu.CompilerParams(collective_id=3, has_side_effects=True, vmem_limit_bytes=VMEM_BYTES),
         cost_estimate=pl.CostEstimate(flops=12 * 4 * own * width * cols, bytes_accessed=20 * own * width, transcendentals=0),

time: 248 us -> 243 us (0.980)
  Pallas kernels: 236 us -> 228 us
  waiting for transfers between devices: 0.01 us -> 4.07 us
    pallas_call x1, Pallas kernels: 32.5 us -> 24.4 us  [attend_backward(): pl.pallas_call(functools.partial(bwd_kernel, n, heads), grid_spec=pltpu.P...]
    pallas_call x1, Pallas kernels: 20.5 us -> 16.5 us  [attend_forward(): pl.pallas_call(functools.partial(fwd_kernel, n, heads), grid_spec=pltpu.P...]
    ppermute x1, waiting for transfers between devices: 0.01 us -> 2.9 us  [local(): lax.ppermute(grad_block, 'mp', [(i, i ^ 2) for i in range(lax.axis_size('...]
    pallas_call x1, Pallas kernels: 47.9 us -> 50.5 us  [last(): pl.pallas_call(functools.partial(last_kernel, dp_count, fits), out_shape=...]
  transfers between devices with their start and end apart: 4 -> 4, of which waited for: 0 -> 2; matrix products, arithmetic and copies ran while one was open for 0% -> 0% of each run, Pallas kernels for 41% -> 38%
where the time goes in v8:
time: 243 us
  Pallas kernels  228 us (94%)
  starting transfers between devices  7.72 us (3%)
  waiting for transfers between devices  4.07 us (2%)
    pallas_call x1, Pallas kernels, middle(): pl.pallas_call(functools.partial(middle_kernel, stages), out_shape=[shape...  101 us
    pallas_call x1, Pallas kernels, last(): pl.pallas_call(functools.partial(last_kernel, dp_count, fits), out_shape=...  50.5 us
    pallas_call x1, Pallas kernels, project(): pl.pallas_call(functools.partial(project_kernel, dp_count), out_shape=[ja...  29.9 us
    pallas_call x1, Pallas kernels, attend_backward(): pl.pallas_call(functools.partial(bwd_kernel, n, heads), grid_spec=pltpu.P...  24.4 us
    pallas_call x1, Pallas kernels, attend_forward(): pl.pallas_call(functools.partial(fwd_kernel, n, heads), grid_spec=pltpu.P...  16.5 us
    pallas_call x1, Pallas kernels, finish(): pl.pallas_call(finish_kernel, grid=(steps,), out_shape=[shape((2 * steps...  6.19 us
  transfers between devices with their start and end apart: 4, of which 2 were waited for; matrix products, arithmetic and copies ran while one was open for 0% of the time, Pallas kernels for 38%

profile of v8, /device:TPU:0, one launch (start us, length us, event | category | flops | bytes accessed | tf_op | source)
XLA Modules:
  0.0 242.6 jit_solution(11388310602435602330)
XLA Ops:
  0.6 29.9 %project.1 = (bf16[2048,768]{1,0:T(8,128)(2,1)}, bf16[2048,192]{1,0:T(8,128)(2,1)}, bf16[2048,192]{1,0:T(8,128)(2,1)}, bf16[2048,192]{1,0:T(8,128)(2,1)}, bf16[5...) custom-call(bf16[512,768]{1,0:T(8,128)(2,1)} %tokens_hbm.5, f32[768]{0:T(1024)} %gain_hbm.5, ...), custom_call_target="tpu_custom_call" | custom-call | flops 1811939328 | bytes 15728640 | tf_op jit(solution)/shard_map/project/pallas_call | solution.py:464
  30.6 0.6 collective-permute-start
  31.2 16.5 %attend_forward.1 = (bf16[2048,192]{1,0:T(8,128)(2,1)}, f32[8,2048]{1,0:T(8,128)}) custom-call(s32[8,128]{1,0:T(8,128)} %get-tuple-element.41.ranges, s32[1,2048]{1,0:T(1,128)} %segv_ref.3, bf16[2048,192]{1,0:T(8,128)(2,1)} %get-tuple-element.42.q_ref, bf16[2048,192]{1,0:T(8,128)(2,1)} %get-tuple-element.43.k_ref, bf16[2048,192]{1,0:T(8,128)(2,1)} %get-tuple-element.44.v_ref), custom_call_target="tpu_custom_call" | custom-call | flops 3221225472 | bytes 3145728 | tf_op jit(solution)/shard_map/attend_forward/pallas_call | solution.py:114
  47.7 2.9 %collective-permute-done.grad_across_hbm = bf16[512,768]{1,0:T(8,128)(2,1)S(1)} collective-permute-done((bf16[512,768]{1,0:T(8,128)(2,1)}, bf16[512,768]{1,0:T(8,128)(2,1)S(1)}, u32[]{:S(2)}, u32[]{:S(2)}) %collective-permute-start) | collective-permute-done | bytes 786464 | tf_op jit(solution)/shard_map/ppermute | solution.py:1152
  50.6 0.9 copy-done.5
  51.5 100.5 %middle.1 = (bf16[2048,768]{1,0:T(8,128)(2,1)}, bf16[2048,192]{1,0:T(8,128)(2,1)}, f32[512,768]{1,0:T(8,128)}, bf16[640,768]{1,0:T(8,128)(2,1)}, bf16[384,768]{1...) custom-call(bf16[2048,192]{1,0:T(8,128)(2,1)} %get-tuple-element.45.merged_hbm.o_ref, ...), custom_call_target="tpu_custom_call" | custom-call | flops 19327352832 | bytes 31457280 | tf_op jit(solution)/shard_map/middle/pallas_call | solution.py:759
  152.0 0.0 copy-start.1
  152.0 0.0 copy-start.2
  152.0 3.9 %all-to-all-start = ((bf16[8,80,768]{2,1,0:T(8,128)(2,1)}), bf16[8,80,768]{2,1,0:T(8,128)(2,1)S(1)}, u32[]{:S(2)}, u32[]{:S(2)}) async-start(bf16[8,80,768]{2,1,0:T(8,128)(2,1)} %bitcast.9), calls=%async_computation | async-start | bytes 1966080 | tf_op jit(solution)/shard_map/all_to_all | solution.py:1163
  155.9 0.0 copy-done.1
  155.9 1.7 collective-permute-start.1
  157.6 0.0 copy-done.2
  157.6 1.5 collective-permute-start.2
  159.1 24.4 %attend_backward.1 = (bf16[2048,192]{1,0:T(8,128)(2,1)}, bf16[2048,192]{1,0:T(8,128)(2,1)}, bf16[2048,192]{1,0:T(8,128)(2,1)}) custom-call(s32[8,128]{1,0:T(8,128)} %get-tuple-element.41.ranges, s32[1,2048]{1,0:T(1,128)} %segv_ref.3, bf16[2048,192]{1,0:T(8,128)(2,1)} %get-tuple-element.42.q_ref, bf16[2048,192]{1,0:T(8,128)(2,1)} %get-tuple-element.43.k_ref, ...), custom_call_target="tpu_custom_call" | custom-call | flops 8053063680 | bytes 6291456 | tf_op jit(solution)/shard_map/attend_backward/pallas_call | solution.py:192
  183.5 0.0 collective-permute-done.1.first_came_ref
  183.5 0.0 copy-start.3
  183.5 1.2 collective-permute-done.2.second_came_ref
  184.7 50.5 %last.1 = (bf16[512,768]{1,0:T(8,128)(2,1)}, bf16[768,768]{1,0:T(8,128)(2,1)}, f32[8,768]{1,0:T(8,128)}) custom-call(bf16[2048,192]{1,0:T(8,128)(2,1)} %get-tuple-element.55.dq_hbm, bf16[2048,192]{1,0:T(8,128)(2,1)} %get-tuple-element.56.dk_hbm, bf16[2048,192]{1,0:T(8,128)(2,1)} %get-tuple-element.57.dv_hbm, bf16[3,192,768]{2,1,0:T(8,128)(2,1)} %bitcast.13, ...), custom_call_target="tpu_custom_call" | custom-call | flops 3623878656 | bytes 7864320 | tf_op jit(solution)/shard_map/last/pallas_call | solution.py:1047
  235.3 0.0 copy-done.3
  235.3 0.0 copy-done.4
  235.3 0.0 all-to-all-done
  235.3 0.0 copy-start
  235.3 0.9 copy-done
  236.2 6.2 %finish.1 = (f32[768,768]{1,0:T(8,128)}, f32[768,768]{1,0:T(8,128)}, f32[192,768]{1,0:T(8,128)}, f32[576,768]{1,0:T(8,128)}, f32[768]{0:T(1024)}, /*index=5*/f32...) custom-call(bf16[384,768]{1,0:T(8,128)(2,1)} %get-tuple-element.48.first_ref, bf16[384,768]{1,0:T(8,128)(2,1)} %copy-done.3, ...), custom_call_target="tpu_custom_call" | custom-call | bytes 8257536 | tf_op jit(solution)/shard_map/finish/pallas_call | solution.py:1124
  (2 shorter events, 0.0 us)
Async XLA Ops:
  30.6 20.0 %collective-permute-start = (bf16[512,768]{1,0:T(8,128)(2,1)}, bf16[512,768]{1,0:T(8,128)(2,1)S(1)}, u32[]{:S(2)}, u32[]{:S(2)}) collective-permute-start(bf16[512,768]{1,0:T(8,128)(2,1)} %get-tuple-element.46.grad_own_hbm), channel_id=1, source_target_pairs={{0,2},{1,3},{2,0},{3,1},{4,6},{5,7},{6,4},{7,5},{8,10},{9,11},{10,... | collective-permute-start | bytes 2359304 | tf_op jit(solution)/shard_map/ppermute | solution.py:1152
  50.6 0.9 copy-start.5
  152.0 3.9 %copy-start.1 = (bf16[384,768]{1,0:T(8,128)(2,1)S(1)}, bf16[384,768]{1,0:T(8,128)(2,1)}, u32[]{:S(2)}) copy-start(bf16[384,768]{1,0:T(8,128)(2,1)} %get-tuple-element.48.first_ref) | copy-start | bytes 1769476
  152.0 5.6 %copy-start.2 = (bf16[384,768]{1,0:T(8,128)(2,1)S(1)}, bf16[384,768]{1,0:T(8,128)(2,1)}, u32[]{:S(2)}) copy-start(bf16[384,768]{1,0:T(8,128)(2,1)} %get-tuple-element.50.second_ref) | copy-start | bytes 1769476
  152.0 83.3 %all-to-all-start = ((bf16[8,80,768]{2,1,0:T(8,128)(2,1)}), bf16[8,80,768]{2,1,0:T(8,128)(2,1)S(1)}, u32[]{:S(2)}, u32[]{:S(2)}) async-start(bf16[8,80,768]{2,1,0:T(8,128)(2,1)} %bitcast.9), calls=%async_computation | async-start | bytes 1966080 | tf_op jit(solution)/shard_map/all_to_all | solution.py:1163
  155.9 27.6 %collective-permute-start.1 = (bf16[384,768]{1,0:T(8,128)(2,1)S(1)}, bf16[384,768]{1,0:T(8,128)(2,1)S(1)}, u32[]{:S(2)}, u32[]{:S(2)}) collective-permute-start(bf16[384,768]{1,0:T(8,128)(2,1)S(1)} %copy-done.1), channel_id=1, source_target_pairs={{0,4},{4,0},{8,12},{12,8},{16,20},{20,16},{24,28},{28,24},{1,5},{5... | collective-permute-start | bytes 1769480 | tf_op jit(solution)/shard_map/ppermute | solution.py:1160
  157.6 27.1 %collective-permute-start.2 = (bf16[384,768]{1,0:T(8,128)(2,1)S(1)}, bf16[384,768]{1,0:T(8,128)(2,1)S(1)}, u32[]{:S(2)}, u32[]{:S(2)}) collective-permute-start(bf16[384,768]{1,0:T(8,128)(2,1)S(1)} %copy-done.2), channel_id=1, source_target_pairs={{0,8},{4,12},{8,0},{12,4},{16,24},{20,28},{24,16},{28,20},{1,9},{5... | collective-permute-start | bytes 1769480 | tf_op jit(solution)/shard_map/ppermute | solution.py:1161
  183.5 51.7 %copy-start.3 = (bf16[384,768]{1,0:T(8,128)(2,1)}, bf16[384,768]{1,0:T(8,128)(2,1)S(1)}, u32[]{:S(2)}) copy-start(bf16[384,768]{1,0:T(8,128)(2,1)S(1)} %collective-permute-done.1.first_came_ref) | copy-start | bytes 1769476
  184.7 50.6 %copy-start.4 = (bf16[384,768]{1,0:T(8,128)(2,1)}, bf16[384,768]{1,0:T(8,128)(2,1)S(1)}, u32[]{:S(2)}) copy-start(bf16[384,768]{1,0:T(8,128)(2,1)S(1)} %collective-permute-done.2.second_came_ref) | copy-start | bytes 1769476
  235.3 1.0 copy-start

commit v9 on v8

--- a/solution.py
+++ b/solution.py
@@ -210,7 +210,7 @@
 PARTS = 4
 VMEM_BYTES = 60 << 20
 MLP_CHUNKS = 6
-QKV_CHUNKS = (128,) * 6
+QKV_CHUNKS = (128, 128, 256, 256)
 
 
 def remote(src, dst, send, recv, device):
@@ -784,7 +784,7 @@
 
 
 def direct_fits(rows, chunks, dp_count):
-    return dp_count % 2 == 0 and rows == sum(chunks) and all(one % (16 * dp_count) == 0 for one in chunks)
+    return dp_count == 8 and rows == sum(chunks) and all(one % (16 * dp_count) == 0 for one in chunks)
 
 
 def direct_steps(dp_count, chunks, acc, came, send, recv, out, out_hbm, keep_sem):
@@ -806,18 +806,26 @@
     def member(j):
         return lax.rem(z + j, group)
 
-    def slot_of(k, j):
-        return span(starts[k] + halves[k] + (j - 1) * slots[k], slots[k])
+    first, second = lax.rem(z, 2), lax.rem(z // 2, 2)
+
+    def piece_of(member_z):
+        return 2 * lax.rem(member_z, 2) + lax.rem(member_z // 2, 2)
 
     def halve(k):
         return remote(acc.at[span(low(k, 1 - y), halves[k])], came.at[span(starts[k], halves[k])], send.at[k, 0], recv.at[k, 0], beside)
 
-    def scatter(k, j):
-        piece = acc.at[span(low(k, y, member(j)), slots[k])]
-        return remote(piece, came.at[slot_of(k, j)], send.at[k, j], recv.at[k, j], (y + 2 * member(j), mp))
+    def split(k):
+        rows = span(low(k, y, 2 * (1 - first)), 2 * slots[k])
+        here = span(starts[k] + halves[k], 2 * slots[k])
+        return remote(acc.at[rows], came.at[here], send.at[k, 1], recv.at[k, 1], (dp + 2 - 4 * first, mp))
+
+    def split_again(k):
+        rows = span(low(k, y, 2 * first + 1 - second), slots[k])
+        here = span(starts[k] + halves[k] + 2 * slots[k], slots[k])
+        return remote(acc.at[rows], came.at[here], send.at[k, 2], recv.at[k, 2], (dp + 4 - 8 * second, mp))
 
     def gather(k, j, mine=True):
-        rows = out.at[span(low(k, y, z if mine else member(group - j)), slots[k])]
+        rows = out.at[span(low(k, y, piece_of(z if mine else member(group - j))), slots[k])]
         return remote(rows, rows, send.at[k, group + j - 1], recv.at[k, group + j - 1], (y + 2 * member(j), mp))
 
     def double(k, mine=True):
@@ -836,18 +844,21 @@
             rows = span(low(k, y), halves[k])
             total = acc[rows, :].astype(jnp.float32) + came[span(starts[k], halves[k]), :].astype(jnp.float32)
             acc[rows, :] = total.astype(jnp.bfloat16)
-            for j in others:
-                scatter(k, j).start()
+            split(k).start()
         elif i == 2:
-            rows = span(low(k, y, z), slots[k])
-            total = acc[rows, :].astype(jnp.float32)
-            for j in others:
-                scatter(k, j).wait_recv()
-                total = total + came[slot_of(k, j), :].astype(jnp.float32)
-            out[rows, :] = total.astype(jnp.bfloat16)
+            split(k).wait_recv()
+            rows = span(low(k, y, 2 * first), 2 * slots[k])
+            here = span(starts[k] + halves[k], 2 * slots[k])
+            acc[rows, :] = (acc[rows, :].astype(jnp.float32) + came[here, :].astype(jnp.float32)).astype(jnp.bfloat16)
+            split_again(k).start()
+        elif i == 3:
+            split_again(k).wait_recv()
+            rows = span(low(k, y, 2 * first + second), slots[k])
+            here = span(starts[k] + halves[k] + 2 * slots[k], slots[k])
+            out[rows, :] = (acc[rows, :].astype(jnp.float32) + came[here, :].astype(jnp.float32)).astype(jnp.bfloat16)
             for j in others:
                 gather(k, j).start()
-        elif i == 3:
+        elif i == 4:
             for j in others:
                 gather(k, j, False).wait_recv()
             double(k).start()
@@ -858,8 +869,9 @@
     def drain():
         for k in range(len(chunks)):
             halve(k).wait_send()
+            split(k).wait_send()
+            split_again(k).wait_send()
             for j in others:
-                scatter(k, j).wait_send()
                 gather(k, j).wait_send()
             double(k).wait_send()
             keep(k).wait()
@@ -937,7 +949,7 @@
     count = len(QKV_CHUNKS)
 
     def tick(t):
-        add(*[(t - i, i) for i in range(1, 5) if 0 <= t - i < count])
+        add(*[(t - i, i) for i in range(1, 6) if 0 <= t - i < count])
 
     loads[0].wait()
     acc[0:cols, :] = d_out_ref[...]
@@ -1006,7 +1018,7 @@
     def norm(c):
         each(1, lambda i: back_norm(i + c))
 
-    for t in range(4, max(count + 4, 5 + PARTS)):
+    for t in range(4, max(count + 5, 5 + PARTS)):
         tick(t)
         if t < 4 + PARTS:
             norm(t - 4)
@@ -1132,7 +1144,7 @@
         out_specs=[block(2 * size)] * 2 + [block(cols // 3), block(cols), vmem, vmem, hbm, hbm],
         scratch_shapes=[pltpu.VMEM(one.shape, one.dtype) for one in (grad_tokens, relaid)]
         + [pltpu.SemaphoreType.DMA((2,)), pltpu.SemaphoreType.DMA((2,))],
-        compiler_params=pltpu.CompilerParams(vmem_limit_bytes=VMEM_BYTES),
+        compiler_params=pltpu.CompilerParams(vmem_limit_bytes=VMEM_BYTES - (6 << 20)),
         cost_estimate=pl.CostEstimate(flops=0, bytes_accessed=14 * rows * width, transcendentals=0),
         name="finish",
     )(first, first_came, second, second_came, weight_sum, weight_sum, gains, grad_tokens, relaid)

time: 243 us -> 241 us (level)
  waiting for transfers between devices: 4.07 us -> 0.01 us
    pallas_call x1, Pallas kernels: 50.5 us -> 44.8 us  [last(): pl.pallas_call(functools.partial(last_kernel, dp_count, fits), out_shape=...]
    pallas_call x1, Pallas kernels: 24.4 us -> 29.4 us  [attend_backward(): pl.pallas_call(functools.partial(bwd_kernel, n, heads), grid_spec=pltpu.P...]
    pallas_call x1, Pallas kernels: 16.5 us -> 20.1 us  [attend_forward(): pl.pallas_call(functools.partial(fwd_kernel, n, heads), grid_spec=pltpu.P...]
    ppermute x1, waiting for transfers between devices: 2.9 us -> 0.01 us  [local(): lax.ppermute(grad_block, 'mp', [(i, i ^ 2) for i in range(lax.axis_size('...]
  transfers between devices with their start and end apart: 4 -> 4, of which waited for: 2 -> 0; matrix products, arithmetic and copies ran while one was open for 0% -> 0% of each run, Pallas kernels for 38% -> 39%
where the time goes in v9:
time: 241 us
  Pallas kernels  230 us (95%)
  starting transfers between devices  7.72 us (3%)
    pallas_call x1, Pallas kernels, middle(): pl.pallas_call(functools.partial(middle_kernel, stages), out_shape=[shape...  99.8 us
    pallas_call x1, Pallas kernels, last(): pl.pallas_call(functools.partial(last_kernel, dp_count, fits), out_shape=...  44.8 us
    pallas_call x1, Pallas kernels, project(): pl.pallas_call(functools.partial(project_kernel, dp_count), out_shape=[ja...  29.9 us
    pallas_call x1, Pallas kernels, attend_backward(): pl.pallas_call(functools.partial(bwd_kernel, n, heads), grid_spec=pltpu.P...  29.4 us
    pallas_call x1, Pallas kernels, attend_forward(): pl.pallas_call(functools.partial(fwd_kernel, n, heads), grid_spec=pltpu.P...  20.1 us
    pallas_call x1, Pallas kernels, finish(): pl.pallas_call(finish_kernel, grid=(steps,), out_shape=[shape((2 * steps...  6.19 us
  transfers between devices with their start and end apart: 4, of which 0 were waited for; matrix products, arithmetic and copies ran while one was open for 0% of the time, Pallas kernels for 39%

profile of v9, /device:TPU:0, one launch (start us, length us, event | category | flops | bytes accessed | tf_op | source)
XLA Modules:
  0.0 240.7 jit_solution(10147537196872603116)
XLA Ops:
  0.6 29.9 %project.1 = (bf16[2048,768]{1,0:T(8,128)(2,1)}, bf16[2048,192]{1,0:T(8,128)(2,1)}, bf16[2048,192]{1,0:T(8,128)(2,1)}, bf16[2048,192]{1,0:T(8,128)(2,1)}, bf16[5...) custom-call(bf16[512,768]{1,0:T(8,128)(2,1)} %tokens_hbm.5, f32[768]{0:T(1024)} %gain_hbm.5, ...), custom_call_target="tpu_custom_call" | custom-call | flops 1811939328 | bytes 15728640 | tf_op jit(solution)/shard_map/project/pallas_call | solution.py:464
  30.6 0.6 collective-permute-start
  31.2 20.1 %attend_forward.1 = (bf16[2048,192]{1,0:T(8,128)(2,1)}, f32[8,2048]{1,0:T(8,128)}) custom-call(s32[8,128]{1,0:T(8,128)} %get-tuple-element.41.ranges, s32[1,2048]{1,0:T(1,128)} %segv_ref.3, bf16[2048,192]{1,0:T(8,128)(2,1)} %get-tuple-element.42.q_ref, bf16[2048,192]{1,0:T(8,128)(2,1)} %get-tuple-element.43.k_ref, bf16[2048,192]{1,0:T(8,128)(2,1)} %get-tuple-element.44.v_ref), custom_call_target="tpu_custom_call" | custom-call | flops 3221225472 | bytes 3145728 | tf_op jit(solution)/shard_map/attend_forward/pallas_call | solution.py:114
  51.3 0.0 collective-permute-done.grad_across_hbm
  51.3 0.9 copy-done.5
  52.2 99.8 %middle.1 = (bf16[2048,768]{1,0:T(8,128)(2,1)}, bf16[2048,192]{1,0:T(8,128)(2,1)}, f32[512,768]{1,0:T(8,128)}, bf16[640,768]{1,0:T(8,128)(2,1)}, bf16[384,768]{1...) custom-call(bf16[2048,192]{1,0:T(8,128)(2,1)} %get-tuple-element.45.merged_hbm.o_ref, ...), custom_call_target="tpu_custom_call" | custom-call | flops 19327352832 | bytes 31457280 | tf_op jit(solution)/shard_map/middle/pallas_call | solution.py:759
  152.0 0.0 copy-start.1
  152.0 0.0 copy-start.2
  152.0 3.9 %all-to-all-start = ((bf16[8,80,768]{2,1,0:T(8,128)(2,1)}), bf16[8,80,768]{2,1,0:T(8,128)(2,1)S(1)}, u32[]{:S(2)}, u32[]{:S(2)}) async-start(bf16[8,80,768]{2,1,0:T(8,128)(2,1)} %bitcast.9), calls=%async_computation | async-start | bytes 1966080 | tf_op jit(solution)/shard_map/all_to_all | solution.py:1175
  155.9 0.0 copy-done.1
  155.9 1.7 collective-permute-start.1
  157.6 0.0 copy-done.2
  157.6 1.5 collective-permute-start.2
  159.1 29.4 %attend_backward.1 = (bf16[2048,192]{1,0:T(8,128)(2,1)}, bf16[2048,192]{1,0:T(8,128)(2,1)}, bf16[2048,192]{1,0:T(8,128)(2,1)}) custom-call(s32[8,128]{1,0:T(8,128)} %get-tuple-element.41.ranges, s32[1,2048]{1,0:T(1,128)} %segv_ref.3, bf16[2048,192]{1,0:T(8,128)(2,1)} %get-tuple-element.42.q_ref, bf16[2048,192]{1,0:T(8,128)(2,1)} %get-tuple-element.43.k_ref, ...), custom_call_target="tpu_custom_call" | custom-call | flops 8053063680 | bytes 6291456 | tf_op jit(solution)/shard_map/attend_backward/pallas_call | solution.py:192
  188.5 0.0 collective-permute-done.1.first_came_ref
  188.5 0.0 copy-start.3
  188.5 0.0 collective-permute-done.2.second_came_ref
  188.5 0.0 copy-start.4
  188.5 44.8 %last.1 = (bf16[512,768]{1,0:T(8,128)(2,1)}, bf16[768,768]{1,0:T(8,128)(2,1)}, f32[8,768]{1,0:T(8,128)}) custom-call(bf16[2048,192]{1,0:T(8,128)(2,1)} %get-tuple-element.55.dq_hbm, bf16[2048,192]{1,0:T(8,128)(2,1)} %get-tuple-element.56.dk_hbm, bf16[2048,192]{1,0:T(8,128)(2,1)} %get-tuple-element.57.dv_hbm, bf16[3,192,768]{2,1,0:T(8,128)(2,1)} %bitcast.13, ...), custom_call_target="tpu_custom_call" | custom-call | flops 3623878656 | bytes 7864320 | tf_op jit(solution)/shard_map/last/pallas_call | solution.py:1059
  233.3 0.0 copy-done.3
  233.3 0.0 all-to-all-done
  233.3 0.0 copy-start
  233.3 0.9 copy-done
  234.3 6.2 %finish.1 = (f32[768,768]{1,0:T(8,128)}, f32[768,768]{1,0:T(8,128)}, f32[192,768]{1,0:T(8,128)}, f32[576,768]{1,0:T(8,128)}, f32[768]{0:T(1024)}, /*index=5*/f32...) custom-call(bf16[384,768]{1,0:T(8,128)(2,1)} %get-tuple-element.48.first_ref, bf16[384,768]{1,0:T(8,128)(2,1)} %copy-done.3, ...), custom_call_target="tpu_custom_call" | custom-call | bytes 8257536 | tf_op jit(solution)/shard_map/finish/pallas_call | solution.py:1136
  (2 shorter events, 0.0 us)
Async XLA Ops:
  30.6 20.7 %collective-permute-start = (bf16[512,768]{1,0:T(8,128)(2,1)}, bf16[512,768]{1,0:T(8,128)(2,1)S(1)}, u32[]{:S(2)}, u32[]{:S(2)}) collective-permute-start(bf16[512,768]{1,0:T(8,128)(2,1)} %get-tuple-element.46.grad_own_hbm), channel_id=1, source_target_pairs={{0,2},{1,3},{2,0},{3,1},{4,6},{5,7},{6,4},{7,5},{8,10},{9,11},{10,... | collective-permute-start | bytes 2359304 | tf_op jit(solution)/shard_map/ppermute | solution.py:1164
  51.3 0.9 copy-start.5
  152.0 3.9 %copy-start.1 = (bf16[384,768]{1,0:T(8,128)(2,1)S(1)}, bf16[384,768]{1,0:T(8,128)(2,1)}, u32[]{:S(2)}) copy-start(bf16[384,768]{1,0:T(8,128)(2,1)} %get-tuple-element.48.first_ref) | copy-start | bytes 1769476
  152.0 5.6 %copy-start.2 = (bf16[384,768]{1,0:T(8,128)(2,1)S(1)}, bf16[384,768]{1,0:T(8,128)(2,1)}, u32[]{:S(2)}) copy-start(bf16[384,768]{1,0:T(8,128)(2,1)} %get-tuple-element.50.second_ref) | copy-start | bytes 1769476
  152.0 81.3 %all-to-all-start = ((bf16[8,80,768]{2,1,0:T(8,128)(2,1)}), bf16[8,80,768]{2,1,0:T(8,128)(2,1)S(1)}, u32[]{:S(2)}, u32[]{:S(2)}) async-start(bf16[8,80,768]{2,1,0:T(8,128)(2,1)} %bitcast.9), calls=%async_computation | async-start | bytes 1966080 | tf_op jit(solution)/shard_map/all_to_all | solution.py:1175
  155.9 32.5 %collective-permute-start.1 = (bf16[384,768]{1,0:T(8,128)(2,1)S(1)}, bf16[384,768]{1,0:T(8,128)(2,1)S(1)}, u32[]{:S(2)}, u32[]{:S(2)}) collective-permute-start(bf16[384,768]{1,0:T(8,128)(2,1)S(1)} %copy-done.1), channel_id=1, source_target_pairs={{0,4},{4,0},{8,12},{12,8},{16,20},{20,16},{24,28},{28,24},{1,5},{5... | collective-permute-start | bytes 1769480 | tf_op jit(solution)/shard_map/ppermute | solution.py:1172
  157.6 30.9 %collective-permute-start.2 = (bf16[384,768]{1,0:T(8,128)(2,1)S(1)}, bf16[384,768]{1,0:T(8,128)(2,1)S(1)}, u32[]{:S(2)}, u32[]{:S(2)}) collective-permute-start(bf16[384,768]{1,0:T(8,128)(2,1)S(1)} %copy-done.2), channel_id=1, source_target_pairs={{0,8},{4,12},{8,0},{12,4},{16,24},{20,28},{24,16},{28,20},{1,9},{5... | collective-permute-start | bytes 1769480 | tf_op jit(solution)/shard_map/ppermute | solution.py:1173
  188.5 44.8 %copy-start.3 = (bf16[384,768]{1,0:T(8,128)(2,1)}, bf16[384,768]{1,0:T(8,128)(2,1)S(1)}, u32[]{:S(2)}) copy-start(bf16[384,768]{1,0:T(8,128)(2,1)S(1)} %collective-permute-done.1.first_came_ref) | copy-start | bytes 1769476
  188.5 44.8 %copy-start.4 = (bf16[384,768]{1,0:T(8,128)(2,1)}, bf16[384,768]{1,0:T(8,128)(2,1)S(1)}, u32[]{:S(2)}) copy-start(bf16[384,768]{1,0:T(8,128)(2,1)S(1)} %collective-permute-done.2.second_came_ref) | copy-start | bytes 1769476
  233.3 1.0 copy-start
